TPU v7x, 512 devices: a whole 4x4x16 slice. The times are simulated.
512 devices in a mesh: genome: 512 (over z, x, y, core).
Axes of the slice: x: 4, y: 4, z: 16, core: 2. Of those that a mesh axis runs over, the one named last changes fastest.
Arguments:
- contacts: int32 [131072, 1024], P('genome'), may hold values from 0 to 1040, as said below
- mappable: int32 [131072], P('genome'), may hold values 0 or 1
Outputs:
- pvalue_donut: float32 [131072, 1024], P('genome')
- pvalue_lower: float32 [131072, 1024], P('genome')
- bin_bias: float32 [131072], P('genome')
Inputs may be any that keep to these rules, and one draw needn't show every extreme that they name: contacts[i, d] counts the contacts of bin i with bin i + d; it is zero where i + d >= 131072 and 1 or more where d = 0 and i < 131072.
All inputs are finite; a program needn't handle non-finite values. No bound on the sum of `mappable` on one device may be relied on, other than what follows from the above.
Results may differ from a plain program's by a relative error of at most 0.0003.
Values sent between devices are 32-bit elements; how exact they have to be, the bound alone decides.
No kernel may reach another device: no remote copies, remote signals or barrier semaphores. Data moves between devices by JAX's collectives and lax.ppermute only.
A program may use at most 64 MiB of HBM per device.

v0:
```python
import jax
import jax.numpy as jnp
from jax import lax
from jax.sharding import PartitionSpec as P

ITERS = 2
OUTER = 5
INNER = 2


def shifted(value, axis, steps):
    count = lax.axis_size(axis)
    leading, last = (max(0, -steps), min(count, count - steps))
    return lax.ppermute(value, axis, [(source, source + steps) for source in range(leading, last)])


def with_halo(cells, sides, width):
    for axis, dim in sides:
        count = lax.axis_size(axis)
        ends = count - 1
        head = lax.slice_in_dim(cells, 0, width, axis=dim)
        tail = lax.slice_in_dim(cells, cells.shape[dim] - width, cells.shape[dim], axis=dim)
        cells = jnp.concatenate(
            [
                lax.ppermute(tail, axis, [(i, (i + 1) % count) for i in range(ends)]),
                cells,
                lax.ppermute(head, axis, [((i + 1) % count, i) for i in range(ends)]),
            ],
            axis=dim,
        )
    return cells


def hankel(ahead_vec, row_count, band_width):
    line_len = row_count + band_width + 1
    tiled_row = jnp.tile(ahead_vec, row_count + 1)[: row_count * line_len]
    return tiled_row.reshape(row_count, line_len)[:, :band_width]


def column_sums(balanced):
    row_count, band_width = balanced.shape
    line_len = row_count + band_width
    padded = jnp.pad(balanced, ((0, 0), (0, row_count + 1)))
    return jnp.sum(padded.reshape(-1)[: row_count * line_len].reshape(row_count, line_len), axis=0)


def shear_sums(rows_in):
    height = rows_in.shape[0] - 2 * OUTER
    band_width = rows_in.shape[1]
    padded = jnp.pad(rows_in, ((0, 0), (2 * OUTER, 2 * OUTER)))
    span_len = band_width + 2 * OUTER

    def across(offset_low, offset_high):
        running = padded[:, OUTER + offset_low : OUTER + offset_low + span_len]
        for offset in range(offset_low + 1, offset_high + 1):
            running = running + padded[:, OUTER + offset : OUTER + offset + span_len]
        return running

    def tilted(sum_table, row_shift):
        return sum_table[
            OUTER + row_shift : OUTER + row_shift + height,
            OUTER - row_shift : OUTER - row_shift + band_width,
        ]

    outer_rows = across(-OUTER, OUTER)
    inner_rows = across(-INNER, INNER)
    left_outer = across(-OUTER, -1)
    left_inner = across(-INNER, -1)
    donut_sum = tilted(inner_rows, 0) - tilted(outer_rows, 0)
    for row_shift in range(-OUTER, OUTER + 1):
        donut_sum = donut_sum + tilted(outer_rows, row_shift)
        if abs(row_shift) <= INNER:
            donut_sum = donut_sum - tilted(inner_rows, row_shift)
        else:
            donut_sum = (
                donut_sum
                - padded[
                    OUTER + row_shift : OUTER + row_shift + height,
                    2 * OUTER - row_shift : 2 * OUTER - row_shift + band_width,
                ]
            )
    lower_sum = tilted(left_outer, 1) - tilted(left_inner, 1)
    for row_shift in range(2, OUTER + 1):
        lower_sum = lower_sum + tilted(left_outer, row_shift)
        if row_shift <= INNER:
            lower_sum = lower_sum - tilted(left_inner, row_shift)
    return (donut_sum, lower_sum)


def poisson_tail(counts, local_mean):
    shape_k = jnp.maximum(counts.astype(jnp.float32), 1.0)
    ninth = 1.0 / (9.0 * shape_k)
    z_score = (jnp.cbrt(local_mean / shape_k) - (1.0 - ninth)) / jnp.sqrt(ninth)
    return 0.5 * lax.erfc(-z_score / jnp.sqrt(jnp.float32(2.0)))


def tail_values(observed, regional, expected, contacts, weight, pair_mask, distance):
    valid_cols = distance >= 2 * OUTER
    local_ratio = observed / jnp.where(valid_cols, regional, 1.0)
    local_mean = expected[None, :] * local_ratio / jnp.where(pair_mask > 0, weight, 1.0)
    tail_prob = poisson_tail(contacts, jnp.maximum(local_mean, 0.0))
    keep_mask = valid_cols & (pair_mask > 0) & (contacts > 0)
    return jnp.where(keep_mask, tail_prob, 1.0)


def shards(contacts, mappable):
    row_count, band_width = contacts.shape
    hop_total = band_width // row_count
    mapped = mappable.astype(jnp.float32)
    counts_float = contacts.astype(jnp.float32)
    distance = lax.broadcasted_iota(jnp.int32, (1, band_width), 1)

    def inverse_ahead(inverse):
        pieces = [inverse]
        for hop_count in range(1, hop_total + 1):
            pieces.append(shifted(inverse, "genome", -hop_count))
        return jnp.concatenate(pieces)

    bias_vec = jnp.ones((row_count,), jnp.float32)
    inverse = mapped
    for iteration in range(ITERS):
        ahead_band = hankel(inverse_ahead(inverse), row_count, band_width)
        balanced = counts_float * inverse[:, None] * ahead_band
        spread = column_sums(jnp.where(distance > 0, balanced, 0.0))
        row_sums = jnp.sum(balanced, axis=1) + spread[:row_count]
        for hop_count in range(1, hop_total + 1):
            row_sums = row_sums + shifted(
                spread[hop_count * row_count : (hop_count + 1) * row_count], "genome", hop_count
            )
        covered = jnp.sum(mapped * row_sums)
        row_total, mapped_count = lax.psum((covered, jnp.sum(mapped)), "genome")
        bias_vec = jnp.where(mappable > 0, bias_vec * row_sums / (row_total / mapped_count), 1.0)
        inverse = jnp.where(mappable > 0, 1.0 / bias_vec, 0.0)
    ahead_band = hankel(inverse_ahead(inverse), row_count, band_width)
    balanced = counts_float * inverse[:, None] * ahead_band
    pair_mask = mapped[:, None] * (ahead_band > 0).astype(jnp.float32)
    diag_total, pair_total = lax.psum(
        (jnp.sum(balanced, axis=0), jnp.sum(pair_mask, axis=0)), "genome"
    )
    expected = diag_total / pair_total
    rows_in = with_halo(balanced, (("genome", 0),), OUTER)
    donut_obs, lower_obs = shear_sums(rows_in)
    donut_exp, lower_exp = shear_sums(
        jnp.broadcast_to(expected[None, :], (2 * OUTER + 1, band_width))
    )
    weight = inverse[:, None] * ahead_band
    pvalue_donut = tail_values(
        donut_obs, donut_exp, expected, contacts, weight, pair_mask, distance
    )
    pvalue_lower = tail_values(
        lower_obs, lower_exp, expected, contacts, weight, pair_mask, distance
    )
    return (pvalue_donut, pvalue_lower, bias_vec)


def solution(mesh):
    placed = (P("genome", None), P("genome"))
    return jax.shard_map(
        shards,
        mesh=mesh,
        in_specs=placed,
        out_specs=(P("genome", None), P("genome", None), P("genome")),
        check_vma=False,
    )
```

profile of v0, /device:TPU:31, one launch (start us, length us, event | category | flops | bytes accessed | tf_op | source)
XLA Modules:
  0.0 468.4 jit_solution(13679270709106280684)
XLA Ops:
  1.3 2.9 collective-permute-start.3
  6.5 4.3 collective-permute-start.1
  10.8 2.5 collective-permute-start
  14.0 5.9 %collective-permute-done = f32[256]{0:T(256)S(1)} collective-permute-done((f32[256]{0:T(256)S(1)}, f32[256]{0:T(256)S(1)}, u32[]{:S(2)}, u32[]{:S(2)}) %collective-permute-start) | collective-permute-done | bytes 1056 | tf_op jit(solution)/shard_map/ppermute | solution.py:14
  32.3 2.6 collective-permute-start.7
  34.9 5.5 %collective-permute-start.6 = (f32[256]{0:T(256)S(1)}, f32[256]{0:T(256)S(1)}, u32[]{:S(2)}, u32[]{:S(2)}) collective-permute-start(f32[256]{0:T(256)S(1)} %get-tuple-element.45), channel_id=1, source_target_pairs={{0,3},{1,4},{2,5},{3,6},{4,7},{5,8},{6,9},{7,10},{8,11},{9,12},{10... | collective-permute-start | bytes 3080 | tf_op jit(solution)/shard_map/ppermute | solution.py:14
  45.3 107.9 %all-reduce.5 = (f32[]{:T(128)}, f32[]{:T(128)}) all-reduce(f32[]{:T(128)} %get-tuple-element.4, f32[]{:T(128)} %get-tuple-element.3), channel_id=1, replica_groups=mesh['genome'=512] {'genome'}, use_global_device_ids=true, to_apply=%region_3.4 | all-reduce | flops 2 | bytes 16 | tf_op jit(solution)/shard_map/psum | solution.py:131
  154.5 2.6 collective-permute-start.8
  157.1 4.3 collective-permute-start.11
  161.4 3.1 collective-permute-start.10
  166.5 6.6 %collective-permute-done.9 = f32[256]{0:T(256)S(1)} collective-permute-done((f32[256]{0:T(256)S(1)}, f32[256]{0:T(256)S(1)}, u32[]{:S(2)}, u32[]{:S(2)}) %collective-permute-start.9) | collective-permute-done | bytes 1056 | tf_op jit(solution)/shard_map/ppermute | solution.py:14
  185.7 4.0 collective-permute-start.12
  191.6 4.7 %collective-permute-start.14 = (f32[256]{0:T(256)S(1)}, f32[256]{0:T(256)S(1)}, u32[]{:S(2)}, u32[]{:S(2)}) collective-permute-start(f32[256]{0:T(256)S(1)} %get-tuple-element.41), channel_id=1, source_target_pairs={{0,3},{1,4},{2,5},{3,6},{4,7},{5,8},{6,9},{7,10},{8,11},{9,12},{10... | collective-permute-start | bytes 3080 | tf_op jit(solution)/shard_map/ppermute | solution.py:14
  201.3 102.6 %psum.40 = f32[]{:T(128)} all-reduce(f32[]{:T(128)} %get-tuple-element.24), channel_id=1, replica_groups=mesh['genome'=512] {'genome'}, use_global_device_ids=true, to_apply=%region_9.10 | all-reduce | flops 1 | bytes 8 | tf_op jit(solution)/shard_map/psum | solution.py:131
  305.8 2.6 collective-permute-start.16
  308.9 4.3 collective-permute-start.19
  313.2 2.8 collective-permute-start.18
  317.9 6.6 %collective-permute-done.17 = f32[256]{0:T(256)S(1)} collective-permute-done((f32[256]{0:T(256)S(1)}, f32[256]{0:T(256)S(1)}, u32[]{:S(2)}, u32[]{:S(2)}) %collective-permute-start.17) | collective-permute-done | bytes 1056 | tf_op jit(solution)/shard_map/ppermute | solution.py:14
  331.9 100.5 %all-reduce.4 = (f32[1024]{0:T(1024)}, f32[1024]{0:T(1024)}) all-reduce(f32[1024]{0:T(1024)S(1)} %get-tuple-element.33, f32[1024]{0:T(1024)S(1)} %get-tuple-element.13), channel_id=1, replica_groups=mesh['genome'=512] {'genome'}, use_global_device_ids=true, to_apply=%region_11.12 | all-reduce | flops 2048 | bytes 16384 | tf_op jit(solution)/shard_map/psum | solution.py:137
  433.2 5.4 %collective-permute-start.20 = (f32[5,1024]{1,0:T(8,128)S(1)}, f32[5,1024]{1,0:T(8,128)S(1)}, u32[]{:S(2)}, u32[]{:S(2)}) collective-permute-start(f32[5,1024]{1,0:T(8,128)S(1)} %get-tuple-element.37), channel_id=1, source_target_pairs={{0,1},{1,2},{2,3},{3,4},{4,5},{5,6},{6,7},{7,8},{8,9},{9,10},{10,1... | collective-permute-start | bytes 61448 | tf_op jit(solution)/shard_map/ppermute | solution.py:25
  440.8 7.3 %collective-permute-done.21 = f32[5,1024]{1,0:T(8,128)S(1)} collective-permute-done((f32[5,1024]{1,0:T(8,128)S(1)}, f32[5,1024]{1,0:T(8,128)S(1)}, u32[]{:S(2)}, u32[]{:S(2)}) %collective-permute-start.21) | collective-permute-done | bytes 20512 | tf_op jit(solution)/shard_map/ppermute | solution.py:27
  448.6 3.3 add_add_fusion
  451.9 9.5 %fusion.5 = f32[256,1024]{1,0:T(8,128)} fusion(f32[266,1044]{1,0:T(8,128)S(1)} %select_maximum_fusion, f32[266,1034]{1,0:T(8,128)S(1)} %get-tuple-element.35, f32[266,1034]{1,0:T(8,128)S(1)} %get-tuple-element.17, s32[256,1024]{1,0:T(8,128)S(1)} %copy-done, f32[256,1281]{1,0:T(8,128)S(1)} %reshape.112, f32[1024]{0:T(1024)S(1)} %fusion.61, f32[1024]{0:T(1024)S(1)} %div.79, ...), kind=kLoop, calls=%fused_computation.20 | loop fusion | flops 27787264 | bytes 26487808 | tf_op jit(solution)/shard_map/jit(_where)/select_n | solution.py:103
  461.4 7.0 %fusion.8 = f32[256,1024]{1,0:T(8,128)} fusion(f32[266,1034]{1,0:T(8,128)S(1)} %get-tuple-element.36, f32[266,1034]{1,0:T(8,128)S(1)} %get-tuple-element.18, s32[256,1024]{1,0:T(8,128)S(1)} %copy-done, f32[256,1281]{1,0:T(8,128)S(1)} %reshape.112, f32[1024]{0:T(1024)S(1)} %fusion.60, f32[1024]{0:T(1024)S(1)} %div.79, f32[256]{0:T(256)S(1)} %get-tuple-element.22, ...), kind=kLoop, calls=%fused_computation.23 | loop fusion | flops 23330816 | bytes 10759168 | tf_op jit(solution)/shard_map/jit(_where)/select_n | solution.py:103
  (93 shorter events, 55.7 us)
Async XLA Ops:
  1.3 18.6 %collective-permute-start.3 = (f32[256]{0:T(256)S(1)}, f32[256]{0:T(256)S(1)}, u32[]{:S(2)}, u32[]{:S(2)}) collective-permute-start(f32[256]{0:T(256)S(1)} %convert_element_type.17), channel_id=1, source_target_pairs={{4,0},{5,1},{6,2},{7,3},{8,4},{9,5},{10,6},{11,7},{12,8},{13,9},{1... | collective-permute-start | bytes 3080 | tf_op jit(solution)/shard_map/ppermute | solution.py:14
  4.2 15.8 %collective-permute-start.2 = (f32[256]{0:T(256)S(1)}, f32[256]{0:T(256)S(1)}, u32[]{:S(2)}, u32[]{:S(2)}) collective-permute-start(f32[256]{0:T(256)S(1)} %convert_element_type.17), channel_id=1, source_target_pairs={{3,0},{4,1},{5,2},{6,3},{7,4},{8,5},{9,6},{10,7},{11,8},{12,9},{13... | collective-permute-start | bytes 3080 | tf_op jit(solution)/shard_map/ppermute | solution.py:14
  6.5 13.4 %collective-permute-start.1 = (f32[256]{0:T(256)S(1)}, f32[256]{0:T(256)S(1)}, u32[]{:S(2)}, u32[]{:S(2)}) collective-permute-start(f32[256]{0:T(256)S(1)} %convert_element_type.17), channel_id=1, source_target_pairs={{2,0},{3,1},{4,2},{5,3},{6,4},{7,5},{8,6},{9,7},{10,8},{11,9},{12,... | collective-permute-start | bytes 3080 | tf_op jit(solution)/shard_map/ppermute | solution.py:14
  10.8 9.1 %collective-permute-start = (f32[256]{0:T(256)S(1)}, f32[256]{0:T(256)S(1)}, u32[]{:S(2)}, u32[]{:S(2)}) collective-permute-start(f32[256]{0:T(256)S(1)} %convert_element_type.17), channel_id=1, source_target_pairs={{1,0},{2,1},{3,2},{4,3},{5,4},{6,5},{7,6},{8,7},{9,8},{10,9},{11,1... | collective-permute-start | bytes 3080 | tf_op jit(solution)/shard_map/ppermute | solution.py:14
  28.9 15.8 %copy-start.2 = (s32[256]{0:T(256)S(1)}, s32[256]{0:T(256)}, u32[]{:S(2)}) copy-start(s32[256]{0:T(256)} %param.3) | copy-start | bytes 3076
  30.3 12.0 %collective-permute-start.4 = (f32[256]{0:T(256)S(1)}, f32[256]{0:T(256)S(1)}, u32[]{:S(2)}, u32[]{:S(2)}) collective-permute-start(f32[256]{0:T(256)S(1)} %get-tuple-element.43), channel_id=1, source_target_pairs={{0,1},{1,2},{2,3},{3,4},{4,5},{5,6},{6,7},{7,8},{8,9},{9,10},{10,1... | collective-permute-start | bytes 3080 | tf_op jit(solution)/shard_map/ppermute | solution.py:14
  32.3 10.0 %collective-permute-start.7 = (f32[256]{0:T(256)S(1)}, f32[256]{0:T(256)S(1)}, u32[]{:S(2)}, u32[]{:S(2)}) collective-permute-start(f32[256]{0:T(256)S(1)} %get-tuple-element.44), channel_id=1, source_target_pairs={{0,4},{1,5},{2,6},{3,7},{4,8},{5,9},{6,10},{7,11},{8,12},{9,13},{1... | collective-permute-start | bytes 3080 | tf_op jit(solution)/shard_map/ppermute | solution.py:14
  34.9 7.4 %collective-permute-start.6 = (f32[256]{0:T(256)S(1)}, f32[256]{0:T(256)S(1)}, u32[]{:S(2)}, u32[]{:S(2)}) collective-permute-start(f32[256]{0:T(256)S(1)} %get-tuple-element.45), channel_id=1, source_target_pairs={{0,3},{1,4},{2,5},{3,6},{4,7},{5,8},{6,9},{7,10},{8,11},{9,12},{10... | collective-permute-start | bytes 3080 | tf_op jit(solution)/shard_map/ppermute | solution.py:14
  40.4 4.3 collective-permute-start.5
  154.5 12.0 %collective-permute-start.8 = (f32[256]{0:T(256)S(1)}, f32[256]{0:T(256)S(1)}, u32[]{:S(2)}, u32[]{:S(2)}) collective-permute-start(f32[256]{0:T(256)S(1)} %get-tuple-element.27), channel_id=1, source_target_pairs={{1,0},{2,1},{3,2},{4,3},{5,4},{6,5},{7,6},{8,7},{9,8},{10,9},{11,1... | collective-permute-start | bytes 3080 | tf_op jit(solution)/shard_map/ppermute | solution.py:14
  157.1 16.0 %collective-permute-start.11 = (f32[256]{0:T(256)S(1)}, f32[256]{0:T(256)S(1)}, u32[]{:S(2)}, u32[]{:S(2)}) collective-permute-start(f32[256]{0:T(256)S(1)} %get-tuple-element.27), channel_id=1, source_target_pairs={{4,0},{5,1},{6,2},{7,3},{8,4},{9,5},{10,6},{11,7},{12,8},{13,9},{1... | collective-permute-start | bytes 3080 | tf_op jit(solution)/shard_map/ppermute | solution.py:14
  161.4 11.7 %collective-permute-start.10 = (f32[256]{0:T(256)S(1)}, f32[256]{0:T(256)S(1)}, u32[]{:S(2)}, u32[]{:S(2)}) collective-permute-start(f32[256]{0:T(256)S(1)} %get-tuple-element.27), channel_id=1, source_target_pairs={{3,0},{4,1},{5,2},{6,3},{7,4},{8,5},{9,6},{10,7},{11,8},{12,9},{13... | collective-permute-start | bytes 3080 | tf_op jit(solution)/shard_map/ppermute | solution.py:14
  164.6 8.6 %collective-permute-start.9 = (f32[256]{0:T(256)S(1)}, f32[256]{0:T(256)S(1)}, u32[]{:S(2)}, u32[]{:S(2)}) collective-permute-start(f32[256]{0:T(256)S(1)} %get-tuple-element.27), channel_id=1, source_target_pairs={{2,0},{3,1},{4,2},{5,3},{6,4},{7,5},{8,6},{9,7},{10,8},{11,9},{12,... | collective-permute-start | bytes 3080 | tf_op jit(solution)/shard_map/ppermute | solution.py:14
  185.7 13.2 %collective-permute-start.12 = (f32[256]{0:T(256)S(1)}, f32[256]{0:T(256)S(1)}, u32[]{:S(2)}, u32[]{:S(2)}) collective-permute-start(f32[256]{0:T(256)S(1)} %get-tuple-element.39), channel_id=1, source_target_pairs={{0,1},{1,2},{2,3},{3,4},{4,5},{5,6},{6,7},{7,8},{8,9},{9,10},{10,1... | collective-permute-start | bytes 3080 | tf_op jit(solution)/shard_map/ppermute | solution.py:14
  189.7 9.2 %collective-permute-start.15 = (f32[256]{0:T(256)S(1)}, f32[256]{0:T(256)S(1)}, u32[]{:S(2)}, u32[]{:S(2)}) collective-permute-start(f32[256]{0:T(256)S(1)} %get-tuple-element.40), channel_id=1, source_target_pairs={{0,4},{1,5},{2,6},{3,7},{4,8},{5,9},{6,10},{7,11},{8,12},{9,13},{1... | collective-permute-start | bytes 3080 | tf_op jit(solution)/shard_map/ppermute | solution.py:14
  191.6 7.3 %collective-permute-start.14 = (f32[256]{0:T(256)S(1)}, f32[256]{0:T(256)S(1)}, u32[]{:S(2)}, u32[]{:S(2)}) collective-permute-start(f32[256]{0:T(256)S(1)} %get-tuple-element.41), channel_id=1, source_target_pairs={{0,3},{1,4},{2,5},{3,6},{4,7},{5,8},{6,9},{7,10},{8,11},{9,12},{10... | collective-permute-start | bytes 3080 | tf_op jit(solution)/shard_map/ppermute | solution.py:14
  196.3 4.3 collective-permute-start.13
  305.8 12.2 %collective-permute-start.16 = (f32[256]{0:T(256)S(1)}, f32[256]{0:T(256)S(1)}, u32[]{:S(2)}, u32[]{:S(2)}) collective-permute-start(f32[256]{0:T(256)S(1)} %get-tuple-element.22), channel_id=1, source_target_pairs={{1,0},{2,1},{3,2},{4,3},{5,4},{6,5},{7,6},{8,7},{9,8},{10,9},{11,1... | collective-permute-start | bytes 3080 | tf_op jit(solution)/shard_map/ppermute | solution.py:14
  308.9 15.7 %collective-permute-start.19 = (f32[256]{0:T(256)S(1)}, f32[256]{0:T(256)S(1)}, u32[]{:S(2)}, u32[]{:S(2)}) collective-permute-start(f32[256]{0:T(256)S(1)} %get-tuple-element.22), channel_id=1, source_target_pairs={{4,0},{5,1},{6,2},{7,3},{8,4},{9,5},{10,6},{11,7},{12,8},{13,9},{1... | collective-permute-start | bytes 3080 | tf_op jit(solution)/shard_map/ppermute | solution.py:14
  313.2 11.4 %collective-permute-start.18 = (f32[256]{0:T(256)S(1)}, f32[256]{0:T(256)S(1)}, u32[]{:S(2)}, u32[]{:S(2)}) collective-permute-start(f32[256]{0:T(256)S(1)} %get-tuple-element.22), channel_id=1, source_target_pairs={{3,0},{4,1},{5,2},{6,3},{7,4},{8,5},{9,6},{10,7},{11,8},{12,9},{13... | collective-permute-start | bytes 3080 | tf_op jit(solution)/shard_map/ppermute | solution.py:14
  316.0 8.6 %collective-permute-start.17 = (f32[256]{0:T(256)S(1)}, f32[256]{0:T(256)S(1)}, u32[]{:S(2)}, u32[]{:S(2)}) collective-permute-start(f32[256]{0:T(256)S(1)} %get-tuple-element.22), channel_id=1, source_target_pairs={{2,0},{3,1},{4,2},{5,3},{6,4},{7,5},{8,6},{9,7},{10,8},{11,9},{12,... | collective-permute-start | bytes 3080 | tf_op jit(solution)/shard_map/ppermute | solution.py:14
  433.2 7.6 %collective-permute-start.20 = (f32[5,1024]{1,0:T(8,128)S(1)}, f32[5,1024]{1,0:T(8,128)S(1)}, u32[]{:S(2)}, u32[]{:S(2)}) collective-permute-start(f32[5,1024]{1,0:T(8,128)S(1)} %get-tuple-element.37), channel_id=1, source_target_pairs={{0,1},{1,2},{2,3},{3,4},{4,5},{5,6},{6,7},{7,8},{8,9},{9,10},{10,1... | collective-permute-start | bytes 61448 | tf_op jit(solution)/shard_map/ppermute | solution.py:25
  438.6 9.5 %collective-permute-start.21 = (f32[5,1024]{1,0:T(8,128)S(1)}, f32[5,1024]{1,0:T(8,128)S(1)}, u32[]{:S(2)}, u32[]{:S(2)}) collective-permute-start(f32[5,1024]{1,0:T(8,128)S(1)} %get-tuple-element.38), channel_id=1, source_target_pairs={{1,0},{2,1},{3,2},{4,3},{5,4},{6,5},{7,6},{8,7},{9,8},{10,9},{11,1... | collective-permute-start | bytes 61448 | tf_op jit(solution)/shard_map/ppermute | solution.py:27
  448.5 3.3 copy-start.1
  (5 other events, 9.8 us)
where the time goes:
time: 470 us; the launch traced here: 468 us
  blocking collectives  311 us (66%)
  starting transfers between devices  67.9 us (14%)
  other arithmetic  30.7 us (7%)
  waiting for transfers between devices  30.6 us (7%)
  local copies, waits for them, and re-layouts  24.3 us (5%)
    psum x2, blocking collectives, shards(): row_total, mapped_count = lax.psum((covered, jnp.sum(mapped)), 'genome')  210 us
    psum x1, blocking collectives, shards(): lax.psum((jnp.sum(balanced, axis=0), jnp.sum(pair_mask, axis=0)), 'genome')  101 us
    ppermute x20, starting transfers between devices, shifted(): lax.ppermute(value, axis, [(source, source + steps) for source in range(l...  60.6 us
    ppermute x20, waiting for transfers between devices, shifted(): lax.ppermute(value, axis, [(source, source + steps) for source in range(l...  23.3 us
    select_n x2, other arithmetic, tail_values(): return jnp.where(keep_mask, tail_prob, 1.0)  16.5 us
  transfers between devices with their start and end apart: 22, of which 6 were waited for; matrix products, arithmetic and copies ran while one was open for 0% of the time, Pallas kernels for 0%

commit v1 on v0

--- a/solution.py
+++ b/solution.py
@@ -87,6 +87,21 @@
     return (donut_sum, lower_sum)
 
 
+def gathered(value, groups):
+    count = len(groups[0])
+    copies = jnp.broadcast_to(value[None], (count,) + value.shape)
+    return lax.all_to_all(copies, "genome", 0, 0, axis_index_groups=groups)
+
+
+def total_over_genome(value):
+    count = lax.axis_size("genome")
+    near = min(count, 32)
+    planes = [[start + i for i in range(near)] for start in range(0, count, near)]
+    lines = [[i + start for start in range(0, count, near)] for i in range(near)]
+    value = jnp.sum(gathered(value, planes), axis=0)
+    return jnp.sum(gathered(value, lines), axis=0)
+
+
 def poisson_tail(counts, local_mean):
     shape_k = jnp.maximum(counts.astype(jnp.float32), 1.0)
     ninth = 1.0 / (9.0 * shape_k)
@@ -118,6 +133,7 @@
 
     bias_vec = jnp.ones((row_count,), jnp.float32)
     inverse = mapped
+    covered = []
     for iteration in range(ITERS):
         ahead_band = hankel(inverse_ahead(inverse), row_count, band_width)
         balanced = counts_float * inverse[:, None] * ahead_band
@@ -127,16 +143,22 @@
             row_sums = row_sums + shifted(
                 spread[hop_count * row_count : (hop_count + 1) * row_count], "genome", hop_count
             )
-        covered = jnp.sum(mapped * row_sums)
-        row_total, mapped_count = lax.psum((covered, jnp.sum(mapped)), "genome")
-        bias_vec = jnp.where(mappable > 0, bias_vec * row_sums / (row_total / mapped_count), 1.0)
+        covered.append(jnp.sum(mapped * row_sums))
+        bias_vec = jnp.where(mappable > 0, bias_vec * row_sums, 1.0)
         inverse = jnp.where(mappable > 0, 1.0 / bias_vec, 0.0)
     ahead_band = hankel(inverse_ahead(inverse), row_count, band_width)
     balanced = counts_float * inverse[:, None] * ahead_band
     pair_mask = mapped[:, None] * (ahead_band > 0).astype(jnp.float32)
-    diag_total, pair_total = lax.psum(
-        (jnp.sum(balanced, axis=0), jnp.sum(pair_mask, axis=0)), "genome"
+    totals = total_over_genome(
+        jnp.concatenate(
+            [jnp.sum(balanced, axis=0), jnp.sum(pair_mask, axis=0), jnp.stack(covered)]
+        )
     )
+    diag_total, pair_total = totals[:band_width], totals[band_width : 2 * band_width]
+    mapped_count = pair_total[0]
+    for iteration in range(ITERS):
+        average = totals[2 * band_width + iteration] / mapped_count
+        bias_vec = jnp.where(mappable > 0, bias_vec / average, 1.0)
     expected = diag_total / pair_total
     rows_in = with_halo(balanced, (("genome", 0),), OUTER)
     donut_obs, lower_obs = shear_sums(rows_in)

time: 470 us -> 211 us (0.45)
  the two profiles are of different devices: /device:TPU:31 before, /device:TPU:32 now
where the time goes in v1:
time: 211 us; the launch traced here: 209 us
  starting transfers between devices  97.6 us (46%)
  other arithmetic  39.7 us (19%)
  waiting for transfers between devices  38.5 us (18%)
  local copies, waits for them, and re-layouts  29.6 us (14%)
  between operations  3.8 us (2%)
    ppermute x20, starting transfers between devices, shifted(): lax.ppermute(value, axis, [(source, source + steps) for source in range(l...  64.3 us
    all_to_all x2, starting transfers between devices, gathered(): return lax.all_to_all(copies, 'genome', 0, 0, axis_index_groups=groups)  23.4 us
    ppermute x20, waiting for transfers between devices, shifted(): lax.ppermute(value, axis, [(source, source + steps) for source in range(l...  20.5 us
    select_n x2, other arithmetic, tail_values(): return jnp.where(keep_mask, tail_prob, 1.0)  19.4 us
    all_to_all x2, waiting for transfers between devices, gathered(): return lax.all_to_all(copies, 'genome', 0, 0, axis_index_groups=groups)  18 us
    ppermute x1, starting transfers between devices, with_halo(): lax.ppermute(head, axis, [((i + 1) % count, i) for i in range(ends)])  7.86 us
    reshape x3, local copies, waits for them, and re-layouts, hankel(): return tiled_row.reshape(row_count, line_len)[:, :band_width]  6.9 us
    reshape x4, local copies, waits for them, and re-layouts, column_sums(): padded.reshape(-1)[:row_count * line_len].reshape(row_count, line_len)  6.48 us
  transfers between devices with their start and end apart: 24, of which 9 were waited for; matrix products, arithmetic and copies ran while one was open for 4% of the time, Pallas kernels for 0%

profile of v1, /device:TPU:32, one launch (start us, length us, event | category | flops | bytes accessed | tf_op | source)
XLA Modules:
  0.0 209.1 jit_solution(531787943246910888)
XLA Ops:
  1.3 6.8 %collective-permute-start.3 = (f32[256]{0:T(256)S(1)}, f32[256]{0:T(256)S(1)}, u32[]{:S(2)}, u32[]{:S(2)}) collective-permute-start(f32[256]{0:T(256)S(1)} %convert_element_type.17), channel_id=1, source_target_pairs={{4,0},{5,1},{6,2},{7,3},{8,4},{9,5},{10,6},{11,7},{12,8},{13,9},{1... | collective-permute-start | bytes 3080 | tf_op jit(solution)/shard_map/ppermute | solution.py:14
  10.1 4.7 %collective-permute-start.1 = (f32[256]{0:T(256)S(1)}, f32[256]{0:T(256)S(1)}, u32[]{:S(2)}, u32[]{:S(2)}) collective-permute-start(f32[256]{0:T(256)S(1)} %convert_element_type.17), channel_id=1, source_target_pairs={{2,0},{3,1},{4,2},{5,3},{6,4},{7,5},{8,6},{9,7},{10,8},{11,9},{12,... | collective-permute-start | bytes 3080 | tf_op jit(solution)/shard_map/ppermute | solution.py:14
  32.7 4.5 %collective-permute-start.7 = (f32[256]{0:T(256)S(1)}, f32[256]{0:T(256)S(1)}, u32[]{:S(2)}, u32[]{:S(2)}) collective-permute-start(f32[256]{0:T(256)S(1)} %get-tuple-element.41), channel_id=1, source_target_pairs={{0,4},{1,5},{2,6},{3,7},{4,8},{5,9},{6,10},{7,11},{8,12},{9,13},{1... | collective-permute-start | bytes 3080 | tf_op jit(solution)/shard_map/ppermute | solution.py:14
  37.2 3.5 %collective-permute-start.6 = (f32[256]{0:T(256)S(1)}, f32[256]{0:T(256)S(1)}, u32[]{:S(2)}, u32[]{:S(2)}) collective-permute-start(f32[256]{0:T(256)S(1)} %get-tuple-element.42), channel_id=1, source_target_pairs={{0,3},{1,4},{2,5},{3,6},{4,7},{5,8},{6,9},{7,10},{8,11},{9,12},{10... | collective-permute-start | bytes 3080 | tf_op jit(solution)/shard_map/ppermute | solution.py:14
  40.7 2.6 %collective-permute-start.5 = (f32[256]{0:T(256)S(1)}, f32[256]{0:T(256)S(1)}, u32[]{:S(2)}, u32[]{:S(2)}) collective-permute-start(f32[256]{0:T(256)S(1)} %get-tuple-element.43), channel_id=1, source_target_pairs={{0,2},{1,3},{2,4},{3,5},{4,6},{5,7},{6,8},{7,9},{8,10},{9,11},{10,... | collective-permute-start | bytes 3080 | tf_op jit(solution)/shard_map/ppermute | solution.py:14
  43.2 3.3 %collective-permute-done.6 = f32[256]{0:T(256)S(1)} collective-permute-done((f32[256]{0:T(256)S(1)}, f32[256]{0:T(256)S(1)}, u32[]{:S(2)}, u32[]{:S(2)}) %collective-permute-start.6) | collective-permute-done | bytes 1056 | tf_op jit(solution)/shard_map/ppermute | solution.py:14
  46.6 3.7 %collective-permute-done.5 = f32[256]{0:T(256)S(1)} collective-permute-done((f32[256]{0:T(256)S(1)}, f32[256]{0:T(256)S(1)}, u32[]{:S(2)}, u32[]{:S(2)}) %collective-permute-start.5) | collective-permute-done | bytes 1056 | tf_op jit(solution)/shard_map/ppermute | solution.py:14
  50.4 2.6 %collective-permute-start.8 = (f32[256]{0:T(256)S(1)}, f32[256]{0:T(256)S(1)}, u32[]{:S(2)}, u32[]{:S(2)}) collective-permute-start(f32[256]{0:T(256)S(1)} %get-tuple-element.21), channel_id=1, source_target_pairs={{1,0},{2,1},{3,2},{4,3},{5,4},{6,5},{7,6},{8,7},{9,8},{10,9},{11,1... | collective-permute-start | bytes 3080 | tf_op jit(solution)/shard_map/ppermute | solution.py:14
  54.9 4.9 %collective-permute-start.10 = (f32[256]{0:T(256)S(1)}, f32[256]{0:T(256)S(1)}, u32[]{:S(2)}, u32[]{:S(2)}) collective-permute-start(f32[256]{0:T(256)S(1)} %get-tuple-element.21), channel_id=1, source_target_pairs={{3,0},{4,1},{5,2},{6,3},{7,4},{8,5},{9,6},{10,7},{11,8},{12,9},{13... | collective-permute-start | bytes 3080 | tf_op jit(solution)/shard_map/ppermute | solution.py:14
  59.7 2.6 %collective-permute-start.9 = (f32[256]{0:T(256)S(1)}, f32[256]{0:T(256)S(1)}, u32[]{:S(2)}, u32[]{:S(2)}) collective-permute-start(f32[256]{0:T(256)S(1)} %get-tuple-element.21), channel_id=1, source_target_pairs={{2,0},{3,1},{4,2},{5,3},{6,4},{7,5},{8,6},{9,7},{10,8},{11,9},{12,... | collective-permute-start | bytes 3080 | tf_op jit(solution)/shard_map/ppermute | solution.py:14
  62.4 2.8 %collective-permute-done.9 = f32[256]{0:T(256)S(1)} collective-permute-done((f32[256]{0:T(256)S(1)}, f32[256]{0:T(256)S(1)}, u32[]{:S(2)}, u32[]{:S(2)}) %collective-permute-start.9) | collective-permute-done | bytes 1056 | tf_op jit(solution)/shard_map/ppermute | solution.py:14
  82.1 5.5 %collective-permute-start.14 = (f32[256]{0:T(256)S(1)}, f32[256]{0:T(256)S(1)}, u32[]{:S(2)}, u32[]{:S(2)}) collective-permute-start(f32[256]{0:T(256)S(1)} %get-tuple-element.38), channel_id=1, source_target_pairs={{0,3},{1,4},{2,5},{3,6},{4,7},{5,8},{6,9},{7,10},{8,11},{9,12},{10... | collective-permute-start | bytes 3080 | tf_op jit(solution)/shard_map/ppermute | solution.py:14
  91.5 5.8 %collective-permute-done.13 = f32[256]{0:T(256)S(1)} collective-permute-done((f32[256]{0:T(256)S(1)}, f32[256]{0:T(256)S(1)}, u32[]{:S(2)}, u32[]{:S(2)}) %collective-permute-start.13) | collective-permute-done | bytes 1056 | tf_op jit(solution)/shard_map/ppermute | solution.py:14
  102.3 5.0 %collective-permute-start.18 = (f32[256]{0:T(256)S(1)}, f32[256]{0:T(256)S(1)}, u32[]{:S(2)}, u32[]{:S(2)}) collective-permute-start(f32[256]{0:T(256)S(1)} %get-tuple-element.19), channel_id=1, source_target_pairs={{3,0},{4,1},{5,2},{6,3},{7,4},{8,5},{9,6},{10,7},{11,8},{12,9},{13... | collective-permute-start | bytes 3080 | tf_op jit(solution)/shard_map/ppermute | solution.py:14
  107.3 3.2 %collective-permute-start.17 = (f32[256]{0:T(256)S(1)}, f32[256]{0:T(256)S(1)}, u32[]{:S(2)}, u32[]{:S(2)}) collective-permute-start(f32[256]{0:T(256)S(1)} %get-tuple-element.19), channel_id=1, source_target_pairs={{2,0},{3,1},{4,2},{5,3},{6,4},{7,5},{8,6},{9,7},{10,8},{11,9},{12,... | collective-permute-start | bytes 3080 | tf_op jit(solution)/shard_map/ppermute | solution.py:14
  114.1 2.5 %slice.505 = f32[327936]{0:T(1024)} slice(f32[328960]{0:T(1024)} %tile.32), slice={[0:327936]} | slice | bytes 2623488 | tf_op jit(solution)/shard_map/slice | solution.py:36
  122.2 7.9 %collective-permute-start.21 = (f32[5,1024]{1,0:T(8,128)S(1)}, f32[5,1024]{1,0:T(8,128)S(1)}, u32[]{:S(2)}, u32[]{:S(2)}) collective-permute-start(f32[5,1024]{1,0:T(8,128)S(1)} %get-tuple-element.32), channel_id=1, source_target_pairs={{1,0},{2,1},{3,2},{4,3},{5,4},{6,5},{7,6},{8,7},{9,8},{10,9},{11,1... | collective-permute-start | bytes 61448 | tf_op jit(solution)/shard_map/ppermute | solution.py:27
  132.9 4.6 %all-to-all-start = ((f32[32,1,2050]{2,1,0:T(1,128)}), f32[32,1,2050]{2,1,0:T(1,128)}, u32[]{:S(2)}, u32[]{:S(2)}) async-start(f32[32,1,2050]{2,1,0:T(1,128)} %broadcast_in_dim.65), calls=%async_computation | async-start | bytes 557056 | tf_op jit(solution)/shard_map/all_to_all | solution.py:93
  137.9 8.6 %all-to-all-done = f32[32,1,2050]{2,1,0:T(1,128)} async-done(((f32[32,1,2050]{2,1,0:T(1,128)}), f32[32,1,2050]{2,1,0:T(1,128)}, u32[]{:S(2)}, u32[]{:S(2)}) %all-to-all-start) | async-done | bytes 262432 | tf_op jit(solution)/shard_map/all_to_all | solution.py:93
  148.4 18.8 %all-to-all-start.1 = ((f32[16,1,2050]{2,1,0:T(1,128)}), f32[16,1,2050]{2,1,0:T(1,128)}, u32[]{:S(2)}, u32[]{:S(2)}) async-start(f32[16,1,2050]{2,1,0:T(1,128)} %broadcast_in_dim.66), calls=%async_computation.1 | async-start | bytes 278528 | tf_op jit(solution)/shard_map/all_to_all | solution.py:93
  167.2 5.2 %add_add_fusion = (f32[266,1034]{1,0:T(8,128)}, f32[266,1034]{1,0:T(8,128)}, f32[266,1034]{1,0:T(8,128)S(1)}, f32[266,1034]{1,0:T(8,128)}) fusion(f32[266,1044]{1,0:T(8,128)S(1)} %select_maximum_fusion), kind=kLoop, calls=%fused_computation.15 | loop fusion | flops 3850616 | bytes 16502640 | tf_op jit(solution)/shard_map/add | solution.py:56
  172.4 9.4 %all-to-all-done.1 = f32[16,1,2050]{2,1,0:T(1,128)} async-done(((f32[16,1,2050]{2,1,0:T(1,128)}), f32[16,1,2050]{2,1,0:T(1,128)}, u32[]{:S(2)}, u32[]{:S(2)}) %all-to-all-start.1) | async-done | bytes 131232 | tf_op jit(solution)/shard_map/all_to_all | solution.py:93
  189.7 12.4 %fusion.5 = f32[256,1024]{1,0:T(8,128)} fusion(f32[266,1044]{1,0:T(8,128)S(1)} %select_maximum_fusion, f32[266,1034]{1,0:T(8,128)S(1)} %get-tuple-element.29, f32[266,1034]{1,0:T(8,128)} %get-tuple-element.14, s32[256,1024]{1,0:T(8,128)S(1)} %copy-done.1, f32[256,1281]{1,0:T(8,128)} %copy-done.2, f32[1024]{0:T(1024)S(1)} %fusion.61, ...), kind=kLoop, calls=%fused_computation.20 | loop fusion | flops 27787264 | bytes 26487808 | tf_op jit(solution)/shard_map/jit(_where)/select_n | solution.py:118
  202.1 7.0 %fusion.8 = f32[256,1024]{1,0:T(8,128)} fusion(f32[266,1034]{1,0:T(8,128)S(1)} %copy-done, f32[266,1034]{1,0:T(8,128)S(1)} %copy-done.4, s32[256,1024]{1,0:T(8,128)S(1)} %copy-done.1, f32[256,1281]{1,0:T(8,128)S(1)} %copy-done.3, f32[1024]{0:T(1024)S(1)} %fusion.60, f32[1024]{0:T(1024)S(1)} %slice_divide_fusion, f32[256]{0:T(256)S(1)} %copy-done.11, ...), kind=kLoop, calls=%fused_computation.23 | loop fusion | flops 23330816 | bytes 10759168 | tf_op jit(solution)/shard_map/jit(_where)/select_n | solution.py:118
  (121 shorter events, 67.4 us)
Async XLA Ops:
  1.3 16.9 %collective-permute-start.3 = (f32[256]{0:T(256)S(1)}, f32[256]{0:T(256)S(1)}, u32[]{:S(2)}, u32[]{:S(2)}) collective-permute-start(f32[256]{0:T(256)S(1)} %convert_element_type.17), channel_id=1, source_target_pairs={{4,0},{5,1},{6,2},{7,3},{8,4},{9,5},{10,6},{11,7},{12,8},{13,9},{1... | collective-permute-start | bytes 3080 | tf_op jit(solution)/shard_map/ppermute | solution.py:14
  8.2 10.1 %collective-permute-start.2 = (f32[256]{0:T(256)S(1)}, f32[256]{0:T(256)S(1)}, u32[]{:S(2)}, u32[]{:S(2)}) collective-permute-start(f32[256]{0:T(256)S(1)} %convert_element_type.17), channel_id=1, source_target_pairs={{3,0},{4,1},{5,2},{6,3},{7,4},{8,5},{9,6},{10,7},{11,8},{12,9},{13... | collective-permute-start | bytes 3080 | tf_op jit(solution)/shard_map/ppermute | solution.py:14
  10.1 8.1 %collective-permute-start.1 = (f32[256]{0:T(256)S(1)}, f32[256]{0:T(256)S(1)}, u32[]{:S(2)}, u32[]{:S(2)}) collective-permute-start(f32[256]{0:T(256)S(1)} %convert_element_type.17), channel_id=1, source_target_pairs={{2,0},{3,1},{4,2},{5,3},{6,4},{7,5},{8,6},{9,7},{10,8},{11,9},{12,... | collective-permute-start | bytes 3080 | tf_op jit(solution)/shard_map/ppermute | solution.py:14
  14.8 3.4 %collective-permute-start = (f32[256]{0:T(256)S(1)}, f32[256]{0:T(256)S(1)}, u32[]{:S(2)}, u32[]{:S(2)}) collective-permute-start(f32[256]{0:T(256)S(1)} %convert_element_type.17), channel_id=1, source_target_pairs={{1,0},{2,1},{3,2},{4,3},{5,4},{6,5},{7,6},{8,7},{9,8},{10,9},{11,1... | collective-permute-start | bytes 3080 | tf_op jit(solution)/shard_map/ppermute | solution.py:14
  30.7 12.5 %collective-permute-start.4 = (f32[256]{0:T(256)S(1)}, f32[256]{0:T(256)S(1)}, u32[]{:S(2)}, u32[]{:S(2)}) collective-permute-start(f32[256]{0:T(256)S(1)} %get-tuple-element.40), channel_id=1, source_target_pairs={{0,1},{1,2},{2,3},{3,4},{4,5},{5,6},{6,7},{7,8},{8,9},{9,10},{10,1... | collective-permute-start | bytes 3080 | tf_op jit(solution)/shard_map/ppermute | solution.py:14
  32.7 10.6 %collective-permute-start.7 = (f32[256]{0:T(256)S(1)}, f32[256]{0:T(256)S(1)}, u32[]{:S(2)}, u32[]{:S(2)}) collective-permute-start(f32[256]{0:T(256)S(1)} %get-tuple-element.41), channel_id=1, source_target_pairs={{0,4},{1,5},{2,6},{3,7},{4,8},{5,9},{6,10},{7,11},{8,12},{9,13},{1... | collective-permute-start | bytes 3080 | tf_op jit(solution)/shard_map/ppermute | solution.py:14
  37.2 9.4 %collective-permute-start.6 = (f32[256]{0:T(256)S(1)}, f32[256]{0:T(256)S(1)}, u32[]{:S(2)}, u32[]{:S(2)}) collective-permute-start(f32[256]{0:T(256)S(1)} %get-tuple-element.42), channel_id=1, source_target_pairs={{0,3},{1,4},{2,5},{3,6},{4,7},{5,8},{6,9},{7,10},{8,11},{9,12},{10... | collective-permute-start | bytes 3080 | tf_op jit(solution)/shard_map/ppermute | solution.py:14
  40.7 9.7 %collective-permute-start.5 = (f32[256]{0:T(256)S(1)}, f32[256]{0:T(256)S(1)}, u32[]{:S(2)}, u32[]{:S(2)}) collective-permute-start(f32[256]{0:T(256)S(1)} %get-tuple-element.43), channel_id=1, source_target_pairs={{0,2},{1,3},{2,4},{3,5},{4,6},{5,7},{6,8},{7,9},{8,10},{9,11},{10,... | collective-permute-start | bytes 3080 | tf_op jit(solution)/shard_map/ppermute | solution.py:14
  50.4 12.0 %collective-permute-start.8 = (f32[256]{0:T(256)S(1)}, f32[256]{0:T(256)S(1)}, u32[]{:S(2)}, u32[]{:S(2)}) collective-permute-start(f32[256]{0:T(256)S(1)} %get-tuple-element.21), channel_id=1, source_target_pairs={{1,0},{2,1},{3,2},{4,3},{5,4},{6,5},{7,6},{8,7},{9,8},{10,9},{11,1... | collective-permute-start | bytes 3080 | tf_op jit(solution)/shard_map/ppermute | solution.py:14
  52.9 12.3 %collective-permute-start.11 = (f32[256]{0:T(256)S(1)}, f32[256]{0:T(256)S(1)}, u32[]{:S(2)}, u32[]{:S(2)}) collective-permute-start(f32[256]{0:T(256)S(1)} %get-tuple-element.21), channel_id=1, source_target_pairs={{4,0},{5,1},{6,2},{7,3},{8,4},{9,5},{10,6},{11,7},{12,8},{13,9},{1... | collective-permute-start | bytes 3080 | tf_op jit(solution)/shard_map/ppermute | solution.py:14
  54.9 10.4 %collective-permute-start.10 = (f32[256]{0:T(256)S(1)}, f32[256]{0:T(256)S(1)}, u32[]{:S(2)}, u32[]{:S(2)}) collective-permute-start(f32[256]{0:T(256)S(1)} %get-tuple-element.21), channel_id=1, source_target_pairs={{3,0},{4,1},{5,2},{6,3},{7,4},{8,5},{9,6},{10,7},{11,8},{12,9},{13... | collective-permute-start | bytes 3080 | tf_op jit(solution)/shard_map/ppermute | solution.py:14
  59.7 5.5 %collective-permute-start.9 = (f32[256]{0:T(256)S(1)}, f32[256]{0:T(256)S(1)}, u32[]{:S(2)}, u32[]{:S(2)}) collective-permute-start(f32[256]{0:T(256)S(1)} %get-tuple-element.21), channel_id=1, source_target_pairs={{2,0},{3,1},{4,2},{5,3},{6,4},{7,5},{8,6},{9,7},{10,8},{11,9},{12,... | collective-permute-start | bytes 3080 | tf_op jit(solution)/shard_map/ppermute | solution.py:14
  77.7 11.9 %collective-permute-start.12 = (f32[256]{0:T(256)S(1)}, f32[256]{0:T(256)S(1)}, u32[]{:S(2)}, u32[]{:S(2)}) collective-permute-start(f32[256]{0:T(256)S(1)} %get-tuple-element.36), channel_id=1, source_target_pairs={{0,1},{1,2},{2,3},{3,4},{4,5},{5,6},{6,7},{7,8},{8,9},{9,10},{10,1... | collective-permute-start | bytes 3080 | tf_op jit(solution)/shard_map/ppermute | solution.py:14
  79.7 10.0 %collective-permute-start.15 = (f32[256]{0:T(256)S(1)}, f32[256]{0:T(256)S(1)}, u32[]{:S(2)}, u32[]{:S(2)}) collective-permute-start(f32[256]{0:T(256)S(1)} %get-tuple-element.37), channel_id=1, source_target_pairs={{0,4},{1,5},{2,6},{3,7},{4,8},{5,9},{6,10},{7,11},{8,12},{9,13},{1... | collective-permute-start | bytes 3080 | tf_op jit(solution)/shard_map/ppermute | solution.py:14
  82.1 9.4 %collective-permute-start.14 = (f32[256]{0:T(256)S(1)}, f32[256]{0:T(256)S(1)}, u32[]{:S(2)}, u32[]{:S(2)}) collective-permute-start(f32[256]{0:T(256)S(1)} %get-tuple-element.38), channel_id=1, source_target_pairs={{0,3},{1,4},{2,5},{3,6},{4,7},{5,8},{6,9},{7,10},{8,11},{9,12},{10... | collective-permute-start | bytes 3080 | tf_op jit(solution)/shard_map/ppermute | solution.py:14
  87.6 9.7 %collective-permute-start.13 = (f32[256]{0:T(256)S(1)}, f32[256]{0:T(256)S(1)}, u32[]{:S(2)}, u32[]{:S(2)}) collective-permute-start(f32[256]{0:T(256)S(1)} %get-tuple-element.39), channel_id=1, source_target_pairs={{0,2},{1,3},{2,4},{3,5},{4,6},{5,7},{6,8},{7,9},{8,10},{9,11},{10,... | collective-permute-start | bytes 3080 | tf_op jit(solution)/shard_map/ppermute | solution.py:14
  98.0 12.6 %collective-permute-start.16 = (f32[256]{0:T(256)S(1)}, f32[256]{0:T(256)S(1)}, u32[]{:S(2)}, u32[]{:S(2)}) collective-permute-start(f32[256]{0:T(256)S(1)} %get-tuple-element.19), channel_id=1, source_target_pairs={{1,0},{2,1},{3,2},{4,3},{5,4},{6,5},{7,6},{8,7},{9,8},{10,9},{11,1... | collective-permute-start | bytes 3080 | tf_op jit(solution)/shard_map/ppermute | solution.py:14
  99.9 12.9 %collective-permute-start.19 = (f32[256]{0:T(256)S(1)}, f32[256]{0:T(256)S(1)}, u32[]{:S(2)}, u32[]{:S(2)}) collective-permute-start(f32[256]{0:T(256)S(1)} %get-tuple-element.19), channel_id=1, source_target_pairs={{4,0},{5,1},{6,2},{7,3},{8,4},{9,5},{10,6},{11,7},{12,8},{13,9},{1... | collective-permute-start | bytes 3080 | tf_op jit(solution)/shard_map/ppermute | solution.py:14
  102.3 10.5 %collective-permute-start.18 = (f32[256]{0:T(256)S(1)}, f32[256]{0:T(256)S(1)}, u32[]{:S(2)}, u32[]{:S(2)}) collective-permute-start(f32[256]{0:T(256)S(1)} %get-tuple-element.19), channel_id=1, source_target_pairs={{3,0},{4,1},{5,2},{6,3},{7,4},{8,5},{9,6},{10,7},{11,8},{12,9},{13... | collective-permute-start | bytes 3080 | tf_op jit(solution)/shard_map/ppermute | solution.py:14
  107.3 5.5 %collective-permute-start.17 = (f32[256]{0:T(256)S(1)}, f32[256]{0:T(256)S(1)}, u32[]{:S(2)}, u32[]{:S(2)}) collective-permute-start(f32[256]{0:T(256)S(1)} %get-tuple-element.19), channel_id=1, source_target_pairs={{2,0},{3,1},{4,2},{5,3},{6,4},{7,5},{8,6},{9,7},{10,8},{11,9},{12,... | collective-permute-start | bytes 3080 | tf_op jit(solution)/shard_map/ppermute | solution.py:14
  120.3 17.2 %collective-permute-start.20 = (f32[5,1024]{1,0:T(8,128)S(1)}, f32[5,1024]{1,0:T(8,128)S(1)}, u32[]{:S(2)}, u32[]{:S(2)}) collective-permute-start(f32[5,1024]{1,0:T(8,128)S(1)} %get-tuple-element.31), channel_id=1, source_target_pairs={{0,1},{1,2},{2,3},{3,4},{4,5},{5,6},{6,7},{7,8},{8,9},{9,10},{10,1... | collective-permute-start | bytes 61448 | tf_op jit(solution)/shard_map/ppermute | solution.py:25
  122.2 15.3 %collective-permute-start.21 = (f32[5,1024]{1,0:T(8,128)S(1)}, f32[5,1024]{1,0:T(8,128)S(1)}, u32[]{:S(2)}, u32[]{:S(2)}) collective-permute-start(f32[5,1024]{1,0:T(8,128)S(1)} %get-tuple-element.32), channel_id=1, source_target_pairs={{1,0},{2,1},{3,2},{4,3},{5,4},{6,5},{7,6},{8,7},{9,8},{10,9},{11,1... | collective-permute-start | bytes 61448 | tf_op jit(solution)/shard_map/ppermute | solution.py:27
  132.9 13.7 %all-to-all-start = ((f32[32,1,2050]{2,1,0:T(1,128)}), f32[32,1,2050]{2,1,0:T(1,128)}, u32[]{:S(2)}, u32[]{:S(2)}) async-start(f32[32,1,2050]{2,1,0:T(1,128)} %broadcast_in_dim.65), calls=%async_computation | async-start | bytes 557056 | tf_op jit(solution)/shard_map/all_to_all | solution.py:93
  148.4 33.4 %all-to-all-start.1 = ((f32[16,1,2050]{2,1,0:T(1,128)}), f32[16,1,2050]{2,1,0:T(1,128)}, u32[]{:S(2)}, u32[]{:S(2)}) async-start(f32[16,1,2050]{2,1,0:T(1,128)} %broadcast_in_dim.66), calls=%async_computation.1 | async-start | bytes 278528 | tf_op jit(solution)/shard_map/all_to_all | solution.py:93
  (18 other events, 319.8 us)

commit v2 on v0

v2 whole, which is shorter than its diff:
```python
import jax
import jax.numpy as jnp
from jax import lax
from jax.experimental import pallas as pl
from jax.experimental.pallas import tpu as pltpu
from jax.sharding import PartitionSpec as P

OUTER = 5
INNER = 2
ROWS = 256
BAND = 1024
LANE = 128
SLAB = ROWS // LANE
HOPS = BAND // ROWS
SPAN = ROWS + BAND
WIDE = SPAN + LANE
STEP = 32
EDGE = 8
MASKED = -1.0
VMEM = pl.BlockSpec(memory_space=pltpu.VMEM)
SMEM = pl.BlockSpec(memory_space=pltpu.SMEM)
F32 = jnp.float32
X_AT, SPREAD_AT, SUMS_AT, MESSAGE = 0, SLAB, SLAB * (HOPS + 2), 16


def lanes(tiles):
    return jnp.concatenate([tiles[r : r + 1] for r in range(tiles.shape[0])], axis=1)


def put_lanes(ref, first, row):
    for t in range(row.shape[1] // LANE):
        ref[first + t : first + t + 1, :] = row[:, t * LANE : (t + 1) * LANE]


def on_diagonal(start, count, width):
    rows = lax.broadcasted_iota(jnp.int32, (count, width), 0) + start
    return rows == lax.broadcasted_iota(jnp.int32, (count, width), 1)


def column_of(row, start, count):
    part = jnp.where(on_diagonal(start, count, ROWS), row, 0.0)
    return jnp.sum(part, axis=1, keepdims=True)


def fold(value):
    total = value[0:8]
    for r in range(8, value.shape[0], 8):
        total = total + value[r : r + 8]
    return total


def spread_of(skewed_ref, weight_row):
    total = jnp.zeros((8, SPAN), F32)
    for start in range(0, ROWS, STEP):
        weight = column_of(weight_row, start, STEP)
        part = skewed_ref[start : start + STEP, :] * weight
        part = jnp.where(on_diagonal(start, STEP, SPAN), 0.0, part)
        total = total + fold(part)
    return jnp.sum(total, axis=0, keepdims=True)


def own_sums(skewed_ref, ahead_row):
    total = jnp.zeros((8, ROWS), F32)
    for start in range(0, ROWS, STEP):
        part = skewed_ref[start : start + STEP, :] * ahead_row
        sums = jnp.sum(part, axis=1, keepdims=True)
        total = total + fold(jnp.where(on_diagonal(start, STEP, ROWS), sums, 0.0))
    return jnp.sum(total, axis=0, keepdims=True)


def put_message(out_ref, x_row, spread_row, sums_row):
    out_ref[...] = jnp.zeros((MESSAGE, LANE), F32)
    put_lanes(out_ref, X_AT, x_row)
    put_lanes(out_ref, SPREAD_AT, spread_row)
    put_lanes(out_ref, SUMS_AT, sums_row)


def begin_kernel(contacts_ref, mapped_ref, skewed_ref, out_ref):
    mapped = lanes(mapped_ref[...]).astype(F32)
    for start in range(0, ROWS, STEP):
        counts = contacts_ref[start : start + STEP, :].astype(F32)
        padded = jnp.concatenate([counts, jnp.zeros((STEP, SPAN - BAND), F32)], axis=1)
        skewed_ref[start : start + STEP, :] = pltpu.roll(padded, start, 1, stride=1, stride_axis=0)
    put_message(out_ref, mapped, spread_of(skewed_ref, mapped), jnp.zeros((1, ROWS), F32))


def ahead_of(core, slabs):
    tiles = [jnp.where(core == 0, slabs[k], slabs[k + 1]) for k in range(HOPS + 1)]
    return jnp.concatenate([lanes(t) for t in tiles], axis=1)


def sum_rows(core_ref, skewed_ref, pair_ref, near_ref, far_ref, mapped_ref):
    core = core_ref[0]

    def message(k):
        at = k % 2
        chip = k // 2
        if chip == 0:
            return pair_ref.at[at]
        ref = near_ref if abs(chip) == 1 else far_ref
        return ref.at[1 if chip > 0 else 0, at]

    x_tiles = [message(k)[X_AT : X_AT + SLAB, :] for k in range(HOPS + 2)]
    arrived = jnp.zeros((SLAB, LANE), F32)
    for k in range(HOPS + 1):
        at = SPREAD_AT + SLAB * k
        arrived = arrived + jnp.where(
            core == 0, message(-k)[at : at + SLAB, :], message(1 - k)[at : at + SLAB, :]
        )
    sums = own_sums(skewed_ref, ahead_of(core, x_tiles)) + lanes(arrived)
    x_row = lanes(jnp.where(core == 0, x_tiles[0], x_tiles[1]))
    mapped = lanes(mapped_ref[...]) > 0
    return mapped, x_row * sums


def middle_kernel(core_ref, skewed_ref, pair_ref, near_ref, far_ref, mapped_ref, out_ref):
    mapped, sums = sum_rows(core_ref, skewed_ref, pair_ref, near_ref, far_ref, mapped_ref)
    x_row = jnp.where(mapped, 1.0 / jnp.where(mapped, sums, 1.0), 0.0)
    put_message(out_ref, x_row, spread_of(skewed_ref, x_row), sums)


def last_kernel(core_ref, skewed_ref, pair_ref, near_ref, far_ref, mapped_ref, out_ref):
    mapped, sums = sum_rows(core_ref, skewed_ref, pair_ref, near_ref, far_ref, mapped_ref)
    before = jnp.where(core_ref[0] == 0, pair_ref[0], pair_ref[1])
    before = lanes(before[SUMS_AT : SUMS_AT + SLAB])
    bias = jnp.where(mapped, before * sums, 1.0)
    out_ref[...] = jnp.zeros((8, LANE), F32)
    put_lanes(out_ref, 0, jnp.where(mapped, 1.0 / bias, 0.0))
    put_lanes(out_ref, SLAB, bias)
    for at, value in ((4, before), (5, sums)):
        total = jnp.sum(jnp.where(mapped, value, 0.0), axis=1, keepdims=True)
        out_ref[at : at + 1, :] = jnp.broadcast_to(total, (1, LANE))


def along_diagonals(rows_of, width):
    total = None
    for g in range(LANE // 8):
        part = None
        for h in range(SLAB):
            rows = rows_of(h * LANE + 8 * g)
            rows = rows[:, h * LANE : h * LANE + SPAN - LANE]
            part = rows if part is None else part + rows
        if g:
            part = pltpu.roll(part, SPAN - LANE - 8 * g, 1)
        total = part if total is None else total + part
    out = total[0:1, :width]
    for s in range(1, 8):
        out = out + pltpu.roll(total, SPAN - LANE - s, 1)[s : s + 1, :width]
    return out


def band_kernel(core_ref, skewed_ref, pair_ref, ahead_ref, own_ref, final_ref, swap_ref, cross_ref, sums_ref):
    core = core_ref[0]
    slabs = [pair_ref[0], pair_ref[1], ahead_ref[0, 0], ahead_ref[0, 1], ahead_ref[1, 0], ahead_ref[1, 1]]
    ahead = ahead_of(core, [s[X_AT : X_AT + SLAB] for s in slabs])
    x_row = ahead[:, :ROWS]
    for start in range(0, ROWS, STEP):
        final_ref[start : start + STEP, :] = (
            skewed_ref[start : start + STEP, :] * column_of(x_row, start, STEP) * ahead
        )
    first, last = final_ref[0:EDGE, :], final_ref[ROWS - EDGE : ROWS, :]
    swap_ref[...] = jnp.where(core == 0, last, first)
    cross_ref[...] = jnp.where(core == 0, first, last)
    mapped_ahead = (ahead > 0).astype(F32)
    mapped_row = mapped_ahead[:, :ROWS]
    diagonals = along_diagonals(lambda r: final_ref[r : r + 8, :], BAND)
    pairs = along_diagonals(lambda r: column_of(mapped_row, r, 8) * mapped_ahead, BAND)
    own = own_ref[...]
    row = jnp.concatenate([diagonals, pairs, own[4:5, : LANE // 2], own[5:6, : LANE // 2]], axis=1)
    for n in range(sums_ref.shape[0]):
        sums_ref[n] = row


def straight(rows, start):
    if start:
        rows = pltpu.roll(rows, SPAN - start, 1)
    rows = rows[:, : BAND + LANE]
    row = lax.broadcasted_iota(jnp.int32, rows.shape, 0)
    for step in (1, 2, 4):
        rows = jnp.where((row & step) > 0, pltpu.roll(rows, BAND + LANE - step, 1), rows)
    return rows[:, :BAND]


def window_kernel(core_ref, final_ref, swap_ref, cross_ref, pair_ref, ahead_ref, contacts_ref,
                  donut_ref, lower_ref, base_ref, edged_ref, lefts_ref, sides_ref, left_in_ref, sides_in_ref):
    core = core_ref[0]
    slabs = [pair_ref[0], pair_ref[1], ahead_ref[0, 0], ahead_ref[0, 1], ahead_ref[1, 0], ahead_ref[1, 1]]

    swap, cross = swap_ref[...], cross_ref[...]
    before = jnp.where(core == 0, cross, swap)
    after = jnp.where(core == 0, swap, cross)
    gap = jnp.zeros((EDGE, LANE), F32)
    edged_ref[0:EDGE, :] = jnp.concatenate(
        [before[:, ROWS:], gap, before[:, :ROWS]], axis=1
    )
    edged_ref[ROWS + EDGE :, :] = jnp.concatenate(
        [gap] * SLAB + [after[:, : WIDE - ROWS]], axis=1
    )
    edged_ref[EDGE : ROWS + EDGE, :SPAN] = final_ref[...]
    edged_ref[EDGE : ROWS + EDGE, SPAN:] = jnp.zeros((ROWS, WIDE - SPAN), F32)
    for start in range(0, ROWS + 2 * EDGE, 16):
        cells = edged_ref[start : start + 16, :]
        two = cells + pltpu.roll(cells, WIDE - 1, 1)
        three = two + pltpu.roll(cells, WIDE - 2, 1)
        left_out = pltpu.roll(three, 5, 1)
        left_in = pltpu.roll(two, 2, 1)
        lefts_ref[start : start + 16, :] = left_out
        left_in_ref[start : start + 16, :] = left_in
        sides_ref[start : start + 16, :] = left_out + pltpu.roll(three, WIDE - 3, 1)
        sides_in_ref[start : start + 16, :] = left_in + pltpu.roll(two, WIDE - 1, 1)

    ahead = ahead_of(core, [s[X_AT : X_AT + SLAB] for s in slabs])
    mapped = ahead > 0
    bias_ahead = jnp.where(mapped, 1.0 / jnp.where(mapped, ahead, 1.0), 0.0)
    bias_row = bias_ahead[:, :ROWS]
    def band_rows(sums, start):
        weight = column_of(bias_row, start, STEP) * bias_ahead
        value = jnp.where(weight > 0, jnp.maximum(sums, 0.0) * weight, MASKED)
        return jnp.concatenate([straight(value[r : r + 8], start + r) for r in range(0, STEP, 8)], axis=0)

    for start in range(0, ROWS, STEP):

        def rows(ref, shift):
            at = start + EDGE + shift
            return ref[at : at + STEP, :SPAN]

        shifts = range(1, OUTER + 1)
        lower = sum(rows(lefts_ref, a) for a in shifts)
        lower = lower + sum(rows(left_in_ref, a) for a in shifts if a > INNER)
        donut = sum(rows(sides_ref, a) + rows(sides_ref, -a) for a in shifts)
        donut = donut + sum(rows(sides_in_ref, a) + rows(sides_in_ref, -a) for a in shifts if a > INNER)
        counts = contacts_ref[start : start + STEP, :]
        k = jnp.maximum(counts, 1).astype(F32)
        inverse_k = 1.0 / k
        scale = jnp.sqrt(k) * (3.0 / 2.0**0.5)
        distance = lax.broadcasted_iota(jnp.int32, (STEP, BAND), 1)
        keep = (counts > 0) & (distance >= 2 * OUTER)
        base = (1.0 - inverse_k * (1.0 / 9.0)) * scale
        for sums, out_ref in ((donut, donut_ref), (lower, lower_ref)):
            value = band_rows(sums, start)
            ok = keep & (value >= 0.0)
            root = jnp.where(value > 0.0, jnp.exp(jnp.log(jnp.where(value > 0.0, value, 1.0) * inverse_k) * (1.0 / 3.0)), 0.0)
            out_ref[start : start + STEP, :] = jnp.where(ok, root * scale, MASKED)
        base_ref[start : start + STEP, :] = base


def half_erfc(x):
    size = jnp.abs(x)
    t = 1.0 / (1.0 + 0.5 * size)
    poly = 0.17087277
    for c in (-0.82215223, 1.48851587, -1.13520398, 0.27886807, -0.18628806, 0.09678418, 0.37409196, 1.00002368, -1.26551223):
        poly = poly * t + c
    tail = 0.5 * t * jnp.exp(poly - size * size)
    return jnp.where(x >= 0.0, tail, 1.0 - tail)


def filter_sums(expected):
    margin = 2 * OUTER
    padded = jnp.concatenate([expected, jnp.zeros((1, LANE), F32)], axis=1)
    donut_weight, lower_weight = {}, {}
    for a in range(-OUTER, OUTER + 1):
        for c in range(-OUTER, OUTER + 1):
            if a and c and not (abs(a) <= INNER and abs(c) <= INNER):
                donut_weight[c - a] = donut_weight.get(c - a, 0) + 1
            if a >= 1 and c <= -1 and not (a <= INNER and c >= -INNER):
                lower_weight[c - a] = lower_weight.get(c - a, 0) + 1
    donut = lower = None
    for k in range(-margin, margin + 1):
        moved = pltpu.roll(padded, (-k) % (BAND + LANE), 1) if k else padded
        moved = moved[:, :BAND]
        if k in donut_weight:
            part = moved * float(donut_weight[k])
            donut = part if donut is None else donut + part
        if k in lower_weight:
            part = moved * float(lower_weight[k])
            lower = part if lower is None else lower + part
    return donut, lower


def cube_root(value):
    positive = value > 0.0
    root = jnp.exp(jnp.log(jnp.where(positive, value, 1.0)) * (1.0 / 3.0))
    return jnp.where(positive, root, value)


def tail_kernel(sums_ref, own_ref, donut_ref, lower_ref, base_ref, pvalue_donut_ref, pvalue_lower_ref, bias_ref, ratio_ref):
    @pl.when(pl.program_id(0) == 0)
    def _():
        total = sums_ref[0]
        for n in range(1, sums_ref.shape[0]):
            total = total + sums_ref[n]
        diagonals, pairs = total[:, :BAND], total[:, BAND : 2 * BAND]
        expected = diagonals / pairs
        donut_exp, lower_exp = filter_sums(expected)
        ratio_ref[0:1, :] = cube_root(expected / donut_exp)
        ratio_ref[1:2, :] = cube_root(expected / lower_exp)
        mapped_count = pairs[:, 0:1]
        half = LANE // 2
        first = total[:, 2 * BAND : 2 * BAND + 1] / mapped_count
        second = total[:, 2 * BAND + half : 2 * BAND + half + 1] / mapped_count
        own = own_ref[...]
        bias = own[SLAB : 2 * SLAB]
        mapped = own[0:SLAB] > 0
        bias_ref[...] = jnp.where(mapped, bias / first / second, 1.0)

    count = base_ref.shape[0]
    for start in range(0, count, STEP):
        base = base_ref[start : start + STEP, :]
        for at, root_ref, out_ref in ((0, donut_ref, pvalue_donut_ref), (1, lower_ref, pvalue_lower_ref)):
            root = root_ref[start : start + STEP, :]
            value = half_erfc(base - root * ratio_ref[at : at + 1, :])
            out_ref[start : start + STEP, :] = jnp.where(root < 0.0, 1.0, value)


def params(mib=48):
    return pltpu.CompilerParams(vmem_limit_bytes=mib * 2**20)


def cost(flops, moved):
    return pl.CostEstimate(flops=flops, bytes_accessed=moved, transcendentals=0)


def call(kernel, ins, outs, specs=None):
    return pl.pallas_call(
        kernel,
        out_shape=[jax.ShapeDtypeStruct(s, F32) for s in outs],
        in_specs=specs or [VMEM] * len(ins),
        out_specs=[VMEM] * len(outs),
        compiler_params=params(),
    )(*ins)


def begin(contacts, mapped):
    return call(begin_kernel, (contacts, mapped), [(ROWS, SPAN), (MESSAGE, LANE)])


def middle(core, skewed, pair, near, far, mapped):
    return call(middle_kernel, (core, skewed, pair, near, far, mapped), [(MESSAGE, LANE)], [SMEM] + [VMEM] * 5)[0]


def last(core, skewed, pair, near, far, mapped):
    return call(last_kernel, (core, skewed, pair, near, far, mapped), [(8, LANE)], [SMEM] + [VMEM] * 5)[0]


def final_band(core, skewed, pair, ahead, own, copies):
    return call(
        band_kernel,
        (core, skewed, pair, ahead, own),
        [(ROWS, SPAN), (EDGE, SPAN), (EDGE, SPAN), (copies, 1, 2 * BAND + LANE)],
        [SMEM] + [VMEM] * 4,
    )


def whole(shape):
    return pl.BlockSpec(shape, lambda i: (0,) * len(shape))


def windows(core, final, swap, cross, pair, ahead, contacts):
    return pl.pallas_call(
        window_kernel,
        out_shape=[jax.ShapeDtypeStruct((ROWS, BAND), F32)] * 3,
        in_specs=[SMEM] + [VMEM] * 6,
        out_specs=[VMEM] * 3,
        scratch_shapes=[pltpu.VMEM((ROWS + 2 * EDGE, WIDE), F32)] * 5,
        compiler_params=params(),
        cost_estimate=cost(2 * 10**7, 6 * 2**20),
    )(core, final, swap, cross, pair, ahead, contacts)


def tails(sums, own, donut, lower, base, count=64):
    block = pl.BlockSpec((count, BAND), lambda i: (i, 0))
    return pl.pallas_call(
        tail_kernel,
        grid=(ROWS // count,),
        out_shape=[jax.ShapeDtypeStruct((ROWS, BAND), F32)] * 2 + [jax.ShapeDtypeStruct((SLAB, LANE), F32)],
        in_specs=[whole(sums.shape), whole(own.shape)] + [block] * 3,
        out_specs=[block] * 2 + [whole((SLAB, LANE))],
        scratch_shapes=[pltpu.VMEM((8, BAND), F32)],
        compiler_params=params(),
    )(sums, own, donut, lower, base)


def solution(mesh):
    count = mesh.shape["genome"]
    plane = min(32, count)
    chips = [[i, i + 1] for i in range(0, count, 2)]
    planes = [[start + i for i in range(plane)] for start in range(0, count, plane)]
    lines = [[i + start for start in range(0, count, plane)] for i in range(plane)]

    def both_cores(value):
        return lax.all_gather(value, "genome", axis_index_groups=chips)

    def moved(value, target):
        pairs = [(i, target(i)) for i in range(count)]
        return lax.ppermute(value, "genome", [(i, t) for i, t in pairs if 0 <= t < count])

    def around(message):
        pair = both_cores(message)
        near = moved(pair, lambda i: i + 2 if i % 2 == 0 else i - 2)
        far = moved(pair, lambda i: i + 4 if i % 2 == 0 else i - 4)
        return pair, both_cores(near), both_cores(far)

    def shards(contacts, mappable):
        core = lax.rem(lax.axis_index("genome"), 2).astype(jnp.int32).reshape(1)
        mapped = mappable.reshape(SLAB, LANE)
        skewed, message = begin(contacts, mapped)
        message = middle(core, skewed, *around(message), mapped)
        own = last(core, skewed, *around(message), mapped)
        pair = both_cores(own)
        ahead = both_cores(moved(pair, lambda i: i - 2 if i % 2 == 0 else i - 4))
        final, swap, cross, sums = final_band(core, skewed, pair, ahead, own, plane)
        swap = moved(swap, lambda i: i ^ 1)
        cross = moved(cross, lambda i: i - 1 if i % 2 == 0 else i + 1)
        sums = lax.all_to_all(sums, "genome", 0, 0, axis_index_groups=planes)
        sums = jnp.broadcast_to(jnp.sum(sums, axis=0, keepdims=True), (count // plane,) + sums.shape[1:])
        sums = lax.all_to_all(sums, "genome", 0, 0, axis_index_groups=lines)
        donut, lower, base = windows(core, final, swap, cross, pair, ahead, contacts)
        pvalue_donut, pvalue_lower, bias = tails(sums, own, donut, lower, base)
        return pvalue_donut, pvalue_lower, bias.reshape(ROWS)

    placed = (P("genome", None), P("genome"))
    return jax.shard_map(
        shards,
        mesh=mesh,
        in_specs=placed,
        out_specs=(P("genome", None), P("genome", None), P("genome")),
        check_vma=False,
    )
```

time: 470 us -> 123 us (0.26)
  the two profiles are of different devices: /device:TPU:31 before, /device:TPU:32 now
where the time goes in v2:
time: 123 us; the launch traced here: 122 us
  starting transfers between devices  35.9 us (29%)
  blocking collectives  30.8 us (25%)
  Pallas kernels  24.3 us (20%)
  waiting for transfers between devices  21 us (17%)
  local copies, waits for them, and re-layouts  9.29 us (8%)
    ppermute x7, waiting for transfers between devices, moved(): lax.ppermute(value, 'genome', [(i, t) for i, t in pairs if 0 <= t < count])  21 us
    ppermute x7, starting transfers between devices, moved(): lax.ppermute(value, 'genome', [(i, t) for i, t in pairs if 0 <= t < count])  19.4 us
    pallas_call x1, Pallas kernels, windows(): pl.pallas_call(window_kernel, out_shape=[jax.ShapeDtypeStruct((ROWS, BAND...  17.6 us
    all_to_all x1, starting transfers between devices, shards(): sums = lax.all_to_all(sums, 'genome', 0, 0, axis_index_groups=lines)  16.5 us
    all_to_all x1, blocking collectives, shards(): sums = lax.all_to_all(sums, 'genome', 0, 0, axis_index_groups=planes)  16.1 us
    all_gather x8, blocking collectives, both_cores(): return lax.all_gather(value, 'genome', axis_index_groups=chips)  14.7 us
    unnamed x24, local copies, waits for them, and re-layouts  8.56 us
    pallas_call x1, Pallas kernels, tails(): pl.pallas_call(tail_kernel, grid=(ROWS // count,), out_shape=[jax.ShapeDt...  3.59 us
  transfers between devices with their start and end apart: 8, of which 5 were waited for; matrix products, arithmetic and copies ran while one was open for 0% of the time, Pallas kernels for 14%

profile of v2, /device:TPU:32, one launch (start us, length us, event | category | flops | bytes accessed | tf_op | source)
XLA Modules:
  0.0 122.2 jit_solution(17606198293934431580)
XLA Ops:
  3.0 1.8 %all-gather = f32[32,128]{1,0:T(8,128)S(1)} all-gather(f32[16,128]{1,0:T(8,128)S(1)} %get-tuple-element.16), channel_id=2, replica_groups={{0,1},{2,3},{4,5},{6,7},{8,9},{10,11},{12,13},{14,15},{16,17},{18,19},{..., dimensions={0}, use_global_device_ids=true | all-gather | bytes 24576 | tf_op jit(solution)/shard_map/all_gather | solution.py:391
  4.8 5.1 %collective-permute-start.1 = (f32[2,16,128]{2,1,0:T(8,128)S(1)}, f32[2,16,128]{2,1,0:T(8,128)S(1)}, u32[]{:S(2)}, u32[]{:S(2)}) collective-permute-start(f32[2,16,128]{2,1,0:T(8,128)S(1)} %bitcast.20), channel_id=1, source_target_pairs={{0,4},{2,6},{4,8},{5,1},{6,10},{7,3},{8,12},{9,5},{10,14},{11,7},{... | collective-permute-start | bytes 49160 | tf_op jit(solution)/shard_map/ppermute | solution.py:395
  9.9 2.6 %collective-permute-start = (f32[2,16,128]{2,1,0:T(8,128)S(1)}, f32[2,16,128]{2,1,0:T(8,128)S(1)}, u32[]{:S(2)}, u32[]{:S(2)}) collective-permute-start(f32[2,16,128]{2,1,0:T(8,128)S(1)} %bitcast.21), channel_id=1, source_target_pairs={{0,2},{2,4},{3,1},{4,6},{5,3},{6,8},{7,5},{8,10},{9,7},{10,12},{11... | collective-permute-start | bytes 49160 | tf_op jit(solution)/shard_map/ppermute | solution.py:395
  12.5 2.4 %collective-permute-done.1 = f32[2,16,128]{2,1,0:T(8,128)S(1)} collective-permute-done((f32[2,16,128]{2,1,0:T(8,128)S(1)}, f32[2,16,128]{2,1,0:T(8,128)S(1)}, u32[]{:S(2)}, u32[]{:S(2)}) %collective-permute-start.1) | collective-permute-done | bytes 16416 | tf_op jit(solution)/shard_map/ppermute | solution.py:395
  15.0 1.8 %all-gather.2 = f32[4,16,128]{2,1,0:T(8,128)S(1)} all-gather(f32[2,16,128]{2,1,0:T(8,128)S(1)} %collective-permute-done.1), channel_id=4, replica_groups={{0,1},{2,3},{4,5},{6,7},{8,9},{10,11},{12,13},{14,15},{16,17},{18,19},{..., dimensions={0}, use_global_device_ids=true | all-gather | bytes 49152 | tf_op jit(solution)/shard_map/all_gather | solution.py:391
  16.8 3.0 %collective-permute-done = f32[2,16,128]{2,1,0:T(8,128)S(1)} collective-permute-done((f32[2,16,128]{2,1,0:T(8,128)S(1)}, f32[2,16,128]{2,1,0:T(8,128)S(1)}, u32[]{:S(2)}, u32[]{:S(2)}) %collective-permute-start) | collective-permute-done | bytes 16416 | tf_op jit(solution)/shard_map/ppermute | solution.py:395
  19.8 1.8 %all-gather.1 = f32[4,16,128]{2,1,0:T(8,128)S(1)} all-gather(f32[2,16,128]{2,1,0:T(8,128)S(1)} %collective-permute-done), channel_id=3, replica_groups={{0,1},{2,3},{4,5},{6,7},{8,9},{10,11},{12,13},{14,15},{16,17},{18,19},{..., dimensions={0}, use_global_device_ids=true | all-gather | bytes 49152 | tf_op jit(solution)/shard_map/all_gather | solution.py:391
  22.6 1.8 %all-gather.3 = f32[32,128]{1,0:T(8,128)S(1)} all-gather(f32[16,128]{1,0:T(8,128)S(1)} %shard_map.50), channel_id=5, replica_groups={{0,1},{2,3},{4,5},{6,7},{8,9},{10,11},{12,13},{14,15},{16,17},{18,19},{..., dimensions={0}, use_global_device_ids=true | all-gather | bytes 24576 | tf_op jit(solution)/shard_map/all_gather | solution.py:391
  24.4 1.9 %collective-permute-start.3 = (f32[2,16,128]{2,1,0:T(8,128)S(1)}, f32[2,16,128]{2,1,0:T(8,128)S(1)}, u32[]{:S(2)}, u32[]{:S(2)}) collective-permute-start(f32[2,16,128]{2,1,0:T(8,128)S(1)} %bitcast.23), channel_id=1, source_target_pairs={{0,4},{2,6},{4,8},{5,1},{6,10},{7,3},{8,12},{9,5},{10,14},{11,7},{... | collective-permute-start | bytes 49160 | tf_op jit(solution)/shard_map/ppermute | solution.py:395
  26.4 1.9 %collective-permute-start.2 = (f32[2,16,128]{2,1,0:T(8,128)S(1)}, f32[2,16,128]{2,1,0:T(8,128)S(1)}, u32[]{:S(2)}, u32[]{:S(2)}) collective-permute-start(f32[2,16,128]{2,1,0:T(8,128)S(1)} %bitcast.24), channel_id=1, source_target_pairs={{0,2},{2,4},{3,1},{4,6},{5,3},{6,8},{7,5},{8,10},{9,7},{10,12},{11... | collective-permute-start | bytes 49160 | tf_op jit(solution)/shard_map/ppermute | solution.py:395
  28.3 6.3 %collective-permute-done.3 = f32[2,16,128]{2,1,0:T(8,128)S(1)} collective-permute-done((f32[2,16,128]{2,1,0:T(8,128)S(1)}, f32[2,16,128]{2,1,0:T(8,128)S(1)}, u32[]{:S(2)}, u32[]{:S(2)}) %collective-permute-start.3) | collective-permute-done | bytes 16416 | tf_op jit(solution)/shard_map/ppermute | solution.py:395
  34.6 1.8 %all-gather.5 = f32[4,16,128]{2,1,0:T(8,128)S(1)} all-gather(f32[2,16,128]{2,1,0:T(8,128)S(1)} %collective-permute-done.3), channel_id=7, replica_groups={{0,1},{2,3},{4,5},{6,7},{8,9},{10,11},{12,13},{14,15},{16,17},{18,19},{..., dimensions={0}, use_global_device_ids=true | all-gather | bytes 49152 | tf_op jit(solution)/shard_map/all_gather | solution.py:391
  36.4 1.8 %all-gather.4 = f32[4,16,128]{2,1,0:T(8,128)S(1)} all-gather(f32[2,16,128]{2,1,0:T(8,128)S(1)} %collective-permute-done.2), channel_id=6, replica_groups={{0,1},{2,3},{4,5},{6,7},{8,9},{10,11},{12,13},{14,15},{16,17},{18,19},{..., dimensions={0}, use_global_device_ids=true | all-gather | bytes 49152 | tf_op jit(solution)/shard_map/all_gather | solution.py:391
  40.3 2.6 %collective-permute-start.4 = (f32[2,8,128]{2,1,0:T(8,128)S(1)}, f32[2,8,128]{2,1,0:T(8,128)S(1)}, u32[]{:S(2)}, u32[]{:S(2)}) collective-permute-start(f32[2,8,128]{2,1,0:T(8,128)S(1)} %bitcast.17), channel_id=1, source_target_pairs={{2,0},{4,2},{5,1},{6,4},{7,3},{8,6},{9,5},{10,8},{11,7},{12,10},{1... | collective-permute-start | bytes 24584 | tf_op jit(solution)/shard_map/ppermute | solution.py:395
  42.8 3.0 %collective-permute-done.4 = f32[2,8,128]{2,1,0:T(8,128)S(1)} collective-permute-done((f32[2,8,128]{2,1,0:T(8,128)S(1)}, f32[2,8,128]{2,1,0:T(8,128)S(1)}, u32[]{:S(2)}, u32[]{:S(2)}) %collective-permute-start.4) | collective-permute-done | bytes 8224 | tf_op jit(solution)/shard_map/ppermute | solution.py:395
  45.8 2.0 %all-gather.7 = f32[4,8,128]{2,1,0:T(8,128)S(1)} all-gather(f32[2,8,128]{2,1,0:T(8,128)S(1)} %collective-permute-done.4), channel_id=9, replica_groups={{0,1},{2,3},{4,5},{6,7},{8,9},{10,11},{12,13},{14,15},{16,17},{18,19},{..., dimensions={0}, use_global_device_ids=true | all-gather | bytes 24576 | tf_op jit(solution)/shard_map/all_gather | solution.py:391
  47.8 2.0 %shard_map.52 = (f32[256,1280]{1,0:T(8,128)S(1)}, f32[8,1280]{1,0:T(8,128)S(1)}, f32[8,1280]{1,0:T(8,128)S(1)}, f32[32,1,2176]{2,1,0:T(1,128)S(1)}) custom-call(s32[1]{0:T(128)} %bitcast.core_ref, f32[256,1280]{1,0:T(8,128)S(1)} %get-tuple-element.15.skewed_ref, f32[2,8,128]{2,1,0:T(8,128)S(1)} %bitcast.18, f32[2,2,8,128]{3,2,1,0:T(8,128)S(1)} %bitcast.11, ...), custom_call_target="tpu_custom_call" | custom-call | tf_op jit(solution)/shard_map/pallas_call | solution.py:324
  50.9 16.1 %all_to_all.10 = f32[32,1,2176]{2,1,0:T(1,128)S(1)} all-to-all(f32[32,1,2176]{2,1,0:T(1,128)S(1)} %get-tuple-element.17), channel_id=1, replica_groups={{0,1,2,3,4,5,6,7,8,9,10,11,12,13,14,15,16,17,18,19,20,21,22,23,24,25,26..., dimensions={0} | all-to-all | bytes 557056 | tf_op jit(solution)/shard_map/all_to_all | solution.py:414
  68.0 16.5 %all-to-all-start.1 = ((f32[16,1,2176]{2,1,0:T(1,128)}), f32[16,1,2176]{2,1,0:T(1,128)S(1)}, u32[]{:S(2)}, u32[]{:S(2)}) async-start(f32[16,1,2176]{2,1,0:T(1,128)} %broadcast_in_dim.2), calls=%async_computation.1 | async-start | bytes 278528 | tf_op jit(solution)/shard_map/all_to_all | solution.py:416
  84.4 1.9 %collective-permute-start.5 = (f32[8,1280]{1,0:T(8,128)S(1)}, f32[8,1280]{1,0:T(8,128)S(1)}, u32[]{:S(2)}, u32[]{:S(2)}) collective-permute-start(f32[8,1280]{1,0:T(8,128)S(1)} %get-tuple-element.19), channel_id=1, source_target_pairs={{0,1},{1,0},{2,3},{3,2},{4,5},{5,4},{6,7},{7,6},{8,9},{9,8},{10,11... | collective-permute-start | bytes 122888 | tf_op jit(solution)/shard_map/ppermute | solution.py:395
  86.3 3.4 %collective-permute-start.6 = (f32[8,1280]{1,0:T(8,128)S(1)}, f32[8,1280]{1,0:T(8,128)S(1)}, u32[]{:S(2)}, u32[]{:S(2)}) collective-permute-start(f32[8,1280]{1,0:T(8,128)S(1)} %get-tuple-element.20), channel_id=1, source_target_pairs={{1,2},{2,1},{3,4},{4,3},{5,6},{6,5},{7,8},{8,7},{9,10},{10,9},{11,... | collective-permute-start | bytes 122888 | tf_op jit(solution)/shard_map/ppermute | solution.py:395
  89.8 6.3 %collective-permute-done.6.cross_ref = f32[8,1280]{1,0:T(8,128)S(1)} collective-permute-done((f32[8,1280]{1,0:T(8,128)S(1)}, f32[8,1280]{1,0:T(8,128)S(1)}, u32[]{:S(2)}, u32[]{:S(2)}) %collective-permute-start.6) | collective-permute-done | bytes 40992 | tf_op jit(solution)/shard_map/ppermute | solution.py:395
  98.1 17.6 %shard_map.53 = (f32[256,1024]{1,0:T(8,128)S(1)}, f32[256,1024]{1,0:T(8,128)S(1)}, f32[256,1024]{1,0:T(8,128)S(1)}) custom-call(s32[1]{0:T(128)} %bitcast.core_ref, f32[256,1280]{1,0:T(8,128)S(1)} %copy-done.3, f32[8,1280]{1,0:T(8,128)S(1)} %collective-permute-done.5.swap_ref, f32[8,1280]{1,0:T(8,128)S(1)} %collective-permute-done.6.cross_ref, ...), custom_call_target="tpu_custom_call" | custom-call | flops 20000000 | bytes 6291456 | tf_op jit(solution)/shard_map/pallas_call | solution.py:359
  118.6 3.6 %shard_map.54 = (f32[256,1024]{1,0:T(8,128)}, f32[256,1024]{1,0:T(8,128)}, f32[2,128]{1,0:T(2,128)}) custom-call(f32[16,1,2176]{2,1,0:T(1,128)S(1)} %all-to-all-done.1.sums_ref, f32[8,128]{1,0:T(8,128)S(1)} %copy-done.9, f32[256,1024]{1,0:T(8,128)S(1)} %get-tuple-element.21.donut_ref, f32[256,1024]{1,0:T(8,128)S(1)} %get-tuple-element.22.lower_ref, ...), custom_call_target="tpu_custom_call" | custom-call | tf_op jit(solution)/shard_map/pallas_call | solution.py:372
  (33 shorter events, 12.3 us)
Async XLA Ops:
  0.6 1.2 %copy-start = (s32[256,1024]{1,0:T(8,128)S(1)}, s32[256,1024]{1,0:T(8,128)}, u32[]{:S(2)}) copy-start(s32[256,1024]{1,0:T(8,128)} %contacts_ref.3) | copy-start | bytes 3145732
  1.9 0.7 copy-start.10
  4.8 10.1 %collective-permute-start.1 = (f32[2,16,128]{2,1,0:T(8,128)S(1)}, f32[2,16,128]{2,1,0:T(8,128)S(1)}, u32[]{:S(2)}, u32[]{:S(2)}) collective-permute-start(f32[2,16,128]{2,1,0:T(8,128)S(1)} %bitcast.20), channel_id=1, source_target_pairs={{0,4},{2,6},{4,8},{5,1},{6,10},{7,3},{8,12},{9,5},{10,14},{11,7},{... | collective-permute-start | bytes 49160 | tf_op jit(solution)/shard_map/ppermute | solution.py:395
  9.9 9.9 %collective-permute-start = (f32[2,16,128]{2,1,0:T(8,128)S(1)}, f32[2,16,128]{2,1,0:T(8,128)S(1)}, u32[]{:S(2)}, u32[]{:S(2)}) collective-permute-start(f32[2,16,128]{2,1,0:T(8,128)S(1)} %bitcast.21), channel_id=1, source_target_pairs={{0,2},{2,4},{3,1},{4,6},{5,3},{6,8},{7,5},{8,10},{9,7},{10,12},{11... | collective-permute-start | bytes 49160 | tf_op jit(solution)/shard_map/ppermute | solution.py:395
  21.6 0.7 copy-start.11
  24.4 10.1 %collective-permute-start.3 = (f32[2,16,128]{2,1,0:T(8,128)S(1)}, f32[2,16,128]{2,1,0:T(8,128)S(1)}, u32[]{:S(2)}, u32[]{:S(2)}) collective-permute-start(f32[2,16,128]{2,1,0:T(8,128)S(1)} %bitcast.23), channel_id=1, source_target_pairs={{0,4},{2,6},{4,8},{5,1},{6,10},{7,3},{8,12},{9,5},{10,14},{11,7},{... | collective-permute-start | bytes 49160 | tf_op jit(solution)/shard_map/ppermute | solution.py:395
  26.4 10.0 %collective-permute-start.2 = (f32[2,16,128]{2,1,0:T(8,128)S(1)}, f32[2,16,128]{2,1,0:T(8,128)S(1)}, u32[]{:S(2)}, u32[]{:S(2)}) collective-permute-start(f32[2,16,128]{2,1,0:T(8,128)S(1)} %bitcast.24), channel_id=1, source_target_pairs={{0,2},{2,4},{3,1},{4,6},{5,3},{6,8},{7,5},{8,10},{9,7},{10,12},{11... | collective-permute-start | bytes 49160 | tf_op jit(solution)/shard_map/ppermute | solution.py:395
  38.5 12.5 %copy-start.8 = (f32[8,128]{1,0:T(8,128)}, f32[8,128]{1,0:T(8,128)S(1)}, u32[]{:S(2)}) copy-start(f32[8,128]{1,0:T(8,128)S(1)} %shard_map.51.own_ref) | copy-start | bytes 12292
  40.3 5.5 %collective-permute-start.4 = (f32[2,8,128]{2,1,0:T(8,128)S(1)}, f32[2,8,128]{2,1,0:T(8,128)S(1)}, u32[]{:S(2)}, u32[]{:S(2)}) collective-permute-start(f32[2,8,128]{2,1,0:T(8,128)S(1)} %bitcast.17), channel_id=1, source_target_pairs={{2,0},{4,2},{5,1},{6,4},{7,3},{8,6},{9,5},{10,8},{11,7},{12,10},{1... | collective-permute-start | bytes 24584 | tf_op jit(solution)/shard_map/ppermute | solution.py:395
  47.8 2.0 %copy-start.6 = (f32[4,8,128]{2,1,0:T(8,128)}, f32[4,8,128]{2,1,0:T(8,128)S(1)}, u32[]{:S(2)}) copy-start(f32[4,8,128]{2,1,0:T(8,128)S(1)} %all-gather.7) | copy-start | bytes 49156
  47.8 48.2 %copy-start.1 = (s32[256,1024]{1,0:T(8,128)S(1)}, s32[256,1024]{1,0:T(8,128)}, u32[]{:S(2)}) copy-start(s32[256,1024]{1,0:T(8,128)} %contacts_ref.3) | copy-start | bytes 3145732
  49.9 1.1 copy-start.2
  68.0 48.7 %all-to-all-start.1 = ((f32[16,1,2176]{2,1,0:T(1,128)}), f32[16,1,2176]{2,1,0:T(1,128)S(1)}, u32[]{:S(2)}, u32[]{:S(2)}) async-start(f32[16,1,2176]{2,1,0:T(1,128)} %broadcast_in_dim.2), calls=%async_computation.1 | async-start | bytes 278528 | tf_op jit(solution)/shard_map/all_to_all | solution.py:416
  84.4 5.3 %collective-permute-start.5 = (f32[8,1280]{1,0:T(8,128)S(1)}, f32[8,1280]{1,0:T(8,128)S(1)}, u32[]{:S(2)}, u32[]{:S(2)}) collective-permute-start(f32[8,1280]{1,0:T(8,128)S(1)} %get-tuple-element.19), channel_id=1, source_target_pairs={{0,1},{1,0},{2,3},{3,2},{4,5},{5,4},{6,7},{7,6},{8,9},{9,8},{10,11... | collective-permute-start | bytes 122888 | tf_op jit(solution)/shard_map/ppermute | solution.py:395
  86.3 9.7 %collective-permute-start.6 = (f32[8,1280]{1,0:T(8,128)S(1)}, f32[8,1280]{1,0:T(8,128)S(1)}, u32[]{:S(2)}, u32[]{:S(2)}) collective-permute-start(f32[8,1280]{1,0:T(8,128)S(1)} %get-tuple-element.20), channel_id=1, source_target_pairs={{1,2},{2,1},{3,4},{4,3},{5,6},{6,5},{7,8},{8,7},{9,10},{10,9},{11,... | collective-permute-start | bytes 122888 | tf_op jit(solution)/shard_map/ppermute | solution.py:395
  96.0 1.3 %copy-start.3 = (f32[256,1280]{1,0:T(8,128)S(1)}, f32[256,1280]{1,0:T(8,128)}, u32[]{:S(2)}) copy-start(f32[256,1280]{1,0:T(8,128)} %copy-done.2) | copy-start | bytes 3932164
  97.4 0.7 copy-start.7
  115.7 1.0 copy-start.4
  116.7 1.2 %copy-start.5 = (f32[256,1024]{1,0:T(8,128)S(1)}, f32[256,1024]{1,0:T(8,128)}, u32[]{:S(2)}) copy-start(f32[256,1024]{1,0:T(8,128)} %copy-done.4) | copy-start | bytes 3145732
  117.9 0.7 copy-start.9

commit v3 on v2

--- a/solution.py
+++ b/solution.py
@@ -20,7 +20,7 @@
 VMEM = pl.BlockSpec(memory_space=pltpu.VMEM)
 SMEM = pl.BlockSpec(memory_space=pltpu.SMEM)
 F32 = jnp.float32
-X_AT, SPREAD_AT, SUMS_AT, MESSAGE = 0, SLAB, SLAB * (HOPS + 2), 16
+X_AT, SPREAD_AT, SUMS_AT, MAPPED_AT, MESSAGE = 0, SLAB, SLAB * (HOPS + 2), SLAB * (HOPS + 3), 16
 
 
 def lanes(tiles):
@@ -49,13 +49,15 @@
     return total
 
 
+def spread_part(rows, weight_row, start):
+    part = rows * column_of(weight_row, start, STEP)
+    return fold(jnp.where(on_diagonal(start, STEP, SPAN), 0.0, part))
+
+
 def spread_of(skewed_ref, weight_row):
     total = jnp.zeros((8, SPAN), F32)
     for start in range(0, ROWS, STEP):
-        weight = column_of(weight_row, start, STEP)
-        part = skewed_ref[start : start + STEP, :] * weight
-        part = jnp.where(on_diagonal(start, STEP, SPAN), 0.0, part)
-        total = total + fold(part)
+        total = total + spread_part(skewed_ref[start : start + STEP, :], weight_row, start)
     return jnp.sum(total, axis=0, keepdims=True)
 
 
@@ -68,20 +70,20 @@
     return jnp.sum(total, axis=0, keepdims=True)
 
 
-def put_message(out_ref, x_row, spread_row, sums_row):
-    out_ref[...] = jnp.zeros((MESSAGE, LANE), F32)
+def put_message(out_ref, x_row, spread_row, sums_row, mapped_row):
     put_lanes(out_ref, X_AT, x_row)
     put_lanes(out_ref, SPREAD_AT, spread_row)
     put_lanes(out_ref, SUMS_AT, sums_row)
+    put_lanes(out_ref, MAPPED_AT, mapped_row)
 
 
 def begin_kernel(contacts_ref, mapped_ref, skewed_ref, out_ref):
-    mapped = lanes(mapped_ref[...]).astype(F32)
     for start in range(0, ROWS, STEP):
         counts = contacts_ref[start : start + STEP, :].astype(F32)
         padded = jnp.concatenate([counts, jnp.zeros((STEP, SPAN - BAND), F32)], axis=1)
         skewed_ref[start : start + STEP, :] = pltpu.roll(padded, start, 1, stride=1, stride_axis=0)
-    put_message(out_ref, mapped, spread_of(skewed_ref, mapped), jnp.zeros((1, ROWS), F32))
+    mapped = lanes(mapped_ref[...]).astype(F32)
+    put_message(out_ref, mapped, spread_of(skewed_ref, mapped), jnp.zeros((1, ROWS), F32), mapped)
 
 
 def ahead_of(core, slabs):
@@ -89,7 +91,7 @@
     return jnp.concatenate([lanes(t) for t in tiles], axis=1)
 
 
-def sum_rows(core_ref, skewed_ref, pair_ref, near_ref, far_ref, mapped_ref):
+def sum_rows(core_ref, skewed_ref, pair_ref, near_ref, far_ref):
     core = core_ref[0]
 
     def message(k):
@@ -109,27 +111,33 @@
         )
     sums = own_sums(skewed_ref, ahead_of(core, x_tiles)) + lanes(arrived)
     x_row = lanes(jnp.where(core == 0, x_tiles[0], x_tiles[1]))
-    mapped = lanes(mapped_ref[...]) > 0
-    return mapped, x_row * sums
-
-
-def middle_kernel(core_ref, skewed_ref, pair_ref, near_ref, far_ref, mapped_ref, out_ref):
-    mapped, sums = sum_rows(core_ref, skewed_ref, pair_ref, near_ref, far_ref, mapped_ref)
-    x_row = jnp.where(mapped, 1.0 / jnp.where(mapped, sums, 1.0), 0.0)
-    put_message(out_ref, x_row, spread_of(skewed_ref, x_row), sums)
-
-
-def last_kernel(core_ref, skewed_ref, pair_ref, near_ref, far_ref, mapped_ref, out_ref):
-    mapped, sums = sum_rows(core_ref, skewed_ref, pair_ref, near_ref, far_ref, mapped_ref)
+    mapped = jnp.where(core == 0, pair_ref[0, MAPPED_AT : MAPPED_AT + SLAB, :], pair_ref[1, MAPPED_AT : MAPPED_AT + SLAB, :])
+    return lanes(mapped), x_row * sums
+
+
+def middle_kernel(core_ref, skewed_ref, pair_ref, near_ref, far_ref, out_ref):
+    mapped, sums = sum_rows(core_ref, skewed_ref, pair_ref, near_ref, far_ref)
+    x_row = jnp.where(mapped > 0, 1.0 / jnp.where(mapped > 0, sums, 1.0), 0.0)
+    put_message(out_ref, x_row, spread_of(skewed_ref, x_row), sums, mapped)
+
+
+def last_kernel(core_ref, skewed_ref, pair_ref, near_ref, far_ref, out_ref):
+    mapped, sums = sum_rows(core_ref, skewed_ref, pair_ref, near_ref, far_ref)
     before = jnp.where(core_ref[0] == 0, pair_ref[0], pair_ref[1])
     before = lanes(before[SUMS_AT : SUMS_AT + SLAB])
-    bias = jnp.where(mapped, before * sums, 1.0)
+    bias = jnp.where(mapped > 0, before * sums, 1.0)
     out_ref[...] = jnp.zeros((8, LANE), F32)
-    put_lanes(out_ref, 0, jnp.where(mapped, 1.0 / bias, 0.0))
+    put_lanes(out_ref, 0, jnp.where(mapped > 0, 1.0 / bias, 0.0))
     put_lanes(out_ref, SLAB, bias)
     for at, value in ((4, before), (5, sums)):
-        total = jnp.sum(jnp.where(mapped, value, 0.0), axis=1, keepdims=True)
+        total = jnp.sum(jnp.where(mapped > 0, value, 0.0), axis=1, keepdims=True)
         out_ref[at : at + 1, :] = jnp.broadcast_to(total, (1, LANE))
+
+
+def flipped(rows):
+    order = 7 - lax.broadcasted_iota(jnp.int32, (8, LANE), 0)
+    tiles = [jnp.take_along_axis(rows[:, t : t + LANE], order, axis=0, mode="promise_in_bounds") for t in range(0, rows.shape[1], LANE)]
+    return jnp.concatenate(tiles, axis=1)
 
 
 def along_diagonals(rows_of, width):
@@ -143,13 +151,18 @@
         if g:
             part = pltpu.roll(part, SPAN - LANE - 8 * g, 1)
         total = part if total is None else total + part
-    out = total[0:1, :width]
-    for s in range(1, 8):
-        out = out + pltpu.roll(total, SPAN - LANE - s, 1)[s : s + 1, :width]
-    return out
-
-
-def band_kernel(core_ref, skewed_ref, pair_ref, ahead_ref, own_ref, final_ref, swap_ref, cross_ref, sums_ref):
+    total = pltpu.roll(flipped(total), SPAN - LANE - 7, 1, stride=1, stride_axis=0)
+    return jnp.sum(total[:, :width], axis=0, keepdims=True)
+
+
+def pairs_kernel(core_ref, pair_ref, near_ref, far_ref, out_ref):
+    refs = [pair_ref.at[0], pair_ref.at[1], near_ref.at[1, 0], near_ref.at[1, 1], far_ref.at[1, 0], far_ref.at[1, 1]]
+    ahead = ahead_of(core_ref[0], [r[MAPPED_AT : MAPPED_AT + SLAB, :] for r in refs])
+    row = ahead[:, :ROWS]
+    out_ref[...] = along_diagonals(lambda r: column_of(row, r, 8) * ahead, BAND)
+
+
+def band_kernel(core_ref, skewed_ref, pair_ref, ahead_ref, own_ref, pairs_ref, final_ref, swap_ref, cross_ref, sums_ref):
     core = core_ref[0]
     slabs = [pair_ref[0], pair_ref[1], ahead_ref[0, 0], ahead_ref[0, 1], ahead_ref[1, 0], ahead_ref[1, 1]]
     ahead = ahead_of(core, [s[X_AT : X_AT + SLAB] for s in slabs])
@@ -161,10 +174,8 @@
     first, last = final_ref[0:EDGE, :], final_ref[ROWS - EDGE : ROWS, :]
     swap_ref[...] = jnp.where(core == 0, last, first)
     cross_ref[...] = jnp.where(core == 0, first, last)
-    mapped_ahead = (ahead > 0).astype(F32)
-    mapped_row = mapped_ahead[:, :ROWS]
     diagonals = along_diagonals(lambda r: final_ref[r : r + 8, :], BAND)
-    pairs = along_diagonals(lambda r: column_of(mapped_row, r, 8) * mapped_ahead, BAND)
+    pairs = pairs_ref[...]
     own = own_ref[...]
     row = jnp.concatenate([diagonals, pairs, own[4:5, : LANE // 2], own[5:6, : LANE // 2]], axis=1)
     for n in range(sums_ref.shape[0]):
@@ -172,17 +183,17 @@
 
 
 def straight(rows, start):
-    if start:
-        rows = pltpu.roll(rows, SPAN - start, 1)
-    rows = rows[:, : BAND + LANE]
-    row = lax.broadcasted_iota(jnp.int32, rows.shape, 0)
-    for step in (1, 2, 4):
-        rows = jnp.where((row & step) > 0, pltpu.roll(rows, BAND + LANE - step, 1), rows)
-    return rows[:, :BAND]
+    rows = pltpu.roll(flipped(rows), SPAN - start - 7, 1, stride=1, stride_axis=0)
+    return flipped(rows[:, :BAND])
+
+
+def put_tiles(ref, start, value):
+    for t in range(WIDE // LANE):
+        ref[t, start : start + value.shape[0], :] = value[:, t * LANE : (t + 1) * LANE]
 
 
 def window_kernel(core_ref, final_ref, swap_ref, cross_ref, pair_ref, ahead_ref, contacts_ref,
-                  donut_ref, lower_ref, base_ref, edged_ref, lefts_ref, sides_ref, left_in_ref, sides_in_ref):
+                  donut_ref, lower_ref, base_ref, left_out_ref, left_ref, sides_out_ref, sides_ref):
     core = core_ref[0]
     slabs = [pair_ref[0], pair_ref[1], ahead_ref[0, 0], ahead_ref[0, 1], ahead_ref[1, 0], ahead_ref[1, 1]]
 
@@ -190,58 +201,53 @@
     before = jnp.where(core == 0, cross, swap)
     after = jnp.where(core == 0, swap, cross)
     gap = jnp.zeros((EDGE, LANE), F32)
-    edged_ref[0:EDGE, :] = jnp.concatenate(
-        [before[:, ROWS:], gap, before[:, :ROWS]], axis=1
-    )
-    edged_ref[ROWS + EDGE :, :] = jnp.concatenate(
-        [gap] * SLAB + [after[:, : WIDE - ROWS]], axis=1
-    )
-    edged_ref[EDGE : ROWS + EDGE, :SPAN] = final_ref[...]
-    edged_ref[EDGE : ROWS + EDGE, SPAN:] = jnp.zeros((ROWS, WIDE - SPAN), F32)
-    for start in range(0, ROWS + 2 * EDGE, 16):
-        cells = edged_ref[start : start + 16, :]
+    for start in range(0, ROWS + 2 * EDGE, EDGE):
+        if start == 0:
+            cells = jnp.concatenate([before[:, ROWS:], gap, before[:, :ROWS]], axis=1)
+        elif start == ROWS + EDGE:
+            cells = jnp.concatenate([gap] * SLAB + [after[:, : WIDE - ROWS]], axis=1)
+        else:
+            cells = jnp.concatenate([final_ref[start - EDGE : start, :], gap], axis=1)
         two = cells + pltpu.roll(cells, WIDE - 1, 1)
         three = two + pltpu.roll(cells, WIDE - 2, 1)
         left_out = pltpu.roll(three, 5, 1)
-        left_in = pltpu.roll(two, 2, 1)
-        lefts_ref[start : start + 16, :] = left_out
-        left_in_ref[start : start + 16, :] = left_in
-        sides_ref[start : start + 16, :] = left_out + pltpu.roll(three, WIDE - 3, 1)
-        sides_in_ref[start : start + 16, :] = left_in + pltpu.roll(two, WIDE - 1, 1)
+        left = left_out + pltpu.roll(two, 2, 1)
+        sides_out = left_out + pltpu.roll(three, WIDE - 3, 1)
+        put_tiles(left_out_ref, start, left_out)
+        put_tiles(left_ref, start, left)
+        put_tiles(sides_out_ref, start, sides_out)
+        put_tiles(sides_ref, start, sides_out + (left - left_out) + pltpu.roll(two, WIDE - 1, 1))
 
     ahead = ahead_of(core, [s[X_AT : X_AT + SLAB] for s in slabs])
     mapped = ahead > 0
     bias_ahead = jnp.where(mapped, 1.0 / jnp.where(mapped, ahead, 1.0), 0.0)
     bias_row = bias_ahead[:, :ROWS]
-    def band_rows(sums, start):
-        weight = column_of(bias_row, start, STEP) * bias_ahead
-        value = jnp.where(weight > 0, jnp.maximum(sums, 0.0) * weight, MASKED)
-        return jnp.concatenate([straight(value[r : r + 8], start + r) for r in range(0, STEP, 8)], axis=0)
-
-    for start in range(0, ROWS, STEP):
+    near, beyond = range(1, INNER + 1), range(INNER + 1, OUTER + 1)
+
+    for start in range(0, ROWS, 8):
 
         def rows(ref, shift):
             at = start + EDGE + shift
-            return ref[at : at + STEP, :SPAN]
-
-        shifts = range(1, OUTER + 1)
-        lower = sum(rows(lefts_ref, a) for a in shifts)
-        lower = lower + sum(rows(left_in_ref, a) for a in shifts if a > INNER)
-        donut = sum(rows(sides_ref, a) + rows(sides_ref, -a) for a in shifts)
-        donut = donut + sum(rows(sides_in_ref, a) + rows(sides_in_ref, -a) for a in shifts if a > INNER)
-        counts = contacts_ref[start : start + STEP, :]
+            return jnp.concatenate([ref[t, at : at + 8, :] for t in range(SPAN // LANE)], axis=1)
+
+        weight = column_of(bias_row, start, 8) * bias_ahead
+        lower = sum([rows(left_out_ref, a) for a in near] + [rows(left_ref, a) for a in beyond])
+        donut = sum([rows(sides_out_ref, s * a) for a in near for s in (1, -1)]
+                    + [rows(sides_ref, s * a) for a in beyond for s in (1, -1)])
+        counts = contacts_ref[start : start + 8, :]
         k = jnp.maximum(counts, 1).astype(F32)
         inverse_k = 1.0 / k
         scale = jnp.sqrt(k) * (3.0 / 2.0**0.5)
-        distance = lax.broadcasted_iota(jnp.int32, (STEP, BAND), 1)
+        distance = lax.broadcasted_iota(jnp.int32, (8, BAND), 1)
         keep = (counts > 0) & (distance >= 2 * OUTER)
-        base = (1.0 - inverse_k * (1.0 / 9.0)) * scale
+        base_ref[start : start + 8, :] = (1.0 - inverse_k * (1.0 / 9.0)) * scale
         for sums, out_ref in ((donut, donut_ref), (lower, lower_ref)):
-            value = band_rows(sums, start)
-            ok = keep & (value >= 0.0)
-            root = jnp.where(value > 0.0, jnp.exp(jnp.log(jnp.where(value > 0.0, value, 1.0) * inverse_k) * (1.0 / 3.0)), 0.0)
-            out_ref[start : start + STEP, :] = jnp.where(ok, root * scale, MASKED)
-        base_ref[start : start + STEP, :] = base
+            value = jnp.where(weight > 0, jnp.maximum(sums, 0.0) * weight, MASKED)
+            value = straight(value, start)
+            positive = value > 0.0
+            root = jnp.exp(jnp.log(jnp.where(positive, value, 1.0) * inverse_k) * (1.0 / 3.0))
+            root = jnp.where(positive, root * scale, 0.0)
+            out_ref[start : start + 8, :] = jnp.where(keep & (value >= 0.0), root, MASKED)
 
 
 def half_erfc(x):
@@ -312,7 +318,7 @@
             out_ref[start : start + STEP, :] = jnp.where(root < 0.0, 1.0, value)
 
 
-def params(mib=48):
+def params(mib=8):
     return pltpu.CompilerParams(vmem_limit_bytes=mib * 2**20)
 
 
@@ -320,13 +326,14 @@
     return pl.CostEstimate(flops=flops, bytes_accessed=moved, transcendentals=0)
 
 
-def call(kernel, ins, outs, specs=None):
+def call(kernel, ins, outs, specs=None, **more):
     return pl.pallas_call(
         kernel,
         out_shape=[jax.ShapeDtypeStruct(s, F32) for s in outs],
         in_specs=specs or [VMEM] * len(ins),
         out_specs=[VMEM] * len(outs),
         compiler_params=params(),
+        **more,
     )(*ins)
 
 
@@ -334,20 +341,26 @@
     return call(begin_kernel, (contacts, mapped), [(ROWS, SPAN), (MESSAGE, LANE)])
 
 
-def middle(core, skewed, pair, near, far, mapped):
-    return call(middle_kernel, (core, skewed, pair, near, far, mapped), [(MESSAGE, LANE)], [SMEM] + [VMEM] * 5)[0]
-
-
-def last(core, skewed, pair, near, far, mapped):
-    return call(last_kernel, (core, skewed, pair, near, far, mapped), [(8, LANE)], [SMEM] + [VMEM] * 5)[0]
-
-
-def final_band(core, skewed, pair, ahead, own, copies):
+def middle(core, skewed, pair, near, far):
+    return call(middle_kernel, (core, skewed, pair, near, far), [(MESSAGE, LANE)], [SMEM] + [VMEM] * 4)[0]
+
+
+def last(core, skewed, pair, near, far):
+    return call(last_kernel, (core, skewed, pair, near, far), [(8, LANE)], [SMEM] + [VMEM] * 4)[0]
+
+
+def pair_counts(core, pair, near, far):
+    return call(
+        pairs_kernel, (core, pair, near, far), [(1, BAND)], [SMEM] + [VMEM] * 3, cost_estimate=cost(10**6, 2**16)
+    )[0]
+
+
+def final_band(core, skewed, pair, ahead, own, pairs, copies):
     return call(
         band_kernel,
-        (core, skewed, pair, ahead, own),
+        (core, skewed, pair, ahead, own, pairs),
         [(ROWS, SPAN), (EDGE, SPAN), (EDGE, SPAN), (copies, 1, 2 * BAND + LANE)],
-        [SMEM] + [VMEM] * 4,
+        [SMEM] + [VMEM] * 5,
     )
 
 
@@ -361,8 +374,8 @@
         out_shape=[jax.ShapeDtypeStruct((ROWS, BAND), F32)] * 3,
         in_specs=[SMEM] + [VMEM] * 6,
         out_specs=[VMEM] * 3,
-        scratch_shapes=[pltpu.VMEM((ROWS + 2 * EDGE, WIDE), F32)] * 5,
-        compiler_params=params(),
+        scratch_shapes=[pltpu.VMEM((WIDE // LANE, ROWS + 2 * EDGE, LANE), F32)] * 4,
+        compiler_params=params(16),
         cost_estimate=cost(2 * 10**7, 6 * 2**20),
     )(core, final, swap, cross, pair, ahead, contacts)
 
@@ -404,14 +417,17 @@
         core = lax.rem(lax.axis_index("genome"), 2).astype(jnp.int32).reshape(1)
         mapped = mappable.reshape(SLAB, LANE)
         skewed, message = begin(contacts, mapped)
-        message = middle(core, skewed, *around(message), mapped)
-        own = last(core, skewed, *around(message), mapped)
+        exchanged = around(message)
+        pairs = pair_counts(core, *exchanged)
+        message = middle(core, skewed, *exchanged)
+        own = last(core, skewed, *around(message))
         pair = both_cores(own)
         ahead = both_cores(moved(pair, lambda i: i - 2 if i % 2 == 0 else i - 4))
-        final, swap, cross, sums = final_band(core, skewed, pair, ahead, own, plane)
+        final, swap, cross, sums = final_band(core, skewed, pair, ahead, own, pairs, plane)
         swap = moved(swap, lambda i: i ^ 1)
         cross = moved(cross, lambda i: i - 1 if i % 2 == 0 else i + 1)
         sums = lax.all_to_all(sums, "genome", 0, 0, axis_index_groups=planes)
+        sums, swap, cross = lax.optimization_barrier((sums, swap, cross))
         sums = jnp.broadcast_to(jnp.sum(sums, axis=0, keepdims=True), (count // plane,) + sums.shape[1:])
         sums = lax.all_to_all(sums, "genome", 0, 0, axis_index_groups=lines)
         donut, lower, base = windows(core, final, swap, cross, pair, ahead, contacts)

time: 123 us -> 106 us (0.86)
  blocking collectives: 30.8 us -> 14.7 us
  starting transfers between devices: 35.9 us -> 47.5 us
  Pallas kernels: 24.3 us -> 15.3 us
  waiting for transfers between devices: 21 us -> 17.8 us
    all_to_all x1 -> x0, blocking collectives: 16.1 us -> none  [shards(): sums = lax.all_to_all(sums, 'genome', 0, 0, axis_index_groups=planes)]
    pallas_call x1, Pallas kernels: 17.6 us -> 8.34 us  [windows(): pl.pallas_call(window_kernel, out_shape=[jax.ShapeDtypeStruct((ROWS, BAND...]
    all_to_all x0 -> x1, starting transfers between devices: none -> 7.25 us  [shards(): sums = lax.all_to_all(sums, 'genome', 0, 0, axis_index_groups=planes)]
    ppermute x7, waiting for transfers between devices: 21 us -> 16.6 us  [moved(): lax.ppermute(value, 'genome', [(i, t) for i, t in pairs if 0 <= t < count])]
    ppermute x7, starting transfers between devices: 19.4 us -> 22.7 us  [moved(): lax.ppermute(value, 'genome', [(i, t) for i, t in pairs if 0 <= t < count])]
    unnamed x24 -> x22, local copies, waits for them, and re-layouts: 8.56 us -> 7.87 us
    pallas_call x4 -> x5, Pallas kernels: 3.07 us -> 3.36 us  [call(): pl.pallas_call(kernel, out_shape=[jax.ShapeDtypeStruct(s, F32) for s in o...]
  transfers between devices with their start and end apart: 8 -> 9, of which waited for: 5 -> 6; matrix products, arithmetic and copies ran while one was open for 0% -> 0% of each run, Pallas kernels for 14% -> 9%
where the time goes in v3:
time: 106 us; the launch traced here: 105 us
  starting transfers between devices  47.5 us (45%)
  waiting for transfers between devices  17.8 us (17%)
  Pallas kernels  15.3 us (14%)
  blocking collectives  14.7 us (14%)
  local copies, waits for them, and re-layouts  8.6 us (8%)
    ppermute x7, starting transfers between devices, moved(): lax.ppermute(value, 'genome', [(i, t) for i, t in pairs if 0 <= t < count])  22.7 us
    all_to_all x1, starting transfers between devices, shards(): sums = lax.all_to_all(sums, 'genome', 0, 0, axis_index_groups=lines)  17.5 us
    ppermute x7, waiting for transfers between devices, moved(): lax.ppermute(value, 'genome', [(i, t) for i, t in pairs if 0 <= t < count])  16.6 us
    all_gather x8, blocking collectives, both_cores(): return lax.all_gather(value, 'genome', axis_index_groups=chips)  14.7 us
    pallas_call x1, Pallas kernels, windows(): pl.pallas_call(window_kernel, out_shape=[jax.ShapeDtypeStruct((ROWS, BAND...  8.34 us
    unnamed x22, local copies, waits for them, and re-layouts  7.87 us
    all_to_all x1, starting transfers between devices, shards(): sums = lax.all_to_all(sums, 'genome', 0, 0, axis_index_groups=planes)  7.25 us
    pallas_call x1, Pallas kernels, tails(): pl.pallas_call(tail_kernel, grid=(ROWS // count,), out_shape=[jax.ShapeDt...  3.59 us
  transfers between devices with their start and end apart: 9, of which 6 were waited for; matrix products, arithmetic and copies ran while one was open for 0% of the time, Pallas kernels for 9%

profile of v3, /device:TPU:32, one launch (start us, length us, event | category | flops | bytes accessed | tf_op | source)
XLA Modules:
  0.0 104.9 jit_solution(10854667246600895017)
XLA Ops:
  3.0 1.8 %all-gather = f32[32,128]{1,0:T(8,128)S(1)} all-gather(f32[16,128]{1,0:T(8,128)S(1)} %get-tuple-element.19), channel_id=2, replica_groups={{0,1},{2,3},{4,5},{6,7},{8,9},{10,11},{12,13},{14,15},{16,17},{18,19},{..., dimensions={0}, use_global_device_ids=true | all-gather | bytes 24576 | tf_op jit(solution)/shard_map/all_gather | solution.py:404
  4.8 5.1 %collective-permute-start.1 = (f32[2,16,128]{2,1,0:T(8,128)S(1)}, f32[2,16,128]{2,1,0:T(8,128)S(1)}, u32[]{:S(2)}, u32[]{:S(2)}) collective-permute-start(f32[2,16,128]{2,1,0:T(8,128)S(1)} %bitcast.17), channel_id=1, source_target_pairs={{0,4},{2,6},{4,8},{5,1},{6,10},{7,3},{8,12},{9,5},{10,14},{11,7},{... | collective-permute-start | bytes 49160 | tf_op jit(solution)/shard_map/ppermute | solution.py:408
  9.9 2.6 %collective-permute-start = (f32[2,16,128]{2,1,0:T(8,128)S(1)}, f32[2,16,128]{2,1,0:T(8,128)S(1)}, u32[]{:S(2)}, u32[]{:S(2)}) collective-permute-start(f32[2,16,128]{2,1,0:T(8,128)S(1)} %bitcast.18), channel_id=1, source_target_pairs={{0,2},{2,4},{3,1},{4,6},{5,3},{6,8},{7,5},{8,10},{9,7},{10,12},{11... | collective-permute-start | bytes 49160 | tf_op jit(solution)/shard_map/ppermute | solution.py:408
  12.5 2.4 %collective-permute-done.1 = f32[2,16,128]{2,1,0:T(8,128)S(1)} collective-permute-done((f32[2,16,128]{2,1,0:T(8,128)S(1)}, f32[2,16,128]{2,1,0:T(8,128)S(1)}, u32[]{:S(2)}, u32[]{:S(2)}) %collective-permute-start.1) | collective-permute-done | bytes 16416 | tf_op jit(solution)/shard_map/ppermute | solution.py:408
  15.0 1.8 %all-gather.2 = f32[4,16,128]{2,1,0:T(8,128)S(1)} all-gather(f32[2,16,128]{2,1,0:T(8,128)S(1)} %collective-permute-done.1), channel_id=4, replica_groups={{0,1},{2,3},{4,5},{6,7},{8,9},{10,11},{12,13},{14,15},{16,17},{18,19},{..., dimensions={0}, use_global_device_ids=true | all-gather | bytes 49152 | tf_op jit(solution)/shard_map/all_gather | solution.py:404
  16.8 3.0 %collective-permute-done = f32[2,16,128]{2,1,0:T(8,128)S(1)} collective-permute-done((f32[2,16,128]{2,1,0:T(8,128)S(1)}, f32[2,16,128]{2,1,0:T(8,128)S(1)}, u32[]{:S(2)}, u32[]{:S(2)}) %collective-permute-start) | collective-permute-done | bytes 16416 | tf_op jit(solution)/shard_map/ppermute | solution.py:408
  19.8 1.8 %all-gather.1 = f32[4,16,128]{2,1,0:T(8,128)S(1)} all-gather(f32[2,16,128]{2,1,0:T(8,128)S(1)} %collective-permute-done), channel_id=3, replica_groups={{0,1},{2,3},{4,5},{6,7},{8,9},{10,11},{12,13},{14,15},{16,17},{18,19},{..., dimensions={0}, use_global_device_ids=true | all-gather | bytes 49152 | tf_op jit(solution)/shard_map/all_gather | solution.py:404
  21.9 1.8 %all-gather.3 = f32[32,128]{1,0:T(8,128)S(1)} all-gather(f32[16,128]{1,0:T(8,128)S(1)} %shard_map.50), channel_id=5, replica_groups={{0,1},{2,3},{4,5},{6,7},{8,9},{10,11},{12,13},{14,15},{16,17},{18,19},{..., dimensions={0}, use_global_device_ids=true | all-gather | bytes 24576 | tf_op jit(solution)/shard_map/all_gather | solution.py:404
  23.8 1.9 %collective-permute-start.3 = (f32[2,16,128]{2,1,0:T(8,128)S(1)}, f32[2,16,128]{2,1,0:T(8,128)S(1)}, u32[]{:S(2)}, u32[]{:S(2)}) collective-permute-start(f32[2,16,128]{2,1,0:T(8,128)S(1)} %bitcast.26), channel_id=1, source_target_pairs={{0,4},{2,6},{4,8},{5,1},{6,10},{7,3},{8,12},{9,5},{10,14},{11,7},{... | collective-permute-start | bytes 49160 | tf_op jit(solution)/shard_map/ppermute | solution.py:408
  25.7 1.9 %collective-permute-start.2 = (f32[2,16,128]{2,1,0:T(8,128)S(1)}, f32[2,16,128]{2,1,0:T(8,128)S(1)}, u32[]{:S(2)}, u32[]{:S(2)}) collective-permute-start(f32[2,16,128]{2,1,0:T(8,128)S(1)} %bitcast.27), channel_id=1, source_target_pairs={{0,2},{2,4},{3,1},{4,6},{5,3},{6,8},{7,5},{8,10},{9,7},{10,12},{11... | collective-permute-start | bytes 49160 | tf_op jit(solution)/shard_map/ppermute | solution.py:408
  27.6 6.3 %collective-permute-done.3 = f32[2,16,128]{2,1,0:T(8,128)S(1)} collective-permute-done((f32[2,16,128]{2,1,0:T(8,128)S(1)}, f32[2,16,128]{2,1,0:T(8,128)S(1)}, u32[]{:S(2)}, u32[]{:S(2)}) %collective-permute-start.3) | collective-permute-done | bytes 16416 | tf_op jit(solution)/shard_map/ppermute | solution.py:408
  33.9 1.8 %all-gather.5 = f32[4,16,128]{2,1,0:T(8,128)S(1)} all-gather(f32[2,16,128]{2,1,0:T(8,128)S(1)} %collective-permute-done.3), channel_id=7, replica_groups={{0,1},{2,3},{4,5},{6,7},{8,9},{10,11},{12,13},{14,15},{16,17},{18,19},{..., dimensions={0}, use_global_device_ids=true | all-gather | bytes 49152 | tf_op jit(solution)/shard_map/all_gather | solution.py:404
  35.7 1.8 %all-gather.4 = f32[4,16,128]{2,1,0:T(8,128)S(1)} all-gather(f32[2,16,128]{2,1,0:T(8,128)S(1)} %collective-permute-done.2), channel_id=6, replica_groups={{0,1},{2,3},{4,5},{6,7},{8,9},{10,11},{12,13},{14,15},{16,17},{18,19},{..., dimensions={0}, use_global_device_ids=true | all-gather | bytes 49152 | tf_op jit(solution)/shard_map/all_gather | solution.py:404
  37.8 1.8 %all-gather.6 = f32[16,128]{1,0:T(8,128)S(1)} all-gather(f32[8,128]{1,0:T(8,128)S(1)} %shard_map.51.own_ref), channel_id=8, replica_groups={{0,1},{2,3},{4,5},{6,7},{8,9},{10,11},{12,13},{14,15},{16,17},{18,19},{..., dimensions={0}, use_global_device_ids=true | all-gather | bytes 12288 | tf_op jit(solution)/shard_map/all_gather | solution.py:404
  39.6 2.6 %collective-permute-start.4 = (f32[2,8,128]{2,1,0:T(8,128)S(1)}, f32[2,8,128]{2,1,0:T(8,128)S(1)}, u32[]{:S(2)}, u32[]{:S(2)}) collective-permute-start(f32[2,8,128]{2,1,0:T(8,128)S(1)} %bitcast.23), channel_id=1, source_target_pairs={{2,0},{4,2},{5,1},{6,4},{7,3},{8,6},{9,5},{10,8},{11,7},{12,10},{1... | collective-permute-start | bytes 24584 | tf_op jit(solution)/shard_map/ppermute | solution.py:408
  43.3 1.8 %collective-permute-done.4 = f32[2,8,128]{2,1,0:T(8,128)S(1)} collective-permute-done((f32[2,8,128]{2,1,0:T(8,128)S(1)}, f32[2,8,128]{2,1,0:T(8,128)S(1)}, u32[]{:S(2)}, u32[]{:S(2)}) %collective-permute-start.4) | collective-permute-done | bytes 8224 | tf_op jit(solution)/shard_map/ppermute | solution.py:408
  45.1 2.0 %all-gather.7 = f32[4,8,128]{2,1,0:T(8,128)S(1)} all-gather(f32[2,8,128]{2,1,0:T(8,128)S(1)} %collective-permute-done.4), channel_id=9, replica_groups={{0,1},{2,3},{4,5},{6,7},{8,9},{10,11},{12,13},{14,15},{16,17},{18,19},{..., dimensions={0}, use_global_device_ids=true | all-gather | bytes 24576 | tf_op jit(solution)/shard_map/all_gather | solution.py:404
  49.4 7.2 %all-to-all-start = ((f32[32,1,2176]{2,1,0:T(1,128)}), f32[32,1,2176]{2,1,0:T(1,128)S(1)}, u32[]{:S(2)}, u32[]{:S(2)}) async-start(f32[32,1,2176]{2,1,0:T(1,128)} %get-tuple-element.20), calls=%async_computation | async-start | bytes 557056 | tf_op jit(solution)/shard_map/all_to_all | solution.py:429
  56.7 2.2 %collective-permute-start.5 = (f32[8,1280]{1,0:T(8,128)S(1)}, f32[8,1280]{1,0:T(8,128)S(1)}, u32[]{:S(2)}, u32[]{:S(2)}) collective-permute-start(f32[8,1280]{1,0:T(8,128)S(1)} %get-tuple-element.21), channel_id=1, source_target_pairs={{0,1},{1,0},{2,3},{3,2},{4,5},{5,4},{6,7},{7,6},{8,9},{9,8},{10,11... | collective-permute-start | bytes 122888 | tf_op jit(solution)/shard_map/ppermute | solution.py:408
  58.9 6.5 %collective-permute-start.6 = (f32[8,1280]{1,0:T(8,128)S(1)}, f32[8,1280]{1,0:T(8,128)S(1)}, u32[]{:S(2)}, u32[]{:S(2)}) collective-permute-start(f32[8,1280]{1,0:T(8,128)S(1)} %get-tuple-element.22), channel_id=1, source_target_pairs={{1,2},{2,1},{3,4},{4,3},{5,6},{6,5},{7,8},{8,7},{9,10},{10,9},{11,... | collective-permute-start | bytes 122888 | tf_op jit(solution)/shard_map/ppermute | solution.py:408
  65.4 3.0 %collective-permute-done.6.cross_ref = f32[8,1280]{1,0:T(8,128)S(1)} collective-permute-done((f32[8,1280]{1,0:T(8,128)S(1)}, f32[8,1280]{1,0:T(8,128)S(1)}, u32[]{:S(2)}, u32[]{:S(2)}) %collective-permute-start.6) | collective-permute-done | bytes 40992 | tf_op jit(solution)/shard_map/ppermute | solution.py:408
  69.3 17.5 %all-to-all-start.1 = ((f32[16,1,2176]{2,1,0:T(1,128)}), f32[16,1,2176]{2,1,0:T(1,128)S(1)}, u32[]{:S(2)}, u32[]{:S(2)}) async-start(f32[16,1,2176]{2,1,0:T(1,128)} %broadcast_in_dim.2), calls=%async_computation.1 | async-start | bytes 278528 | tf_op jit(solution)/shard_map/all_to_all | solution.py:432
  88.8 8.3 %shard_map.54 = (f32[256,1024]{1,0:T(8,128)S(1)}, f32[256,1024]{1,0:T(8,128)S(1)}, f32[256,1024]{1,0:T(8,128)S(1)}) custom-call(s32[1]{0:T(128)} %bitcast.core_ref, f32[256,1280]{1,0:T(8,128)S(1)} %copy-done.3, f32[8,1280]{1,0:T(8,128)S(1)} %collective-permute-done.5.swap_ref, f32[8,1280]{1,0:T(8,128)S(1)} %collective-permute-done.6.cross_ref, ...), custom_call_target="tpu_custom_call" | custom-call | flops 20000000 | bytes 6291456 | tf_op jit(solution)/shard_map/pallas_call | solution.py:372
  101.3 3.6 %shard_map.55 = (f32[256,1024]{1,0:T(8,128)}, f32[256,1024]{1,0:T(8,128)}, f32[2,128]{1,0:T(2,128)}) custom-call(f32[16,1,2176]{2,1,0:T(1,128)S(1)} %all-to-all-done.1.sums_ref, f32[8,128]{1,0:T(8,128)S(1)} %copy-done.9, f32[256,1024]{1,0:T(8,128)S(1)} %get-tuple-element.27.donut_ref, f32[256,1024]{1,0:T(8,128)S(1)} %get-tuple-element.28.lower_ref, ...), custom_call_target="tpu_custom_call" | custom-call | tf_op jit(solution)/shard_map/pallas_call | solution.py:385
  (33 shorter events, 13.4 us)
Async XLA Ops:
  0.6 1.2 %copy-start = (s32[256,1024]{1,0:T(8,128)S(1)}, s32[256,1024]{1,0:T(8,128)}, u32[]{:S(2)}) copy-start(s32[256,1024]{1,0:T(8,128)} %contacts_ref.3) | copy-start | bytes 3145732
  1.9 0.7 copy-start.10
  4.8 10.1 %collective-permute-start.1 = (f32[2,16,128]{2,1,0:T(8,128)S(1)}, f32[2,16,128]{2,1,0:T(8,128)S(1)}, u32[]{:S(2)}, u32[]{:S(2)}) collective-permute-start(f32[2,16,128]{2,1,0:T(8,128)S(1)} %bitcast.17), channel_id=1, source_target_pairs={{0,4},{2,6},{4,8},{5,1},{6,10},{7,3},{8,12},{9,5},{10,14},{11,7},{... | collective-permute-start | bytes 49160 | tf_op jit(solution)/shard_map/ppermute | solution.py:408
  9.9 9.9 %collective-permute-start = (f32[2,16,128]{2,1,0:T(8,128)S(1)}, f32[2,16,128]{2,1,0:T(8,128)S(1)}, u32[]{:S(2)}, u32[]{:S(2)}) collective-permute-start(f32[2,16,128]{2,1,0:T(8,128)S(1)} %bitcast.18), channel_id=1, source_target_pairs={{0,2},{2,4},{3,1},{4,6},{5,3},{6,8},{7,5},{8,10},{9,7},{10,12},{11... | collective-permute-start | bytes 49160 | tf_op jit(solution)/shard_map/ppermute | solution.py:408
  23.8 10.1 %collective-permute-start.3 = (f32[2,16,128]{2,1,0:T(8,128)S(1)}, f32[2,16,128]{2,1,0:T(8,128)S(1)}, u32[]{:S(2)}, u32[]{:S(2)}) collective-permute-start(f32[2,16,128]{2,1,0:T(8,128)S(1)} %bitcast.26), channel_id=1, source_target_pairs={{0,4},{2,6},{4,8},{5,1},{6,10},{7,3},{8,12},{9,5},{10,14},{11,7},{... | collective-permute-start | bytes 49160 | tf_op jit(solution)/shard_map/ppermute | solution.py:408
  25.7 10.0 %collective-permute-start.2 = (f32[2,16,128]{2,1,0:T(8,128)S(1)}, f32[2,16,128]{2,1,0:T(8,128)S(1)}, u32[]{:S(2)}, u32[]{:S(2)}) collective-permute-start(f32[2,16,128]{2,1,0:T(8,128)S(1)} %bitcast.27), channel_id=1, source_target_pairs={{0,2},{2,4},{3,1},{4,6},{5,3},{6,8},{7,5},{8,10},{9,7},{10,12},{11... | collective-permute-start | bytes 49160 | tf_op jit(solution)/shard_map/ppermute | solution.py:408
  37.8 31.5 %copy-start.8 = (f32[8,128]{1,0:T(8,128)}, f32[8,128]{1,0:T(8,128)S(1)}, u32[]{:S(2)}) copy-start(f32[8,128]{1,0:T(8,128)S(1)} %shard_map.51.own_ref) | copy-start | bytes 12292
  39.6 5.5 %collective-permute-start.4 = (f32[2,8,128]{2,1,0:T(8,128)S(1)}, f32[2,8,128]{2,1,0:T(8,128)S(1)}, u32[]{:S(2)}, u32[]{:S(2)}) collective-permute-start(f32[2,8,128]{2,1,0:T(8,128)S(1)} %bitcast.23), channel_id=1, source_target_pairs={{2,0},{4,2},{5,1},{6,4},{7,3},{8,6},{9,5},{10,8},{11,7},{12,10},{1... | collective-permute-start | bytes 24584 | tf_op jit(solution)/shard_map/ppermute | solution.py:408
  47.1 1.2 %copy-start.6 = (f32[4,8,128]{2,1,0:T(8,128)}, f32[4,8,128]{2,1,0:T(8,128)S(1)}, u32[]{:S(2)}) copy-start(f32[4,8,128]{2,1,0:T(8,128)S(1)} %all-gather.7) | copy-start | bytes 49156
  47.1 39.6 %copy-start.1 = (s32[256,1024]{1,0:T(8,128)S(1)}, s32[256,1024]{1,0:T(8,128)}, u32[]{:S(2)}) copy-start(s32[256,1024]{1,0:T(8,128)} %contacts_ref.3) | copy-start | bytes 3145732
  48.3 1.1 %copy-start.2 = (f32[256,1280]{1,0:T(8,128)}, f32[256,1280]{1,0:T(8,128)S(1)}, u32[]{:S(2)}) copy-start(f32[256,1280]{1,0:T(8,128)S(1)} %get-tuple-element.24.final_ref) | copy-start | bytes 3932164
  49.4 19.0 %all-to-all-start = ((f32[32,1,2176]{2,1,0:T(1,128)}), f32[32,1,2176]{2,1,0:T(1,128)S(1)}, u32[]{:S(2)}, u32[]{:S(2)}) async-start(f32[32,1,2176]{2,1,0:T(1,128)} %get-tuple-element.20), calls=%async_computation | async-start | bytes 557056 | tf_op jit(solution)/shard_map/all_to_all | solution.py:429
  56.7 8.7 %collective-permute-start.5 = (f32[8,1280]{1,0:T(8,128)S(1)}, f32[8,1280]{1,0:T(8,128)S(1)}, u32[]{:S(2)}, u32[]{:S(2)}) collective-permute-start(f32[8,1280]{1,0:T(8,128)S(1)} %get-tuple-element.21), channel_id=1, source_target_pairs={{0,1},{1,0},{2,3},{3,2},{4,5},{5,4},{6,7},{7,6},{8,9},{9,8},{10,11... | collective-permute-start | bytes 122888 | tf_op jit(solution)/shard_map/ppermute | solution.py:408
  58.9 9.5 %collective-permute-start.6 = (f32[8,1280]{1,0:T(8,128)S(1)}, f32[8,1280]{1,0:T(8,128)S(1)}, u32[]{:S(2)}, u32[]{:S(2)}) collective-permute-start(f32[8,1280]{1,0:T(8,128)S(1)} %get-tuple-element.22), channel_id=1, source_target_pairs={{1,2},{2,1},{3,4},{4,3},{5,6},{6,5},{7,8},{8,7},{9,10},{10,9},{11,... | collective-permute-start | bytes 122888 | tf_op jit(solution)/shard_map/ppermute | solution.py:408
  69.3 30.1 %all-to-all-start.1 = ((f32[16,1,2176]{2,1,0:T(1,128)}), f32[16,1,2176]{2,1,0:T(1,128)S(1)}, u32[]{:S(2)}, u32[]{:S(2)}) async-start(f32[16,1,2176]{2,1,0:T(1,128)} %broadcast_in_dim.2), calls=%async_computation.1 | async-start | bytes 278528 | tf_op jit(solution)/shard_map/all_to_all | solution.py:432
  86.8 1.3 %copy-start.3 = (f32[256,1280]{1,0:T(8,128)S(1)}, f32[256,1280]{1,0:T(8,128)}, u32[]{:S(2)}) copy-start(f32[256,1280]{1,0:T(8,128)} %copy-done.2) | copy-start | bytes 3932164
  88.1 0.7 copy-start.7
  97.2 1.0 copy-start.4
  99.4 1.2 %copy-start.5 = (f32[256,1024]{1,0:T(8,128)S(1)}, f32[256,1024]{1,0:T(8,128)}, u32[]{:S(2)}) copy-start(f32[256,1024]{1,0:T(8,128)} %copy-done.4) | copy-start | bytes 3145732
  100.6 0.7 copy-start.9

commit v4 on v3

--- a/solution.py
+++ b/solution.py
@@ -162,7 +162,8 @@
     out_ref[...] = along_diagonals(lambda r: column_of(row, r, 8) * ahead, BAND)
 
 
-def band_kernel(core_ref, skewed_ref, pair_ref, ahead_ref, own_ref, pairs_ref, final_ref, swap_ref, cross_ref, sums_ref):
+def band_kernel(core_ref, skewed_ref, pair_ref, ahead_ref, own_ref, pairs_ref,
+                swap_ref, cross_ref, sums_ref, vectors_ref, final_ref):
     core = core_ref[0]
     slabs = [pair_ref[0], pair_ref[1], ahead_ref[0, 0], ahead_ref[0, 1], ahead_ref[1, 0], ahead_ref[1, 1]]
     ahead = ahead_of(core, [s[X_AT : X_AT + SLAB] for s in slabs])
@@ -175,11 +176,13 @@
     swap_ref[...] = jnp.where(core == 0, last, first)
     cross_ref[...] = jnp.where(core == 0, first, last)
     diagonals = along_diagonals(lambda r: final_ref[r : r + 8, :], BAND)
-    pairs = pairs_ref[...]
     own = own_ref[...]
-    row = jnp.concatenate([diagonals, pairs, own[4:5, : LANE // 2], own[5:6, : LANE // 2]], axis=1)
+    row = jnp.concatenate([diagonals, pairs_ref[...], own[4:5, : LANE // 2], own[5:6, : LANE // 2]], axis=1)
     for n in range(sums_ref.shape[0]):
         sums_ref[n] = row
+    vectors_ref[0:1, :] = ahead
+    vectors_ref[1:2, :] = jnp.where(ahead > 0, 1.0 / jnp.where(ahead > 0, ahead, 1.0), 0.0)
+    vectors_ref[2:3, :] = jnp.concatenate([lanes(own[SLAB : 2 * SLAB]), jnp.zeros((1, SPAN - ROWS), F32)], axis=1)
 
 
 def straight(rows, start):
@@ -188,66 +191,112 @@
 
 
 def put_tiles(ref, start, value):
-    for t in range(WIDE // LANE):
+    for t in range(value.shape[1] // LANE):
         ref[t, start : start + value.shape[0], :] = value[:, t * LANE : (t + 1) * LANE]
 
 
-def window_kernel(core_ref, final_ref, swap_ref, cross_ref, pair_ref, ahead_ref, contacts_ref,
-                  donut_ref, lower_ref, base_ref, left_out_ref, left_ref, sides_out_ref, sides_ref):
+def put_tables(refs, start, cells):
+    left_out_ref, left_ref, sides_out_ref, sides_ref = refs
+    two = cells + pltpu.roll(cells, WIDE - 1, 1)
+    three = two + pltpu.roll(cells, WIDE - 2, 1)
+    left_out = pltpu.roll(three, 5, 1)
+    left_in = pltpu.roll(two, 2, 1)
+    sides_out = left_out + pltpu.roll(three, WIDE - 3, 1)
+    put_tiles(left_out_ref, start, left_out)
+    put_tiles(left_ref, start, left_out + left_in)
+    put_tiles(sides_out_ref, start, sides_out)
+    put_tiles(sides_ref, start, sides_out + left_in + pltpu.roll(two, WIDE - 1, 1))
+
+
+NEAR, BEYOND = range(1, INNER + 1), range(INNER + 1, OUTER + 1)
+
+
+def box_sums(out_ref, in_ref, at, signs):
+    def rows(ref, shift):
+        return jnp.concatenate([ref[t, at + shift : at + shift + 8, :] for t in range(SPAN // LANE)], axis=1)
+
+    return sum([rows(out_ref, s * a) for a in NEAR for s in signs] + [rows(in_ref, s * a) for a in BEYOND for s in signs])
+
+
+def scale_of(counts):
+    k = jnp.maximum(counts, 1).astype(F32)
+    return 1.0 / k, jnp.sqrt(k) * (3.0 / 2.0**0.5)
+
+
+def root_of(sums, weight, start, counts, inverse_k, scale):
+    value = jnp.where(weight > 0, jnp.maximum(sums, 0.0) * weight, MASKED)
+    value = straight(value, start)
+    positive = value > 0.0
+    root = jnp.exp(jnp.log(jnp.where(positive, value, 1.0) * inverse_k) * (1.0 / 3.0))
+    root = jnp.where(positive, root * scale, 0.0)
+    distance = lax.broadcasted_iota(jnp.int32, (8, BAND), 1)
+    return jnp.where((counts > 0) & (distance >= 2 * OUTER) & (value >= 0.0), root, MASKED)
+
+
+def window_kernel(contacts_ref, vectors_ref, donut_ref, lower_ref, base_hbm, partial_ref, counts_ref,
+                  left_out_ref, left_ref, sides_out_ref, sides_ref, base_ref, sems):
+    ahead, bias_ahead = vectors_ref[0:1, :], vectors_ref[1:2, :]
+    x_row, bias_row = ahead[:, :ROWS], bias_ahead[:, :ROWS]
+    tables = (left_out_ref, left_ref, sides_out_ref, sides_ref)
+    empty = jnp.zeros((EDGE, WIDE), F32)
+    for ref in tables:
+        put_tiles(ref, 0, empty)
+        put_tiles(ref, ROWS + EDGE, empty)
+    for start in range(0, ROWS, 8):
+        cells = contacts_ref[start : start + 8, :].astype(F32)
+        cells = jnp.concatenate([cells, jnp.zeros((8, SPAN - BAND), F32)], axis=1)
+        cells = pltpu.roll(cells, start, 1, stride=1, stride_axis=0) * column_of(x_row, start, 8) * ahead
+        put_tables(tables, start + EDGE, jnp.concatenate([cells, jnp.zeros((8, WIDE - SPAN), F32)], axis=1))
+    copies = []
+    for start in range(0, ROWS, 8):
+        weight = column_of(bias_row, start, 8) * bias_ahead
+        lower = box_sums(left_out_ref, left_ref, start + EDGE, (1,))
+        donut = box_sums(sides_out_ref, sides_ref, start + EDGE, (1, -1))
+        counts = contacts_ref[start : start + 8, :]
+        inverse_k, scale = scale_of(counts)
+        base_ref[start : start + 8, :] = (1.0 - inverse_k * (1.0 / 9.0)) * scale
+        donut_ref[start : start + 8, :] = root_of(donut, weight, start, counts, inverse_k, scale)
+        lower_ref[start : start + 8, :] = root_of(lower, weight, start, counts, inverse_k, scale)
+        if start == 0:
+            partial_ref[0:8, :] = donut
+            counts_ref[0:8, :] = counts
+        if start == ROWS - 8:
+            partial_ref[8:16, :] = donut
+            partial_ref[16:24, :] = lower
+            counts_ref[8:16, :] = counts
+        if (start + 8) % (ROWS // 4) == 0:
+            n = len(copies)
+            part = pl.ds(n * (ROWS // 4), ROWS // 4)
+            copies.append(pltpu.make_async_copy(base_ref.at[part, :], base_hbm.at[part, :], sems.at[n]))
+            copies[n].start()
+    for copy in copies:
+        copy.wait()
+
+
+def edge_kernel(core_ref, swap_ref, cross_ref, partial_ref, counts_ref, vectors_ref, out_ref,
+                left_out_ref, left_ref, sides_out_ref, sides_ref):
     core = core_ref[0]
-    slabs = [pair_ref[0], pair_ref[1], ahead_ref[0, 0], ahead_ref[0, 1], ahead_ref[1, 0], ahead_ref[1, 1]]
-
     swap, cross = swap_ref[...], cross_ref[...]
     before = jnp.where(core == 0, cross, swap)
     after = jnp.where(core == 0, swap, cross)
     gap = jnp.zeros((EDGE, LANE), F32)
-    for start in range(0, ROWS + 2 * EDGE, EDGE):
-        if start == 0:
-            cells = jnp.concatenate([before[:, ROWS:], gap, before[:, :ROWS]], axis=1)
-        elif start == ROWS + EDGE:
-            cells = jnp.concatenate([gap] * SLAB + [after[:, : WIDE - ROWS]], axis=1)
-        else:
-            cells = jnp.concatenate([final_ref[start - EDGE : start, :], gap], axis=1)
-        two = cells + pltpu.roll(cells, WIDE - 1, 1)
-        three = two + pltpu.roll(cells, WIDE - 2, 1)
-        left_out = pltpu.roll(three, 5, 1)
-        left = left_out + pltpu.roll(two, 2, 1)
-        sides_out = left_out + pltpu.roll(three, WIDE - 3, 1)
-        put_tiles(left_out_ref, start, left_out)
-        put_tiles(left_ref, start, left)
-        put_tiles(sides_out_ref, start, sides_out)
-        put_tiles(sides_ref, start, sides_out + (left - left_out) + pltpu.roll(two, WIDE - 1, 1))
-
-    ahead = ahead_of(core, [s[X_AT : X_AT + SLAB] for s in slabs])
-    mapped = ahead > 0
-    bias_ahead = jnp.where(mapped, 1.0 / jnp.where(mapped, ahead, 1.0), 0.0)
+    empty = jnp.zeros((EDGE, WIDE), F32)
+    tables = (left_out_ref, left_ref, sides_out_ref, sides_ref)
+    for ref in tables:
+        put_tiles(ref, EDGE, empty)
+    put_tables(tables, 0, jnp.concatenate([before[:, ROWS:], gap, before[:, :ROWS]], axis=1))
+    put_tables(tables, 2 * EDGE, jnp.concatenate([gap] * SLAB + [after[:, : WIDE - ROWS]], axis=1))
+    bias_ahead = vectors_ref[1:2, :]
     bias_row = bias_ahead[:, :ROWS]
-    near, beyond = range(1, INNER + 1), range(INNER + 1, OUTER + 1)
-
-    for start in range(0, ROWS, 8):
-
-        def rows(ref, shift):
-            at = start + EDGE + shift
-            return jnp.concatenate([ref[t, at : at + 8, :] for t in range(SPAN // LANE)], axis=1)
-
+    last = ROWS - 8
+    donut_first = partial_ref[0:8, :] + box_sums(sides_out_ref, sides_ref, EDGE, (-1,))
+    donut_last = partial_ref[8:16, :] + box_sums(sides_out_ref, sides_ref, EDGE, (1,))
+    lower_last = partial_ref[16:24, :] + box_sums(left_out_ref, left_ref, EDGE, (1,))
+    for at, sums, start, half in ((0, donut_first, 0, 0), (8, donut_last, last, 8), (16, lower_last, last, 8)):
+        counts = counts_ref[half : half + 8, :]
         weight = column_of(bias_row, start, 8) * bias_ahead
-        lower = sum([rows(left_out_ref, a) for a in near] + [rows(left_ref, a) for a in beyond])
-        donut = sum([rows(sides_out_ref, s * a) for a in near for s in (1, -1)]
-                    + [rows(sides_ref, s * a) for a in beyond for s in (1, -1)])
-        counts = contacts_ref[start : start + 8, :]
-        k = jnp.maximum(counts, 1).astype(F32)
-        inverse_k = 1.0 / k
-        scale = jnp.sqrt(k) * (3.0 / 2.0**0.5)
-        distance = lax.broadcasted_iota(jnp.int32, (8, BAND), 1)
-        keep = (counts > 0) & (distance >= 2 * OUTER)
-        base_ref[start : start + 8, :] = (1.0 - inverse_k * (1.0 / 9.0)) * scale
-        for sums, out_ref in ((donut, donut_ref), (lower, lower_ref)):
-            value = jnp.where(weight > 0, jnp.maximum(sums, 0.0) * weight, MASKED)
-            value = straight(value, start)
-            positive = value > 0.0
-            root = jnp.exp(jnp.log(jnp.where(positive, value, 1.0) * inverse_k) * (1.0 / 3.0))
-            root = jnp.where(positive, root * scale, 0.0)
-            out_ref[start : start + 8, :] = jnp.where(keep & (value >= 0.0), root, MASKED)
+        out_ref[at : at + 8, :] = root_of(sums, weight, start, counts, *scale_of(counts))
+    out_ref[24:25, :] = jnp.concatenate([vectors_ref[2:3, :ROWS], vectors_ref[0:1, : BAND - ROWS]], axis=1)
 
 
 def half_erfc(x):
@@ -261,8 +310,10 @@
 
 
 def filter_sums(expected):
-    margin = 2 * OUTER
-    padded = jnp.concatenate([expected, jnp.zeros((1, LANE), F32)], axis=1)
+    lane = lax.broadcasted_iota(jnp.int32, expected.shape, 1)
+    none = jnp.zeros((1, LANE), F32)
+    after = jnp.concatenate([expected[1:], none], axis=0)
+    before = jnp.concatenate([none, expected[:-1]], axis=0)
     donut_weight, lower_weight = {}, {}
     for a in range(-OUTER, OUTER + 1):
         for c in range(-OUTER, OUTER + 1):
@@ -271,9 +322,12 @@
             if a >= 1 and c <= -1 and not (a <= INNER and c >= -INNER):
                 lower_weight[c - a] = lower_weight.get(c - a, 0) + 1
     donut = lower = None
-    for k in range(-margin, margin + 1):
-        moved = pltpu.roll(padded, (-k) % (BAND + LANE), 1) if k else padded
-        moved = moved[:, :BAND]
+    for k in range(-2 * OUTER, 2 * OUTER + 1):
+        moved = expected
+        if k:
+            turn = (-k) % LANE
+            here = (lane + k < LANE) if k > 0 else (lane + k >= 0)
+            moved = jnp.where(here, pltpu.roll(expected, turn, 1), pltpu.roll(after if k > 0 else before, turn, 1))
         if k in donut_weight:
             part = moved * float(donut_weight[k])
             donut = part if donut is None else donut + part
@@ -289,31 +343,56 @@
     return jnp.where(positive, root, value)
 
 
-def tail_kernel(sums_ref, own_ref, donut_ref, lower_ref, base_ref, pvalue_donut_ref, pvalue_lower_ref, bias_ref, ratio_ref):
-    @pl.when(pl.program_id(0) == 0)
+def tiled(row):
+    return jnp.concatenate([row[:, t : t + LANE] for t in range(0, row.shape[1], LANE)], axis=0)
+
+
+def tail_kernel(sums_ref, edge_ref, donut_ref, lower_ref, base_hbm, pvalue_donut_ref, pvalue_lower_ref, bias_ref,
+                ratio_ref, base_ref, sems):
+    step = pl.program_id(0)
+    count = donut_ref.shape[0]
+
+    def copy_of(n):
+        part = pl.ds(n * count, count)
+        return pltpu.make_async_copy(base_hbm.at[part, :], base_ref.at[part, :], sems.at[n])
+
+    @pl.when(step == 0)
     def _():
+        for n in range(ROWS // count):
+            copy_of(n).start()
         total = sums_ref[0]
         for n in range(1, sums_ref.shape[0]):
             total = total + sums_ref[n]
-        diagonals, pairs = total[:, :BAND], total[:, BAND : 2 * BAND]
-        expected = diagonals / pairs
+        pairs = tiled(total[:, BAND : 2 * BAND])
+        expected = tiled(total[:, :BAND]) / pairs
         donut_exp, lower_exp = filter_sums(expected)
-        ratio_ref[0:1, :] = cube_root(expected / donut_exp)
-        ratio_ref[1:2, :] = cube_root(expected / lower_exp)
-        mapped_count = pairs[:, 0:1]
+        ratio_ref[0:1, :] = lanes(cube_root(expected / donut_exp))
+        ratio_ref[1:2, :] = lanes(cube_root(expected / lower_exp))
+        mapped_count = pairs[0:1, 0:1]
         half = LANE // 2
         first = total[:, 2 * BAND : 2 * BAND + 1] / mapped_count
         second = total[:, 2 * BAND + half : 2 * BAND + half + 1] / mapped_count
-        own = own_ref[...]
-        bias = own[SLAB : 2 * SLAB]
-        mapped = own[0:SLAB] > 0
-        bias_ref[...] = jnp.where(mapped, bias / first / second, 1.0)
-
-    count = base_ref.shape[0]
+        own = edge_ref[24:25, :]
+        bias = jnp.where(own[:, ROWS : 2 * ROWS] > 0, own[:, :ROWS] / first / second, 1.0)
+        put_lanes(bias_ref, 0, bias)
+
+    for n in range(ROWS // count):
+
+        @pl.when(step == n)
+        def _():
+            copy_of(n).wait()
+
     for start in range(0, count, STEP):
-        base = base_ref[start : start + STEP, :]
+        base = base_ref[pl.ds(pl.multiple_of(step * count + start, STEP), STEP), :]
         for at, root_ref, out_ref in ((0, donut_ref, pvalue_donut_ref), (1, lower_ref, pvalue_lower_ref)):
             root = root_ref[start : start + STEP, :]
+            if start == 0 and at == 0:
+                top = jnp.where(step == 0, edge_ref[0:8, :], root[0:8])
+                root = jnp.concatenate([top, root[8:]], axis=0)
+            if start == count - STEP:
+                edge = edge_ref[8:16, :] if at == 0 else edge_ref[16:24, :]
+                bottom = jnp.where(step == ROWS // count - 1, edge, root[STEP - 8 :])
+                root = jnp.concatenate([root[: STEP - 8], bottom], axis=0)
             value = half_erfc(base - root * ratio_ref[at : at + 1, :])
             out_ref[start : start + STEP, :] = jnp.where(root < 0.0, 1.0, value)
 
@@ -359,8 +438,9 @@
     return call(
         band_kernel,
         (core, skewed, pair, ahead, own, pairs),
-        [(ROWS, SPAN), (EDGE, SPAN), (EDGE, SPAN), (copies, 1, 2 * BAND + LANE)],
+        [(EDGE, SPAN), (EDGE, SPAN), (copies, 1, 2 * BAND + LANE), (8, SPAN)],
         [SMEM] + [VMEM] * 5,
+        scratch_shapes=[pltpu.VMEM((ROWS, SPAN), F32)],
     )
 
 
@@ -368,29 +448,46 @@
     return pl.BlockSpec(shape, lambda i: (0,) * len(shape))
 
 
-def windows(core, final, swap, cross, pair, ahead, contacts):
+def windows(contacts, vectors):
     return pl.pallas_call(
         window_kernel,
-        out_shape=[jax.ShapeDtypeStruct((ROWS, BAND), F32)] * 3,
-        in_specs=[SMEM] + [VMEM] * 6,
-        out_specs=[VMEM] * 3,
-        scratch_shapes=[pltpu.VMEM((WIDE // LANE, ROWS + 2 * EDGE, LANE), F32)] * 4,
+        out_shape=[jax.ShapeDtypeStruct((ROWS, BAND), F32)] * 3
+        + [jax.ShapeDtypeStruct((24, SPAN), F32), jax.ShapeDtypeStruct((16, BAND), jnp.int32)],
+        in_specs=[VMEM] * 2,
+        out_specs=[VMEM, VMEM, pl.BlockSpec(memory_space=pltpu.HBM), VMEM, VMEM],
+        scratch_shapes=[pltpu.VMEM((WIDE // LANE, ROWS + 2 * EDGE, LANE), F32)] * 4
+        + [pltpu.VMEM((ROWS, BAND), F32), pltpu.SemaphoreType.DMA((4,))],
         compiler_params=params(16),
         cost_estimate=cost(2 * 10**7, 6 * 2**20),
-    )(core, final, swap, cross, pair, ahead, contacts)
-
-
-def tails(sums, own, donut, lower, base, count=64):
+    )(contacts, vectors)
+
+
+def edges(core, swap, cross, partial, counts, vectors):
+    return call(
+        edge_kernel,
+        (core, swap, cross, partial, counts, vectors),
+        [(32, BAND)],
+        [SMEM] + [VMEM] * 5,
+        scratch_shapes=[pltpu.VMEM((WIDE // LANE, 3 * EDGE, LANE), F32)] * 4,
+        cost_estimate=cost(10**6, 2**20),
+    )[0]
+
+
+def tails(sums, edge, donut, lower, base, count=64):
     block = pl.BlockSpec((count, BAND), lambda i: (i, 0))
     return pl.pallas_call(
         tail_kernel,
         grid=(ROWS // count,),
         out_shape=[jax.ShapeDtypeStruct((ROWS, BAND), F32)] * 2 + [jax.ShapeDtypeStruct((SLAB, LANE), F32)],
-        in_specs=[whole(sums.shape), whole(own.shape)] + [block] * 3,
+        in_specs=[whole(sums.shape), whole(edge.shape)] + [block] * 2 + [pl.BlockSpec(memory_space=pltpu.HBM)],
         out_specs=[block] * 2 + [whole((SLAB, LANE))],
-        scratch_shapes=[pltpu.VMEM((8, BAND), F32)],
+        scratch_shapes=[
+            pltpu.VMEM((8, BAND), F32),
+            pltpu.VMEM((ROWS, BAND), F32),
+            pltpu.SemaphoreType.DMA((ROWS // count,)),
+        ],
         compiler_params=params(),
-    )(sums, own, donut, lower, base)
+    )(sums, edge, donut, lower, base)
 
 
 def solution(mesh):
@@ -423,15 +520,16 @@
         own = last(core, skewed, *around(message))
         pair = both_cores(own)
         ahead = both_cores(moved(pair, lambda i: i - 2 if i % 2 == 0 else i - 4))
-        final, swap, cross, sums = final_band(core, skewed, pair, ahead, own, pairs, plane)
+        swap, cross, sums, vectors = final_band(core, skewed, pair, ahead, own, pairs, plane)
+        sums = lax.all_to_all(sums, "genome", 0, 0, axis_index_groups=planes)
+        donut, lower, base, partial, counts = windows(contacts, vectors)
+        sums, swap, cross, partial = lax.optimization_barrier((sums, swap, cross, partial))
+        sums = jnp.broadcast_to(jnp.sum(sums, axis=0, keepdims=True), (count // plane,) + sums.shape[1:])
+        sums = lax.all_to_all(sums, "genome", 0, 0, axis_index_groups=lines)
         swap = moved(swap, lambda i: i ^ 1)
         cross = moved(cross, lambda i: i - 1 if i % 2 == 0 else i + 1)
-        sums = lax.all_to_all(sums, "genome", 0, 0, axis_index_groups=planes)
-        sums, swap, cross = lax.optimization_barrier((sums, swap, cross))
-        sums = jnp.broadcast_to(jnp.sum(sums, axis=0, keepdims=True), (count // plane,) + sums.shape[1:])
-        sums = lax.all_to_all(sums, "genome", 0, 0, axis_index_groups=lines)
-        donut, lower, base = windows(core, final, swap, cross, pair, ahead, contacts)
-        pvalue_donut, pvalue_lower, bias = tails(sums, own, donut, lower, base)
+        edge = edges(core, swap, cross, partial, counts, vectors)
+        pvalue_donut, pvalue_lower, bias = tails(sums, edge, donut, lower, base)
         return pvalue_donut, pvalue_lower, bias.reshape(ROWS)
 
     placed = (P("genome", None), P("genome"))

time: 106 us -> 107 us (level)
  Pallas kernels: 15.3 us -> 18.1 us
  local copies, waits for them, and re-layouts: 8.6 us -> 7.4 us
    pallas_call x1, Pallas kernels: 8.34 us -> 10.7 us  [windows(): pl.pallas_call(window_kernel, out_shape=[jax.ShapeDtypeStruct((ROWS, BAND...]
    all_to_all x1, waiting for transfers between devices: 1.22 us -> 0.01 us  [shards(): sums = lax.all_to_all(sums, 'genome', 0, 0, axis_index_groups=lines)]
    unnamed x22, local copies, waits for them, and re-layouts: 7.87 us -> 6.67 us
    ppermute x7, waiting for transfers between devices: 16.6 us -> 17.7 us  [moved(): lax.ppermute(value, 'genome', [(i, t) for i, t in pairs if 0 <= t < count])]
    pallas_call x5 -> x6, Pallas kernels: 3.36 us -> 3.69 us  [call(): pl.pallas_call(kernel, out_shape=[jax.ShapeDtypeStruct(s, F32) for s in o...]
  transfers between devices with their start and end apart: 9 -> 9, of which waited for: 6 -> 5; matrix products, arithmetic and copies ran while one was open for 0% -> 0% of each run, Pallas kernels for 9% -> 12%
where the time goes in v4:
time: 107 us
  starting transfers between devices  46.5 us (43%)
  Pallas kernels  18.1 us (17%)
  waiting for transfers between devices  17.7 us (17%)
  blocking collectives  14.9 us (14%)
  local copies, waits for them, and re-layouts  7.4 us (7%)
  other arithmetic  1.22 us (1%)
    ppermute x7, starting transfers between devices, moved(): lax.ppermute(value, 'genome', [(i, t) for i, t in pairs if 0 <= t < count])  22.7 us
    ppermute x7, waiting for transfers between devices, moved(): lax.ppermute(value, 'genome', [(i, t) for i, t in pairs if 0 <= t < count])  17.7 us
    all_to_all x1, starting transfers between devices, shards(): sums = lax.all_to_all(sums, 'genome', 0, 0, axis_index_groups=lines)  16.5 us
    all_gather x8, blocking collectives, both_cores(): return lax.all_gather(value, 'genome', axis_index_groups=chips)  14.9 us
    pallas_call x1, Pallas kernels, windows(): pl.pallas_call(window_kernel, out_shape=[jax.ShapeDtypeStruct((ROWS, BAND...  10.7 us
    all_to_all x1, starting transfers between devices, shards(): sums = lax.all_to_all(sums, 'genome', 0, 0, axis_index_groups=planes)  7.36 us
    unnamed x22, local copies, waits for them, and re-layouts  6.67 us
    pallas_call x6, Pallas kernels, call(): pl.pallas_call(kernel, out_shape=[jax.ShapeDtypeStruct(s, F32) for s in o...  3.69 us
  transfers between devices with their start and end apart: 9, of which 5 were waited for; matrix products, arithmetic and copies ran while one was open for 0% of the time, Pallas kernels for 12%

profile of v4, /device:TPU:32, one launch (start us, length us, event | category | flops | bytes accessed | tf_op | source)
XLA Modules:
  0.0 106.5 jit_solution(7366046871738506439)
XLA Ops:
  3.0 1.8 %all-gather = f32[32,128]{1,0:T(8,128)S(1)} all-gather(f32[16,128]{1,0:T(8,128)S(1)} %get-tuple-element.22), channel_id=2, replica_groups={{0,1},{2,3},{4,5},{6,7},{8,9},{10,11},{12,13},{14,15},{16,17},{18,19},{..., dimensions={0}, use_global_device_ids=true | all-gather | bytes 24576 | tf_op jit(solution)/shard_map/all_gather | solution.py:501
  4.8 5.1 %collective-permute-start.1 = (f32[2,16,128]{2,1,0:T(8,128)S(1)}, f32[2,16,128]{2,1,0:T(8,128)S(1)}, u32[]{:S(2)}, u32[]{:S(2)}) collective-permute-start(f32[2,16,128]{2,1,0:T(8,128)S(1)} %bitcast.15), channel_id=1, source_target_pairs={{0,4},{2,6},{4,8},{5,1},{6,10},{7,3},{8,12},{9,5},{10,14},{11,7},{... | collective-permute-start | bytes 49160 | tf_op jit(solution)/shard_map/ppermute | solution.py:505
  9.9 2.6 %collective-permute-start = (f32[2,16,128]{2,1,0:T(8,128)S(1)}, f32[2,16,128]{2,1,0:T(8,128)S(1)}, u32[]{:S(2)}, u32[]{:S(2)}) collective-permute-start(f32[2,16,128]{2,1,0:T(8,128)S(1)} %bitcast.16), channel_id=1, source_target_pairs={{0,2},{2,4},{3,1},{4,6},{5,3},{6,8},{7,5},{8,10},{9,7},{10,12},{11... | collective-permute-start | bytes 49160 | tf_op jit(solution)/shard_map/ppermute | solution.py:505
  12.5 2.4 %collective-permute-done.1 = f32[2,16,128]{2,1,0:T(8,128)S(1)} collective-permute-done((f32[2,16,128]{2,1,0:T(8,128)S(1)}, f32[2,16,128]{2,1,0:T(8,128)S(1)}, u32[]{:S(2)}, u32[]{:S(2)}) %collective-permute-start.1) | collective-permute-done | bytes 16416 | tf_op jit(solution)/shard_map/ppermute | solution.py:505
  15.0 1.8 %all-gather.2 = f32[4,16,128]{2,1,0:T(8,128)S(1)} all-gather(f32[2,16,128]{2,1,0:T(8,128)S(1)} %collective-permute-done.1), channel_id=4, replica_groups={{0,1},{2,3},{4,5},{6,7},{8,9},{10,11},{12,13},{14,15},{16,17},{18,19},{..., dimensions={0}, use_global_device_ids=true | all-gather | bytes 49152 | tf_op jit(solution)/shard_map/all_gather | solution.py:501
  16.8 3.0 %collective-permute-done = f32[2,16,128]{2,1,0:T(8,128)S(1)} collective-permute-done((f32[2,16,128]{2,1,0:T(8,128)S(1)}, f32[2,16,128]{2,1,0:T(8,128)S(1)}, u32[]{:S(2)}, u32[]{:S(2)}) %collective-permute-start) | collective-permute-done | bytes 16416 | tf_op jit(solution)/shard_map/ppermute | solution.py:505
  19.8 1.8 %all-gather.1 = f32[4,16,128]{2,1,0:T(8,128)S(1)} all-gather(f32[2,16,128]{2,1,0:T(8,128)S(1)} %collective-permute-done), channel_id=3, replica_groups={{0,1},{2,3},{4,5},{6,7},{8,9},{10,11},{12,13},{14,15},{16,17},{18,19},{..., dimensions={0}, use_global_device_ids=true | all-gather | bytes 49152 | tf_op jit(solution)/shard_map/all_gather | solution.py:501
  21.9 1.8 %all-gather.3 = f32[32,128]{1,0:T(8,128)S(1)} all-gather(f32[16,128]{1,0:T(8,128)S(1)} %shard_map.50), channel_id=5, replica_groups={{0,1},{2,3},{4,5},{6,7},{8,9},{10,11},{12,13},{14,15},{16,17},{18,19},{..., dimensions={0}, use_global_device_ids=true | all-gather | bytes 24576 | tf_op jit(solution)/shard_map/all_gather | solution.py:501
  23.8 1.9 %collective-permute-start.3 = (f32[2,16,128]{2,1,0:T(8,128)S(1)}, f32[2,16,128]{2,1,0:T(8,128)S(1)}, u32[]{:S(2)}, u32[]{:S(2)}) collective-permute-start(f32[2,16,128]{2,1,0:T(8,128)S(1)} %bitcast.21), channel_id=1, source_target_pairs={{0,4},{2,6},{4,8},{5,1},{6,10},{7,3},{8,12},{9,5},{10,14},{11,7},{... | collective-permute-start | bytes 49160 | tf_op jit(solution)/shard_map/ppermute | solution.py:505
  25.7 1.9 %collective-permute-start.2 = (f32[2,16,128]{2,1,0:T(8,128)S(1)}, f32[2,16,128]{2,1,0:T(8,128)S(1)}, u32[]{:S(2)}, u32[]{:S(2)}) collective-permute-start(f32[2,16,128]{2,1,0:T(8,128)S(1)} %bitcast.22), channel_id=1, source_target_pairs={{0,2},{2,4},{3,1},{4,6},{5,3},{6,8},{7,5},{8,10},{9,7},{10,12},{11... | collective-permute-start | bytes 49160 | tf_op jit(solution)/shard_map/ppermute | solution.py:505
  27.6 6.3 %collective-permute-done.3 = f32[2,16,128]{2,1,0:T(8,128)S(1)} collective-permute-done((f32[2,16,128]{2,1,0:T(8,128)S(1)}, f32[2,16,128]{2,1,0:T(8,128)S(1)}, u32[]{:S(2)}, u32[]{:S(2)}) %collective-permute-start.3) | collective-permute-done | bytes 16416 | tf_op jit(solution)/shard_map/ppermute | solution.py:505
  33.9 1.8 %all-gather.5 = f32[4,16,128]{2,1,0:T(8,128)S(1)} all-gather(f32[2,16,128]{2,1,0:T(8,128)S(1)} %collective-permute-done.3), channel_id=7, replica_groups={{0,1},{2,3},{4,5},{6,7},{8,9},{10,11},{12,13},{14,15},{16,17},{18,19},{..., dimensions={0}, use_global_device_ids=true | all-gather | bytes 49152 | tf_op jit(solution)/shard_map/all_gather | solution.py:501
  35.7 1.8 %all-gather.4 = f32[4,16,128]{2,1,0:T(8,128)S(1)} all-gather(f32[2,16,128]{2,1,0:T(8,128)S(1)} %collective-permute-done.2), channel_id=6, replica_groups={{0,1},{2,3},{4,5},{6,7},{8,9},{10,11},{12,13},{14,15},{16,17},{18,19},{..., dimensions={0}, use_global_device_ids=true | all-gather | bytes 49152 | tf_op jit(solution)/shard_map/all_gather | solution.py:501
  37.8 1.9 %all-gather.6 = f32[16,128]{1,0:T(8,128)S(1)} all-gather(f32[8,128]{1,0:T(8,128)S(1)} %shard_map.51.own_ref), channel_id=8, replica_groups={{0,1},{2,3},{4,5},{6,7},{8,9},{10,11},{12,13},{14,15},{16,17},{18,19},{..., dimensions={0}, use_global_device_ids=true | all-gather | bytes 12288 | tf_op jit(solution)/shard_map/all_gather | solution.py:501
  39.7 2.6 %collective-permute-start.4 = (f32[2,8,128]{2,1,0:T(8,128)S(1)}, f32[2,8,128]{2,1,0:T(8,128)S(1)}, u32[]{:S(2)}, u32[]{:S(2)}) collective-permute-start(f32[2,8,128]{2,1,0:T(8,128)S(1)} %bitcast.25), channel_id=1, source_target_pairs={{2,0},{4,2},{5,1},{6,4},{7,3},{8,6},{9,5},{10,8},{11,7},{12,10},{1... | collective-permute-start | bytes 24584 | tf_op jit(solution)/shard_map/ppermute | solution.py:505
  43.4 1.8 %collective-permute-done.4 = f32[2,8,128]{2,1,0:T(8,128)S(1)} collective-permute-done((f32[2,8,128]{2,1,0:T(8,128)S(1)}, f32[2,8,128]{2,1,0:T(8,128)S(1)}, u32[]{:S(2)}, u32[]{:S(2)}) %collective-permute-start.4) | collective-permute-done | bytes 8224 | tf_op jit(solution)/shard_map/ppermute | solution.py:505
  45.2 2.0 %all-gather.7 = f32[4,8,128]{2,1,0:T(8,128)S(1)} all-gather(f32[2,8,128]{2,1,0:T(8,128)S(1)} %collective-permute-done.4), channel_id=9, replica_groups={{0,1},{2,3},{4,5},{6,7},{8,9},{10,11},{12,13},{14,15},{16,17},{18,19},{..., dimensions={0}, use_global_device_ids=true | all-gather | bytes 24576 | tf_op jit(solution)/shard_map/all_gather | solution.py:501
  48.4 7.4 %all-to-all-start = ((f32[32,1,2176]{2,1,0:T(1,128)}), f32[32,1,2176]{2,1,0:T(1,128)}, u32[]{:S(2)}, u32[]{:S(2)}) async-start(f32[32,1,2176]{2,1,0:T(1,128)} %get-tuple-element.23), calls=%async_computation | async-start | bytes 557056 | tf_op jit(solution)/shard_map/all_to_all | solution.py:524
  55.8 10.7 %shard_map.54 = (f32[256,1024]{1,0:T(8,128)S(1)}, f32[256,1024]{1,0:T(8,128)S(1)}, f32[256,1024]{1,0:T(8,128)S(1)}, f32[24,1280]{1,0:T(8,128)S(1)}, s32[16,1024]{1,0:T(8,128)S(1)}) custom-call(s32[256,1024]{1,0:T(8,128)S(1)} %copy-done.1, f32[8,1280]{1,0:T(8,128)S(1)} %get-tuple-element.26.vectors_ref), custom_call_target="tpu_custom_call" | custom-call | flops 20000000 | bytes 6291456 | tf_op jit(solution)/shard_map/pallas_call | solution.py:452
  70.7 16.5 %all-to-all-start.1 = ((f32[16,1,2176]{2,1,0:T(1,128)}), f32[16,1,2176]{2,1,0:T(1,128)S(1)}, u32[]{:S(2)}, u32[]{:S(2)}) async-start(f32[16,1,2176]{2,1,0:T(1,128)} %broadcast_in_dim.2), calls=%async_computation.1 | async-start | bytes 278528 | tf_op jit(solution)/shard_map/all_to_all | solution.py:528
  87.2 1.9 %collective-permute-start.5 = (f32[8,1280]{1,0:T(8,128)S(1)}, f32[8,1280]{1,0:T(8,128)S(1)}, u32[]{:S(2)}, u32[]{:S(2)}) collective-permute-start(f32[8,1280]{1,0:T(8,128)S(1)} %get-tuple-element.29), channel_id=1, source_target_pairs={{0,1},{1,0},{2,3},{3,2},{4,5},{5,4},{6,7},{7,6},{8,9},{9,8},{10,11... | collective-permute-start | bytes 122888 | tf_op jit(solution)/shard_map/ppermute | solution.py:505
  89.1 6.7 %collective-permute-start.6 = (f32[8,1280]{1,0:T(8,128)S(1)}, f32[8,1280]{1,0:T(8,128)S(1)}, u32[]{:S(2)}, u32[]{:S(2)}) collective-permute-start(f32[8,1280]{1,0:T(8,128)S(1)} %get-tuple-element.30), channel_id=1, source_target_pairs={{1,2},{2,1},{3,4},{4,3},{5,6},{6,5},{7,8},{8,7},{9,10},{10,9},{11,... | collective-permute-start | bytes 122888 | tf_op jit(solution)/shard_map/ppermute | solution.py:505
  95.8 4.1 %collective-permute-done.6.cross_ref = f32[8,1280]{1,0:T(8,128)S(1)} collective-permute-done((f32[8,1280]{1,0:T(8,128)S(1)}, f32[8,1280]{1,0:T(8,128)S(1)}, u32[]{:S(2)}, u32[]{:S(2)}) %collective-permute-start.6) | collective-permute-done | bytes 40992 | tf_op jit(solution)/shard_map/ppermute | solution.py:505
  102.9 3.6 %shard_map.56 = (f32[256,1024]{1,0:T(8,128)}, f32[256,1024]{1,0:T(8,128)}, f32[2,128]{1,0:T(2,128)}) custom-call(f32[16,1,2176]{2,1,0:T(1,128)S(1)} %all-to-all-done.1.sums_ref, f32[32,1024]{1,0:T(8,128)S(1)} %shard_map.55.edge_ref, f32[256,1024]{1,0:T(8,128)S(1)} %get-tuple-element.33.donut_ref, f32[256,1024]{1,0:T(8,128)S(1)} %get-tuple-element.34.lower_ref, ...), custom_call_target="tpu_custom_call" | custom-call | tf_op jit(solution)/shard_map/pallas_call | solution.py:478
  (34 shorter events, 12.3 us)
Async XLA Ops:
  0.6 1.2 %copy-start = (s32[256,1024]{1,0:T(8,128)S(1)}, s32[256,1024]{1,0:T(8,128)}, u32[]{:S(2)}) copy-start(s32[256,1024]{1,0:T(8,128)} %contacts_ref.3) | copy-start | bytes 3145732
  1.9 0.7 copy-start.10
  4.8 10.1 %collective-permute-start.1 = (f32[2,16,128]{2,1,0:T(8,128)S(1)}, f32[2,16,128]{2,1,0:T(8,128)S(1)}, u32[]{:S(2)}, u32[]{:S(2)}) collective-permute-start(f32[2,16,128]{2,1,0:T(8,128)S(1)} %bitcast.15), channel_id=1, source_target_pairs={{0,4},{2,6},{4,8},{5,1},{6,10},{7,3},{8,12},{9,5},{10,14},{11,7},{... | collective-permute-start | bytes 49160 | tf_op jit(solution)/shard_map/ppermute | solution.py:505
  9.9 9.9 %collective-permute-start = (f32[2,16,128]{2,1,0:T(8,128)S(1)}, f32[2,16,128]{2,1,0:T(8,128)S(1)}, u32[]{:S(2)}, u32[]{:S(2)}) collective-permute-start(f32[2,16,128]{2,1,0:T(8,128)S(1)} %bitcast.16), channel_id=1, source_target_pairs={{0,2},{2,4},{3,1},{4,6},{5,3},{6,8},{7,5},{8,10},{9,7},{10,12},{11... | collective-permute-start | bytes 49160 | tf_op jit(solution)/shard_map/ppermute | solution.py:505
  23.8 10.1 %collective-permute-start.3 = (f32[2,16,128]{2,1,0:T(8,128)S(1)}, f32[2,16,128]{2,1,0:T(8,128)S(1)}, u32[]{:S(2)}, u32[]{:S(2)}) collective-permute-start(f32[2,16,128]{2,1,0:T(8,128)S(1)} %bitcast.21), channel_id=1, source_target_pairs={{0,4},{2,6},{4,8},{5,1},{6,10},{7,3},{8,12},{9,5},{10,14},{11,7},{... | collective-permute-start | bytes 49160 | tf_op jit(solution)/shard_map/ppermute | solution.py:505
  25.7 10.0 %collective-permute-start.2 = (f32[2,16,128]{2,1,0:T(8,128)S(1)}, f32[2,16,128]{2,1,0:T(8,128)S(1)}, u32[]{:S(2)}, u32[]{:S(2)}) collective-permute-start(f32[2,16,128]{2,1,0:T(8,128)S(1)} %bitcast.22), channel_id=1, source_target_pairs={{0,2},{2,4},{3,1},{4,6},{5,3},{6,8},{7,5},{8,10},{9,7},{10,12},{11... | collective-permute-start | bytes 49160 | tf_op jit(solution)/shard_map/ppermute | solution.py:505
  37.8 18.0 %copy-start.1 = (s32[256,1024]{1,0:T(8,128)S(1)}, s32[256,1024]{1,0:T(8,128)}, u32[]{:S(2)}) copy-start(s32[256,1024]{1,0:T(8,128)} %contacts_ref.3) | copy-start | bytes 3145732
  39.7 5.5 %collective-permute-start.4 = (f32[2,8,128]{2,1,0:T(8,128)S(1)}, f32[2,8,128]{2,1,0:T(8,128)S(1)}, u32[]{:S(2)}, u32[]{:S(2)}) collective-permute-start(f32[2,8,128]{2,1,0:T(8,128)S(1)} %bitcast.25), channel_id=1, source_target_pairs={{2,0},{4,2},{5,1},{6,4},{7,3},{8,6},{9,5},{10,8},{11,7},{12,10},{1... | collective-permute-start | bytes 24584 | tf_op jit(solution)/shard_map/ppermute | solution.py:505
  48.4 51.6 %copy-start.4 = (f32[8,1280]{1,0:T(8,128)}, f32[8,1280]{1,0:T(8,128)S(1)}, u32[]{:S(2)}) copy-start(f32[8,1280]{1,0:T(8,128)S(1)} %get-tuple-element.26.vectors_ref) | copy-start | bytes 122884
  48.4 20.4 %all-to-all-start = ((f32[32,1,2176]{2,1,0:T(1,128)}), f32[32,1,2176]{2,1,0:T(1,128)}, u32[]{:S(2)}, u32[]{:S(2)}) async-start(f32[32,1,2176]{2,1,0:T(1,128)} %get-tuple-element.23), calls=%async_computation | async-start | bytes 557056 | tf_op jit(solution)/shard_map/all_to_all | solution.py:524
  66.5 1.0 copy-start.2
  67.5 0.6 copy-start.6
  68.1 0.6 copy-start.8
  68.8 34.1 %copy-start.3 = (f32[256,1024]{1,0:T(8,128)S(1)}, f32[256,1024]{1,0:T(8,128)}, u32[]{:S(2)}) copy-start(f32[256,1024]{1,0:T(8,128)} %copy-done.2) | copy-start | bytes 3145732
  70.7 32.2 %all-to-all-start.1 = ((f32[16,1,2176]{2,1,0:T(1,128)}), f32[16,1,2176]{2,1,0:T(1,128)S(1)}, u32[]{:S(2)}, u32[]{:S(2)}) async-start(f32[16,1,2176]{2,1,0:T(1,128)} %broadcast_in_dim.2), calls=%async_computation.1 | async-start | bytes 278528 | tf_op jit(solution)/shard_map/all_to_all | solution.py:528
  87.2 8.6 %collective-permute-start.5 = (f32[8,1280]{1,0:T(8,128)S(1)}, f32[8,1280]{1,0:T(8,128)S(1)}, u32[]{:S(2)}, u32[]{:S(2)}) collective-permute-start(f32[8,1280]{1,0:T(8,128)S(1)} %get-tuple-element.29), channel_id=1, source_target_pairs={{0,1},{1,0},{2,3},{3,2},{4,5},{5,4},{6,7},{7,6},{8,9},{9,8},{10,11... | collective-permute-start | bytes 122888 | tf_op jit(solution)/shard_map/ppermute | solution.py:505
  89.1 10.9 %collective-permute-start.6 = (f32[8,1280]{1,0:T(8,128)S(1)}, f32[8,1280]{1,0:T(8,128)S(1)}, u32[]{:S(2)}, u32[]{:S(2)}) collective-permute-start(f32[8,1280]{1,0:T(8,128)S(1)} %get-tuple-element.30), channel_id=1, source_target_pairs={{1,2},{2,1},{3,4},{4,3},{5,6},{6,5},{7,8},{8,7},{9,10},{10,9},{11,... | collective-permute-start | bytes 122888 | tf_op jit(solution)/shard_map/ppermute | solution.py:505
  100.0 0.8 copy-start.5
  100.7 0.9 copy-start.7
  101.6 0.8 copy-start.9

commit v5 on v3

--- a/solution.py
+++ b/solution.py
@@ -17,6 +17,7 @@
 STEP = 32
 EDGE = 8
 MASKED = -1.0
+TABLE_STEP = 32
 VMEM = pl.BlockSpec(memory_space=pltpu.VMEM)
 SMEM = pl.BlockSpec(memory_space=pltpu.SMEM)
 F32 = jnp.float32
@@ -77,9 +78,11 @@
     put_lanes(out_ref, MAPPED_AT, mapped_row)
 
 
-def begin_kernel(contacts_ref, mapped_ref, skewed_ref, out_ref):
+def begin_kernel(contacts_ref, mapped_ref, skewed_ref, out_ref, counts_ref):
     for start in range(0, ROWS, STEP):
-        counts = contacts_ref[start : start + STEP, :].astype(F32)
+        counts = contacts_ref[start : start + STEP, :]
+        counts_ref[start : start + STEP, :] = counts.astype(jnp.int16)
+        counts = counts.astype(F32)
         padded = jnp.concatenate([counts, jnp.zeros((STEP, SPAN - BAND), F32)], axis=1)
         skewed_ref[start : start + STEP, :] = pltpu.roll(padded, start, 1, stride=1, stride_axis=0)
     mapped = lanes(mapped_ref[...]).astype(F32)
@@ -162,7 +165,8 @@
     out_ref[...] = along_diagonals(lambda r: column_of(row, r, 8) * ahead, BAND)
 
 
-def band_kernel(core_ref, skewed_ref, pair_ref, ahead_ref, own_ref, pairs_ref, final_ref, swap_ref, cross_ref, sums_ref):
+def band_kernel(core_ref, skewed_ref, pair_ref, ahead_ref, own_ref, pairs_ref,
+                final_ref, swap_ref, cross_ref, sums_ref, vectors_ref):
     core = core_ref[0]
     slabs = [pair_ref[0], pair_ref[1], ahead_ref[0, 0], ahead_ref[0, 1], ahead_ref[1, 0], ahead_ref[1, 1]]
     ahead = ahead_of(core, [s[X_AT : X_AT + SLAB] for s in slabs])
@@ -175,79 +179,97 @@
     swap_ref[...] = jnp.where(core == 0, last, first)
     cross_ref[...] = jnp.where(core == 0, first, last)
     diagonals = along_diagonals(lambda r: final_ref[r : r + 8, :], BAND)
-    pairs = pairs_ref[...]
     own = own_ref[...]
-    row = jnp.concatenate([diagonals, pairs, own[4:5, : LANE // 2], own[5:6, : LANE // 2]], axis=1)
+    row = jnp.concatenate([diagonals, pairs_ref[...], own[4:5, : LANE // 2], own[5:6, : LANE // 2]], axis=1)
     for n in range(sums_ref.shape[0]):
         sums_ref[n] = row
-
-
-def straight(rows, start):
-    rows = pltpu.roll(flipped(rows), SPAN - start - 7, 1, stride=1, stride_axis=0)
-    return flipped(rows[:, :BAND])
+    vectors_ref[0:1, :] = ahead
+    vectors_ref[1:2, :] = jnp.where(ahead > 0, 1.0 / jnp.where(ahead > 0, ahead, 1.0), 0.0)
+    vectors_ref[2:3, :] = jnp.concatenate([lanes(own[SLAB : 2 * SLAB]), jnp.zeros((1, SPAN - ROWS), F32)], axis=1)
+
+
+def straight(rows, start, tile):
+    rows = pltpu.roll(flipped(rows), SPAN - 7 - start, 1, stride=1, stride_axis=0)
+    return flipped(rows[:, tile * LANE : tile * LANE + BAND])
 
 
 def put_tiles(ref, start, value):
-    for t in range(WIDE // LANE):
-        ref[t, start : start + value.shape[0], :] = value[:, t * LANE : (t + 1) * LANE]
-
-
-def window_kernel(core_ref, final_ref, swap_ref, cross_ref, pair_ref, ahead_ref, contacts_ref,
-                  donut_ref, lower_ref, base_ref, left_out_ref, left_ref, sides_out_ref, sides_ref):
+    for t in range(value.shape[1] // LANE):
+        ref[t, pl.ds(start, value.shape[0]), :] = value[:, t * LANE : (t + 1) * LANE]
+
+
+def put_tables(refs, start, cells):
+    left_out_ref, left_ref, sides_out_ref, sides_ref = refs
+    two = cells + pltpu.roll(cells, WIDE - 1, 1)
+    three = two + pltpu.roll(cells, WIDE - 2, 1)
+    left_out = pltpu.roll(three, 5, 1)
+    left_in = pltpu.roll(two, 2, 1)
+    sides_out = left_out + pltpu.roll(three, WIDE - 3, 1)
+    put_tiles(left_out_ref, start, left_out)
+    put_tiles(left_ref, start, left_out + left_in)
+    put_tiles(sides_out_ref, start, sides_out)
+    put_tiles(sides_ref, start, sides_out + left_in + pltpu.roll(two, WIDE - 1, 1))
+
+
+NEAR, BEYOND = range(1, INNER + 1), range(INNER + 1, OUTER + 1)
+
+
+def box_sums(out_ref, in_ref, at, signs):
+    def rows(ref, shift):
+        return jnp.concatenate([ref[t, at + shift : at + shift + 8, :] for t in range(SPAN // LANE)], axis=1)
+
+    return sum([rows(out_ref, s * a) for a in NEAR for s in signs] + [rows(in_ref, s * a) for a in BEYOND for s in signs])
+
+
+def inverse_root(count):
+    k = jnp.maximum(count, 1.0)
+    q = lax.rsqrt(k)
+    return k, q * (1.5 - 0.5 * k * q * q)
+
+
+def root_of(sums, weight, start, tile, counts, k, q):
+    value = jnp.where(weight > 0, jnp.maximum(sums, 0.0) * weight, MASKED)
+    value = straight(value, start, tile)
+    positive = value > 0.0
+    root = jnp.exp(jnp.log(jnp.where(positive, value, 1.0) * (q * q)) * (1.0 / 3.0))
+    root = jnp.where(positive, root * (k * q * (3.0 / 2.0**0.5)), 0.0)
+    distance = lax.broadcasted_iota(jnp.int32, (8, BAND), 1)
+    return jnp.where((counts > 0) & (distance >= 2 * OUTER) & (value >= 0.0), root, MASKED)
+
+
+def window_kernel(core_ref, final_ref, counts_ref, swap_ref, cross_ref, vectors_ref,
+                  donut_ref, lower_ref, own_ref, left_out_ref, left_ref, sides_out_ref, sides_ref, float_ref):
     core = core_ref[0]
-    slabs = [pair_ref[0], pair_ref[1], ahead_ref[0, 0], ahead_ref[0, 1], ahead_ref[1, 0], ahead_ref[1, 1]]
-
+    ahead, bias_ahead = vectors_ref[0:1, :], vectors_ref[1:2, :]
+    bias_row = bias_ahead[:, :ROWS]
+    own_ref[0:1, :] = jnp.concatenate([vectors_ref[2:3, :ROWS], ahead[:, : BAND - ROWS]], axis=1)
+    tables = (left_out_ref, left_ref, sides_out_ref, sides_ref)
     swap, cross = swap_ref[...], cross_ref[...]
     before = jnp.where(core == 0, cross, swap)
     after = jnp.where(core == 0, swap, cross)
     gap = jnp.zeros((EDGE, LANE), F32)
-    for start in range(0, ROWS + 2 * EDGE, EDGE):
-        if start == 0:
-            cells = jnp.concatenate([before[:, ROWS:], gap, before[:, :ROWS]], axis=1)
-        elif start == ROWS + EDGE:
-            cells = jnp.concatenate([gap] * SLAB + [after[:, : WIDE - ROWS]], axis=1)
-        else:
-            cells = jnp.concatenate([final_ref[start - EDGE : start, :], gap], axis=1)
-        two = cells + pltpu.roll(cells, WIDE - 1, 1)
-        three = two + pltpu.roll(cells, WIDE - 2, 1)
-        left_out = pltpu.roll(three, 5, 1)
-        left = left_out + pltpu.roll(two, 2, 1)
-        sides_out = left_out + pltpu.roll(three, WIDE - 3, 1)
-        put_tiles(left_out_ref, start, left_out)
-        put_tiles(left_ref, start, left)
-        put_tiles(sides_out_ref, start, sides_out)
-        put_tiles(sides_ref, start, sides_out + (left - left_out) + pltpu.roll(two, WIDE - 1, 1))
-
-    ahead = ahead_of(core, [s[X_AT : X_AT + SLAB] for s in slabs])
-    mapped = ahead > 0
-    bias_ahead = jnp.where(mapped, 1.0 / jnp.where(mapped, ahead, 1.0), 0.0)
-    bias_row = bias_ahead[:, :ROWS]
-    near, beyond = range(1, INNER + 1), range(INNER + 1, OUTER + 1)
+    put_tables(tables, 0, jnp.concatenate([before[:, ROWS:], gap, before[:, :ROWS]], axis=1))
+    put_tables(tables, ROWS + EDGE, jnp.concatenate([gap] * SLAB + [after[:, : WIDE - ROWS]], axis=1))
 
     for start in range(0, ROWS, 8):
-
-        def rows(ref, shift):
-            at = start + EDGE + shift
-            return jnp.concatenate([ref[t, at : at + 8, :] for t in range(SPAN // LANE)], axis=1)
-
-        weight = column_of(bias_row, start, 8) * bias_ahead
-        lower = sum([rows(left_out_ref, a) for a in near] + [rows(left_ref, a) for a in beyond])
-        donut = sum([rows(sides_out_ref, s * a) for a in near for s in (1, -1)]
-                    + [rows(sides_ref, s * a) for a in beyond for s in (1, -1)])
-        counts = contacts_ref[start : start + 8, :]
-        k = jnp.maximum(counts, 1).astype(F32)
-        inverse_k = 1.0 / k
-        scale = jnp.sqrt(k) * (3.0 / 2.0**0.5)
-        distance = lax.broadcasted_iota(jnp.int32, (8, BAND), 1)
-        keep = (counts > 0) & (distance >= 2 * OUTER)
-        base_ref[start : start + 8, :] = (1.0 - inverse_k * (1.0 / 9.0)) * scale
-        for sums, out_ref in ((donut, donut_ref), (lower, lower_ref)):
-            value = jnp.where(weight > 0, jnp.maximum(sums, 0.0) * weight, MASKED)
-            value = straight(value, start)
-            positive = value > 0.0
-            root = jnp.exp(jnp.log(jnp.where(positive, value, 1.0) * inverse_k) * (1.0 / 3.0))
-            root = jnp.where(positive, root * scale, 0.0)
-            out_ref[start : start + 8, :] = jnp.where(keep & (value >= 0.0), root, MASKED)
+        put_tables(tables, start + EDGE, jnp.concatenate([final_ref[start : start + 8, :], gap], axis=1))
+
+    for start in range(0, ROWS, STEP):
+        here = slice(start, start + STEP)
+        float_ref[here, :] = counts_ref[here, :].astype(jnp.int32).astype(F32)
+
+    for i in range(SLAB):
+        begin = i * LANE
+        views = [ref.at[:, pl.ds(begin, LANE + 2 * EDGE), :] for ref in tables]
+        for start in range(0, LANE, 8):
+            here = pl.ds(begin + start, 8)
+            weight = column_of(bias_row, begin + start, 8) * bias_ahead
+            counts = float_ref[here, :]
+            k, q = inverse_root(counts)
+            donut = box_sums(views[2], views[3], start + EDGE, (1, -1))
+            donut_ref[here, :BAND] = root_of(donut, weight, start, i, counts, k, q)
+            lower = box_sums(views[0], views[1], start + EDGE, (1,))
+            lower_ref[here, :] = root_of(lower, weight, start, i, counts, k, q)
 
 
 def half_erfc(x):
@@ -261,8 +283,10 @@
 
 
 def filter_sums(expected):
-    margin = 2 * OUTER
-    padded = jnp.concatenate([expected, jnp.zeros((1, LANE), F32)], axis=1)
+    lane = lax.broadcasted_iota(jnp.int32, expected.shape, 1)
+    none = jnp.zeros((1, LANE), F32)
+    after = jnp.concatenate([expected[1:], none], axis=0)
+    before = jnp.concatenate([none, expected[:-1]], axis=0)
     donut_weight, lower_weight = {}, {}
     for a in range(-OUTER, OUTER + 1):
         for c in range(-OUTER, OUTER + 1):
@@ -271,9 +295,12 @@
             if a >= 1 and c <= -1 and not (a <= INNER and c >= -INNER):
                 lower_weight[c - a] = lower_weight.get(c - a, 0) + 1
     donut = lower = None
-    for k in range(-margin, margin + 1):
-        moved = pltpu.roll(padded, (-k) % (BAND + LANE), 1) if k else padded
-        moved = moved[:, :BAND]
+    for k in range(-2 * OUTER, 2 * OUTER + 1):
+        moved = expected
+        if k:
+            turn = (-k) % LANE
+            here = (lane + k < LANE) if k > 0 else (lane + k >= 0)
+            moved = jnp.where(here, pltpu.roll(expected, turn, 1), pltpu.roll(after if k > 0 else before, turn, 1))
         if k in donut_weight:
             part = moved * float(donut_weight[k])
             donut = part if donut is None else donut + part
@@ -289,33 +316,37 @@
     return jnp.where(positive, root, value)
 
 
-def tail_kernel(sums_ref, own_ref, donut_ref, lower_ref, base_ref, pvalue_donut_ref, pvalue_lower_ref, bias_ref, ratio_ref):
+def tiled(row):
+    return jnp.concatenate([row[:, t : t + LANE] for t in range(0, row.shape[1], LANE)], axis=0)
+
+
+def tail_kernel(sums_ref, own_ref, donut_ref, lower_ref, counts_ref, pvalue_donut_ref, pvalue_lower_ref, bias_ref,
+                ratio_ref):
     @pl.when(pl.program_id(0) == 0)
     def _():
         total = sums_ref[0]
         for n in range(1, sums_ref.shape[0]):
             total = total + sums_ref[n]
-        diagonals, pairs = total[:, :BAND], total[:, BAND : 2 * BAND]
-        expected = diagonals / pairs
+        pairs = tiled(total[:, BAND : 2 * BAND])
+        expected = tiled(total[:, :BAND]) / pairs
         donut_exp, lower_exp = filter_sums(expected)
-        ratio_ref[0:1, :] = cube_root(expected / donut_exp)
-        ratio_ref[1:2, :] = cube_root(expected / lower_exp)
-        mapped_count = pairs[:, 0:1]
+        ratio_ref[0:1, :] = lanes(cube_root(expected / donut_exp))
+        ratio_ref[1:2, :] = lanes(cube_root(expected / lower_exp))
+        mapped_count = pairs[0:1, 0:1]
         half = LANE // 2
         first = total[:, 2 * BAND : 2 * BAND + 1] / mapped_count
         second = total[:, 2 * BAND + half : 2 * BAND + half + 1] / mapped_count
-        own = own_ref[...]
-        bias = own[SLAB : 2 * SLAB]
-        mapped = own[0:SLAB] > 0
-        bias_ref[...] = jnp.where(mapped, bias / first / second, 1.0)
-
-    count = base_ref.shape[0]
-    for start in range(0, count, STEP):
-        base = base_ref[start : start + STEP, :]
+        own = own_ref[0:1, :]
+        put_lanes(bias_ref, 0, jnp.where(own[:, ROWS : 2 * ROWS] > 0, own[:, :ROWS] / first / second, 1.0))
+
+    for start in range(0, pvalue_donut_ref.shape[0], STEP):
+        here = slice(start, start + STEP)
+        k, q = inverse_root(counts_ref[here, :].astype(jnp.int32).astype(F32))
+        base = q * (k * (3.0 / 2.0**0.5) - 1.0 / (3.0 * 2.0**0.5))
         for at, root_ref, out_ref in ((0, donut_ref, pvalue_donut_ref), (1, lower_ref, pvalue_lower_ref)):
-            root = root_ref[start : start + STEP, :]
+            root = root_ref[here, :]
             value = half_erfc(base - root * ratio_ref[at : at + 1, :])
-            out_ref[start : start + STEP, :] = jnp.where(root < 0.0, 1.0, value)
+            out_ref[here, :] = jnp.where(root < 0.0, 1.0, value)
 
 
 def params(mib=8):
@@ -338,7 +369,14 @@
 
 
 def begin(contacts, mapped):
-    return call(begin_kernel, (contacts, mapped), [(ROWS, SPAN), (MESSAGE, LANE)])
+    shapes = [((ROWS, SPAN), F32), ((MESSAGE, LANE), F32), ((ROWS, BAND), jnp.int16)]
+    return pl.pallas_call(
+        begin_kernel,
+        out_shape=[jax.ShapeDtypeStruct(*s) for s in shapes],
+        in_specs=[VMEM] * 2,
+        out_specs=[VMEM] * 3,
+        compiler_params=params(),
+    )(contacts, mapped)
 
 
 def middle(core, skewed, pair, near, far):
@@ -359,53 +397,54 @@
     return call(
         band_kernel,
         (core, skewed, pair, ahead, own, pairs),
-        [(ROWS, SPAN), (EDGE, SPAN), (EDGE, SPAN), (copies, 1, 2 * BAND + LANE)],
+        [(ROWS, SPAN), (EDGE, SPAN), (EDGE, SPAN), (copies, 1, 2 * BAND + LANE), (8, SPAN)],
         [SMEM] + [VMEM] * 5,
     )
 
 
+def windows(core, final, counts, swap, cross, vectors):
+    return pl.pallas_call(
+        window_kernel,
+        out_shape=[jax.ShapeDtypeStruct(s, F32) for s in ((ROWS, SPAN), (ROWS, BAND), (8, BAND))],
+        in_specs=[SMEM] + [VMEM] * 5,
+        out_specs=[VMEM] * 3,
+        scratch_shapes=[pltpu.VMEM((WIDE // LANE, ROWS + 2 * EDGE, LANE), F32)] * 4 + [pltpu.VMEM((ROWS, BAND), F32)],
+        input_output_aliases={1: 0},
+        compiler_params=params(16),
+        cost_estimate=cost(2 * 10**7, 6 * 2**20),
+    )(core, final, counts, swap, cross, vectors)
+
+
 def whole(shape):
     return pl.BlockSpec(shape, lambda i: (0,) * len(shape))
 
 
-def windows(core, final, swap, cross, pair, ahead, contacts):
-    return pl.pallas_call(
-        window_kernel,
-        out_shape=[jax.ShapeDtypeStruct((ROWS, BAND), F32)] * 3,
-        in_specs=[SMEM] + [VMEM] * 6,
-        out_specs=[VMEM] * 3,
-        scratch_shapes=[pltpu.VMEM((WIDE // LANE, ROWS + 2 * EDGE, LANE), F32)] * 4,
-        compiler_params=params(16),
-        cost_estimate=cost(2 * 10**7, 6 * 2**20),
-    )(core, final, swap, cross, pair, ahead, contacts)
-
-
-def tails(sums, own, donut, lower, base, count=64):
-    block = pl.BlockSpec((count, BAND), lambda i: (i, 0))
+def tails(sums, own, donut, lower, counts, rows=64):
+    block = pl.BlockSpec((rows, BAND), lambda i: (i, 0))
     return pl.pallas_call(
         tail_kernel,
-        grid=(ROWS // count,),
+        grid=(ROWS // rows,),
         out_shape=[jax.ShapeDtypeStruct((ROWS, BAND), F32)] * 2 + [jax.ShapeDtypeStruct((SLAB, LANE), F32)],
         in_specs=[whole(sums.shape), whole(own.shape)] + [block] * 3,
         out_specs=[block] * 2 + [whole((SLAB, LANE))],
         scratch_shapes=[pltpu.VMEM((8, BAND), F32)],
         compiler_params=params(),
-    )(sums, own, donut, lower, base)
+    )(sums, own, donut, lower, counts)
 
 
 def solution(mesh):
-    count = mesh.shape["genome"]
-    plane = min(32, count)
-    chips = [[i, i + 1] for i in range(0, count, 2)]
-    planes = [[start + i for i in range(plane)] for start in range(0, count, plane)]
-    lines = [[i + start for start in range(0, count, plane)] for i in range(plane)]
+    size = mesh.shape["genome"]
+    plane = min(32, size)
+    chips = [[i, i + 1] for i in range(0, size, 2)]
+    planes = [[start + i for i in range(plane)] for start in range(0, size, plane)]
+    lines = [[i + start for start in range(0, size, plane)] for i in range(plane)]
 
     def both_cores(value):
         return lax.all_gather(value, "genome", axis_index_groups=chips)
 
     def moved(value, target):
-        pairs = [(i, target(i)) for i in range(count)]
-        return lax.ppermute(value, "genome", [(i, t) for i, t in pairs if 0 <= t < count])
+        pairs = [(i, target(i)) for i in range(size)]
+        return lax.ppermute(value, "genome", [(i, t) for i, t in pairs if 0 <= t < size])
 
     def around(message):
         pair = both_cores(message)
@@ -416,22 +455,22 @@
     def shards(contacts, mappable):
         core = lax.rem(lax.axis_index("genome"), 2).astype(jnp.int32).reshape(1)
         mapped = mappable.reshape(SLAB, LANE)
-        skewed, message = begin(contacts, mapped)
+        skewed, message, counts = begin(contacts, mapped)
         exchanged = around(message)
         pairs = pair_counts(core, *exchanged)
         message = middle(core, skewed, *exchanged)
         own = last(core, skewed, *around(message))
         pair = both_cores(own)
         ahead = both_cores(moved(pair, lambda i: i - 2 if i % 2 == 0 else i - 4))
-        final, swap, cross, sums = final_band(core, skewed, pair, ahead, own, pairs, plane)
+        final, swap, cross, sums, vectors = final_band(core, skewed, pair, ahead, own, pairs, plane)
+        cross = moved(cross, lambda i: i - 1 if i % 2 == 0 else i + 1)
         swap = moved(swap, lambda i: i ^ 1)
-        cross = moved(cross, lambda i: i - 1 if i % 2 == 0 else i + 1)
         sums = lax.all_to_all(sums, "genome", 0, 0, axis_index_groups=planes)
         sums, swap, cross = lax.optimization_barrier((sums, swap, cross))
-        sums = jnp.broadcast_to(jnp.sum(sums, axis=0, keepdims=True), (count // plane,) + sums.shape[1:])
+        sums = jnp.broadcast_to(jnp.sum(sums, axis=0, keepdims=True), (size // plane,) + sums.shape[1:])
         sums = lax.all_to_all(sums, "genome", 0, 0, axis_index_groups=lines)
-        donut, lower, base = windows(core, final, swap, cross, pair, ahead, contacts)
-        pvalue_donut, pvalue_lower, bias = tails(sums, own, donut, lower, base)
+        donut, lower, own = windows(core, final, counts, swap, cross, vectors)
+        pvalue_donut, pvalue_lower, bias = tails(sums, own, donut, lower, counts)
         return pvalue_donut, pvalue_lower, bias.reshape(ROWS)
 
     placed = (P("genome", None), P("genome"))

time: 106 us -> 103 us (0.972)
  local copies, waits for them, and re-layouts: 8.6 us -> 2.63 us
  waiting for transfers between devices: 17.8 us -> 20.9 us
    unnamed x22 -> x4, local copies, waits for them, and re-layouts: 7.87 us -> 1.9 us
    all_to_all x1, waiting for transfers between devices: 1.22 us -> 4.28 us  [shards(): sums = lax.all_to_all(sums, 'genome', 0, 0, axis_index_groups=lines)]
    pallas_call x2 -> x3, Pallas kernels: 11.9 us -> 12.7 us  [the longest x1 8.3 us: windows(): pl.pallas_call(window_kernel, out_shape=[jax.ShapeDtypeStruct(s, F32) for...]
    pallas_call x5 -> x4, Pallas kernels: 3.36 us -> 2.89 us  [call(): pl.pallas_call(kernel, out_shape=[jax.ShapeDtypeStruct(s, F32) for s in o...]
where the time goes in v5:
time: 103 us; the launch traced here: 102 us
  starting transfers between devices  47.5 us (46%)
  waiting for transfers between devices  20.9 us (20%)
  Pallas kernels  15.6 us (15%)
  blocking collectives  14.7 us (14%)
  local copies, waits for them, and re-layouts  2.63 us (3%)
    ppermute x7, starting transfers between devices, moved(): lax.ppermute(value, 'genome', [(i, t) for i, t in pairs if 0 <= t < size])  22.7 us
    all_to_all x1, starting transfers between devices, shards(): sums = lax.all_to_all(sums, 'genome', 0, 0, axis_index_groups=lines)  17.5 us
    ppermute x7, waiting for transfers between devices, moved(): lax.ppermute(value, 'genome', [(i, t) for i, t in pairs if 0 <= t < size])  16.6 us
    all_gather x8, blocking collectives, both_cores(): return lax.all_gather(value, 'genome', axis_index_groups=chips)  14.7 us
    pallas_call x1, Pallas kernels, windows(): pl.pallas_call(window_kernel, out_shape=[jax.ShapeDtypeStruct(s, F32) for...  8.3 us
    all_to_all x1, starting transfers between devices, shards(): sums = lax.all_to_all(sums, 'genome', 0, 0, axis_index_groups=planes)  7.25 us
    all_to_all x1, waiting for transfers between devices, shards(): sums = lax.all_to_all(sums, 'genome', 0, 0, axis_index_groups=lines)  4.28 us
    pallas_call x1, Pallas kernels, tails(): pl.pallas_call(tail_kernel, grid=(ROWS // rows,), out_shape=[jax.ShapeDty...  3.9 us
  transfers between devices with their start and end apart: 9, of which 6 were waited for; matrix products, arithmetic and copies ran while one was open for 0% of the time, Pallas kernels for 9%

profile of v5, /device:TPU:32, one launch (start us, length us, event | category | flops | bytes accessed | tf_op | source)
XLA Modules:
  0.0 102.2 jit_solution(3270960879176491678)
XLA Ops:
  3.0 1.8 %all-gather = f32[32,128]{1,0:T(8,128)S(1)} all-gather(f32[16,128]{1,0:T(8,128)S(1)} %get-tuple-element.21), channel_id=2, replica_groups={{0,1},{2,3},{4,5},{6,7},{8,9},{10,11},{12,13},{14,15},{16,17},{18,19},{..., dimensions={0}, use_global_device_ids=true | all-gather | bytes 24576 | tf_op jit(solution)/shard_map/all_gather | solution.py:443
  4.8 5.1 %collective-permute-start.1 = (f32[2,16,128]{2,1,0:T(8,128)S(1)}, f32[2,16,128]{2,1,0:T(8,128)S(1)}, u32[]{:S(2)}, u32[]{:S(2)}) collective-permute-start(f32[2,16,128]{2,1,0:T(8,128)S(1)} %bitcast.15), channel_id=1, source_target_pairs={{0,4},{2,6},{4,8},{5,1},{6,10},{7,3},{8,12},{9,5},{10,14},{11,7},{... | collective-permute-start | bytes 49160 | tf_op jit(solution)/shard_map/ppermute | solution.py:447
  9.9 2.6 %collective-permute-start = (f32[2,16,128]{2,1,0:T(8,128)S(1)}, f32[2,16,128]{2,1,0:T(8,128)S(1)}, u32[]{:S(2)}, u32[]{:S(2)}) collective-permute-start(f32[2,16,128]{2,1,0:T(8,128)S(1)} %bitcast.16), channel_id=1, source_target_pairs={{0,2},{2,4},{3,1},{4,6},{5,3},{6,8},{7,5},{8,10},{9,7},{10,12},{11... | collective-permute-start | bytes 49160 | tf_op jit(solution)/shard_map/ppermute | solution.py:447
  12.5 2.4 %collective-permute-done.1 = f32[2,16,128]{2,1,0:T(8,128)S(1)} collective-permute-done((f32[2,16,128]{2,1,0:T(8,128)S(1)}, f32[2,16,128]{2,1,0:T(8,128)S(1)}, u32[]{:S(2)}, u32[]{:S(2)}) %collective-permute-start.1) | collective-permute-done | bytes 16416 | tf_op jit(solution)/shard_map/ppermute | solution.py:447
  15.0 1.8 %all-gather.2 = f32[4,16,128]{2,1,0:T(8,128)S(1)} all-gather(f32[2,16,128]{2,1,0:T(8,128)S(1)} %collective-permute-done.1), channel_id=4, replica_groups={{0,1},{2,3},{4,5},{6,7},{8,9},{10,11},{12,13},{14,15},{16,17},{18,19},{..., dimensions={0}, use_global_device_ids=true | all-gather | bytes 49152 | tf_op jit(solution)/shard_map/all_gather | solution.py:443
  16.8 3.0 %collective-permute-done = f32[2,16,128]{2,1,0:T(8,128)S(1)} collective-permute-done((f32[2,16,128]{2,1,0:T(8,128)S(1)}, f32[2,16,128]{2,1,0:T(8,128)S(1)}, u32[]{:S(2)}, u32[]{:S(2)}) %collective-permute-start) | collective-permute-done | bytes 16416 | tf_op jit(solution)/shard_map/ppermute | solution.py:447
  19.8 1.8 %all-gather.1 = f32[4,16,128]{2,1,0:T(8,128)S(1)} all-gather(f32[2,16,128]{2,1,0:T(8,128)S(1)} %collective-permute-done), channel_id=3, replica_groups={{0,1},{2,3},{4,5},{6,7},{8,9},{10,11},{12,13},{14,15},{16,17},{18,19},{..., dimensions={0}, use_global_device_ids=true | all-gather | bytes 49152 | tf_op jit(solution)/shard_map/all_gather | solution.py:443
  21.9 1.8 %all-gather.3 = f32[32,128]{1,0:T(8,128)S(1)} all-gather(f32[16,128]{1,0:T(8,128)S(1)} %shard_map.50), channel_id=5, replica_groups={{0,1},{2,3},{4,5},{6,7},{8,9},{10,11},{12,13},{14,15},{16,17},{18,19},{..., dimensions={0}, use_global_device_ids=true | all-gather | bytes 24576 | tf_op jit(solution)/shard_map/all_gather | solution.py:443
  23.8 1.9 %collective-permute-start.3 = (f32[2,16,128]{2,1,0:T(8,128)S(1)}, f32[2,16,128]{2,1,0:T(8,128)S(1)}, u32[]{:S(2)}, u32[]{:S(2)}) collective-permute-start(f32[2,16,128]{2,1,0:T(8,128)S(1)} %bitcast.21), channel_id=1, source_target_pairs={{0,4},{2,6},{4,8},{5,1},{6,10},{7,3},{8,12},{9,5},{10,14},{11,7},{... | collective-permute-start | bytes 49160 | tf_op jit(solution)/shard_map/ppermute | solution.py:447
  25.7 1.9 %collective-permute-start.2 = (f32[2,16,128]{2,1,0:T(8,128)S(1)}, f32[2,16,128]{2,1,0:T(8,128)S(1)}, u32[]{:S(2)}, u32[]{:S(2)}) collective-permute-start(f32[2,16,128]{2,1,0:T(8,128)S(1)} %bitcast.22), channel_id=1, source_target_pairs={{0,2},{2,4},{3,1},{4,6},{5,3},{6,8},{7,5},{8,10},{9,7},{10,12},{11... | collective-permute-start | bytes 49160 | tf_op jit(solution)/shard_map/ppermute | solution.py:447
  27.6 6.3 %collective-permute-done.3 = f32[2,16,128]{2,1,0:T(8,128)S(1)} collective-permute-done((f32[2,16,128]{2,1,0:T(8,128)S(1)}, f32[2,16,128]{2,1,0:T(8,128)S(1)}, u32[]{:S(2)}, u32[]{:S(2)}) %collective-permute-start.3) | collective-permute-done | bytes 16416 | tf_op jit(solution)/shard_map/ppermute | solution.py:447
  33.9 1.8 %all-gather.5 = f32[4,16,128]{2,1,0:T(8,128)S(1)} all-gather(f32[2,16,128]{2,1,0:T(8,128)S(1)} %collective-permute-done.3), channel_id=7, replica_groups={{0,1},{2,3},{4,5},{6,7},{8,9},{10,11},{12,13},{14,15},{16,17},{18,19},{..., dimensions={0}, use_global_device_ids=true | all-gather | bytes 49152 | tf_op jit(solution)/shard_map/all_gather | solution.py:443
  35.7 1.8 %all-gather.4 = f32[4,16,128]{2,1,0:T(8,128)S(1)} all-gather(f32[2,16,128]{2,1,0:T(8,128)S(1)} %collective-permute-done.2), channel_id=6, replica_groups={{0,1},{2,3},{4,5},{6,7},{8,9},{10,11},{12,13},{14,15},{16,17},{18,19},{..., dimensions={0}, use_global_device_ids=true | all-gather | bytes 49152 | tf_op jit(solution)/shard_map/all_gather | solution.py:443
  39.6 2.6 %collective-permute-start.4 = (f32[2,8,128]{2,1,0:T(8,128)S(1)}, f32[2,8,128]{2,1,0:T(8,128)S(1)}, u32[]{:S(2)}, u32[]{:S(2)}) collective-permute-start(f32[2,8,128]{2,1,0:T(8,128)S(1)} %bitcast.25), channel_id=1, source_target_pairs={{2,0},{4,2},{5,1},{6,4},{7,3},{8,6},{9,5},{10,8},{11,7},{12,10},{1... | collective-permute-start | bytes 24584 | tf_op jit(solution)/shard_map/ppermute | solution.py:447
  43.3 1.8 %collective-permute-done.4 = f32[2,8,128]{2,1,0:T(8,128)S(1)} collective-permute-done((f32[2,8,128]{2,1,0:T(8,128)S(1)}, f32[2,8,128]{2,1,0:T(8,128)S(1)}, u32[]{:S(2)}, u32[]{:S(2)}) %collective-permute-start.4) | collective-permute-done | bytes 8224 | tf_op jit(solution)/shard_map/ppermute | solution.py:447
  45.1 2.0 %all-gather.7 = f32[4,8,128]{2,1,0:T(8,128)S(1)} all-gather(f32[2,8,128]{2,1,0:T(8,128)S(1)} %collective-permute-done.4), channel_id=9, replica_groups={{0,1},{2,3},{4,5},{6,7},{8,9},{10,11},{12,13},{14,15},{16,17},{18,19},{..., dimensions={0}, use_global_device_ids=true | all-gather | bytes 24576 | tf_op jit(solution)/shard_map/all_gather | solution.py:443
  48.3 7.2 %all-to-all-start = ((f32[32,1,2176]{2,1,0:T(1,128)}), f32[32,1,2176]{2,1,0:T(1,128)S(1)}, u32[]{:S(2)}, u32[]{:S(2)}) async-start(f32[32,1,2176]{2,1,0:T(1,128)} %get-tuple-element.22), calls=%async_computation | async-start | bytes 557056 | tf_op jit(solution)/shard_map/all_to_all | solution.py:468
  55.6 2.2 %collective-permute-start.5 = (f32[8,1280]{1,0:T(8,128)S(1)}, f32[8,1280]{1,0:T(8,128)S(1)}, u32[]{:S(2)}, u32[]{:S(2)}) collective-permute-start(f32[8,1280]{1,0:T(8,128)S(1)} %get-tuple-element.23), channel_id=1, source_target_pairs={{0,1},{1,0},{2,3},{3,2},{4,5},{5,4},{6,7},{7,6},{8,9},{9,8},{10,11... | collective-permute-start | bytes 122888 | tf_op jit(solution)/shard_map/ppermute | solution.py:447
  57.8 6.5 %collective-permute-start.6 = (f32[8,1280]{1,0:T(8,128)S(1)}, f32[8,1280]{1,0:T(8,128)S(1)}, u32[]{:S(2)}, u32[]{:S(2)}) collective-permute-start(f32[8,1280]{1,0:T(8,128)S(1)} %get-tuple-element.24), channel_id=1, source_target_pairs={{1,2},{2,1},{3,4},{4,3},{5,6},{6,5},{7,8},{8,7},{9,10},{10,9},{11,... | collective-permute-start | bytes 122888 | tf_op jit(solution)/shard_map/ppermute | solution.py:447
  64.3 3.0 %collective-permute-done.6.cross_ref = f32[8,1280]{1,0:T(8,128)S(1)} collective-permute-done((f32[8,1280]{1,0:T(8,128)S(1)}, f32[8,1280]{1,0:T(8,128)S(1)}, u32[]{:S(2)}, u32[]{:S(2)}) %collective-permute-start.6) | collective-permute-done | bytes 40992 | tf_op jit(solution)/shard_map/ppermute | solution.py:447
  68.2 17.5 %all-to-all-start.1 = ((f32[16,1,2176]{2,1,0:T(1,128)}), f32[16,1,2176]{2,1,0:T(1,128)S(1)}, u32[]{:S(2)}, u32[]{:S(2)}) async-start(f32[16,1,2176]{2,1,0:T(1,128)} %broadcast_in_dim.2), calls=%async_computation.1 | async-start | bytes 278528 | tf_op jit(solution)/shard_map/all_to_all | solution.py:471
  85.7 8.3 %shard_map.54 = (f32[256,1280]{1,0:T(8,128)S(1)}, f32[256,1024]{1,0:T(8,128)S(1)}, f32[8,1024]{1,0:T(8,128)S(1)}) custom-call(s32[1]{0:T(128)} %bitcast.core_ref, f32[256,1280]{1,0:T(8,128)S(1)} %get-tuple-element.26.final_ref, s16[256,1024]{1,0:T(8,128)(2,1)S(1)} %get-tuple-element.27.counts_ref, ...), custom_call_target="tpu_custom_call", output_to_operand_aliasing={{0}: (1, {})} | custom-call | flops 20000000 | bytes 6291456 | tf_op jit(solution)/shard_map/pallas_call | solution.py:406
  94.0 4.3 %all-to-all-done.1.sums_ref = f32[16,1,2176]{2,1,0:T(1,128)S(1)} async-done(((f32[16,1,2176]{2,1,0:T(1,128)}), f32[16,1,2176]{2,1,0:T(1,128)S(1)}, u32[]{:S(2)}, u32[]{:S(2)}) %all-to-all-start.1) | async-done | bytes 139296 | tf_op jit(solution)/shard_map/all_to_all | solution.py:471
  98.3 3.9 %shard_map.55 = (f32[256,1024]{1,0:T(8,128)}, f32[256,1024]{1,0:T(8,128)}, f32[2,128]{1,0:T(2,128)}) custom-call(f32[16,1,2176]{2,1,0:T(1,128)S(1)} %all-to-all-done.1.sums_ref, f32[8,1024]{1,0:T(8,128)S(1)} %get-tuple-element.31.own_ref, f32[256,1280]{1,0:T(8,128)S(1)} %get-tuple-element.32.donut_ref, f32[256,1024]{1,0:T(8,128)S(1)} %get-tuple-element.33.lower_ref, ...), custom_call_target="tpu_custom_call" | custom-call | tf_op jit(solution)/shard_map/pallas_call | solution.py:424
  (15 shorter events, 8.0 us)
Async XLA Ops:
  0.6 1.2 %copy-start = (s32[256,1024]{1,0:T(8,128)S(1)}, s32[256,1024]{1,0:T(8,128)}, u32[]{:S(2)}) copy-start(s32[256,1024]{1,0:T(8,128)} %contacts_ref.1) | copy-start | bytes 3145732
  1.9 0.7 copy-start.1
  4.8 10.1 %collective-permute-start.1 = (f32[2,16,128]{2,1,0:T(8,128)S(1)}, f32[2,16,128]{2,1,0:T(8,128)S(1)}, u32[]{:S(2)}, u32[]{:S(2)}) collective-permute-start(f32[2,16,128]{2,1,0:T(8,128)S(1)} %bitcast.15), channel_id=1, source_target_pairs={{0,4},{2,6},{4,8},{5,1},{6,10},{7,3},{8,12},{9,5},{10,14},{11,7},{... | collective-permute-start | bytes 49160 | tf_op jit(solution)/shard_map/ppermute | solution.py:447
  9.9 9.9 %collective-permute-start = (f32[2,16,128]{2,1,0:T(8,128)S(1)}, f32[2,16,128]{2,1,0:T(8,128)S(1)}, u32[]{:S(2)}, u32[]{:S(2)}) collective-permute-start(f32[2,16,128]{2,1,0:T(8,128)S(1)} %bitcast.16), channel_id=1, source_target_pairs={{0,2},{2,4},{3,1},{4,6},{5,3},{6,8},{7,5},{8,10},{9,7},{10,12},{11... | collective-permute-start | bytes 49160 | tf_op jit(solution)/shard_map/ppermute | solution.py:447
  23.8 10.1 %collective-permute-start.3 = (f32[2,16,128]{2,1,0:T(8,128)S(1)}, f32[2,16,128]{2,1,0:T(8,128)S(1)}, u32[]{:S(2)}, u32[]{:S(2)}) collective-permute-start(f32[2,16,128]{2,1,0:T(8,128)S(1)} %bitcast.21), channel_id=1, source_target_pairs={{0,4},{2,6},{4,8},{5,1},{6,10},{7,3},{8,12},{9,5},{10,14},{11,7},{... | collective-permute-start | bytes 49160 | tf_op jit(solution)/shard_map/ppermute | solution.py:447
  25.7 10.0 %collective-permute-start.2 = (f32[2,16,128]{2,1,0:T(8,128)S(1)}, f32[2,16,128]{2,1,0:T(8,128)S(1)}, u32[]{:S(2)}, u32[]{:S(2)}) collective-permute-start(f32[2,16,128]{2,1,0:T(8,128)S(1)} %bitcast.22), channel_id=1, source_target_pairs={{0,2},{2,4},{3,1},{4,6},{5,3},{6,8},{7,5},{8,10},{9,7},{10,12},{11... | collective-permute-start | bytes 49160 | tf_op jit(solution)/shard_map/ppermute | solution.py:447
  39.6 5.5 %collective-permute-start.4 = (f32[2,8,128]{2,1,0:T(8,128)S(1)}, f32[2,8,128]{2,1,0:T(8,128)S(1)}, u32[]{:S(2)}, u32[]{:S(2)}) collective-permute-start(f32[2,8,128]{2,1,0:T(8,128)S(1)} %bitcast.25), channel_id=1, source_target_pairs={{2,0},{4,2},{5,1},{6,4},{7,3},{8,6},{9,5},{10,8},{11,7},{12,10},{1... | collective-permute-start | bytes 24584 | tf_op jit(solution)/shard_map/ppermute | solution.py:447
  48.3 19.0 %all-to-all-start = ((f32[32,1,2176]{2,1,0:T(1,128)}), f32[32,1,2176]{2,1,0:T(1,128)S(1)}, u32[]{:S(2)}, u32[]{:S(2)}) async-start(f32[32,1,2176]{2,1,0:T(1,128)} %get-tuple-element.22), calls=%async_computation | async-start | bytes 557056 | tf_op jit(solution)/shard_map/all_to_all | solution.py:468
  55.6 8.7 %collective-permute-start.5 = (f32[8,1280]{1,0:T(8,128)S(1)}, f32[8,1280]{1,0:T(8,128)S(1)}, u32[]{:S(2)}, u32[]{:S(2)}) collective-permute-start(f32[8,1280]{1,0:T(8,128)S(1)} %get-tuple-element.23), channel_id=1, source_target_pairs={{0,1},{1,0},{2,3},{3,2},{4,5},{5,4},{6,7},{7,6},{8,9},{9,8},{10,11... | collective-permute-start | bytes 122888 | tf_op jit(solution)/shard_map/ppermute | solution.py:447
  57.8 9.5 %collective-permute-start.6 = (f32[8,1280]{1,0:T(8,128)S(1)}, f32[8,1280]{1,0:T(8,128)S(1)}, u32[]{:S(2)}, u32[]{:S(2)}) collective-permute-start(f32[8,1280]{1,0:T(8,128)S(1)} %get-tuple-element.24), channel_id=1, source_target_pairs={{1,2},{2,1},{3,4},{4,3},{5,6},{6,5},{7,8},{8,7},{9,10},{10,9},{11,... | collective-permute-start | bytes 122888 | tf_op jit(solution)/shard_map/ppermute | solution.py:447
  68.2 30.1 %all-to-all-start.1 = ((f32[16,1,2176]{2,1,0:T(1,128)}), f32[16,1,2176]{2,1,0:T(1,128)S(1)}, u32[]{:S(2)}, u32[]{:S(2)}) async-start(f32[16,1,2176]{2,1,0:T(1,128)} %broadcast_in_dim.2), calls=%async_computation.1 | async-start | bytes 278528 | tf_op jit(solution)/shard_map/all_to_all | solution.py:471

commit v6 on v5

--- a/solution.py
+++ b/solution.py
@@ -13,6 +13,7 @@
 SLAB = ROWS // LANE
 HOPS = BAND // ROWS
 SPAN = ROWS + BAND
+HALF = BAND + LANE
 WIDE = SPAN + LANE
 STEP = 32
 EDGE = 8
@@ -180,9 +181,9 @@
     cross_ref[...] = jnp.where(core == 0, first, last)
     diagonals = along_diagonals(lambda r: final_ref[r : r + 8, :], BAND)
     own = own_ref[...]
-    row = jnp.concatenate([diagonals, pairs_ref[...], own[4:5, : LANE // 2], own[5:6, : LANE // 2]], axis=1)
+    row = jnp.concatenate([diagonals, pairs_ref[...], own[4:5], own[5:6]], axis=1)
     for n in range(sums_ref.shape[0]):
-        sums_ref[n] = row
+        sums_ref[n] = row[:, :HALF] if n % 2 == 0 else row[:, HALF:]
     vectors_ref[0:1, :] = ahead
     vectors_ref[1:2, :] = jnp.where(ahead > 0, 1.0 / jnp.where(ahead > 0, ahead, 1.0), 0.0)
     vectors_ref[2:3, :] = jnp.concatenate([lanes(own[SLAB : 2 * SLAB]), jnp.zeros((1, SPAN - ROWS), F32)], axis=1)
@@ -324,18 +325,15 @@
                 ratio_ref):
     @pl.when(pl.program_id(0) == 0)
     def _():
-        total = sums_ref[0]
-        for n in range(1, sums_ref.shape[0]):
-            total = total + sums_ref[n]
+        total = jnp.concatenate([sum(sums_ref[core, n] for n in range(sums_ref.shape[1])) for core in range(2)], axis=1)
         pairs = tiled(total[:, BAND : 2 * BAND])
         expected = tiled(total[:, :BAND]) / pairs
         donut_exp, lower_exp = filter_sums(expected)
         ratio_ref[0:1, :] = lanes(cube_root(expected / donut_exp))
         ratio_ref[1:2, :] = lanes(cube_root(expected / lower_exp))
         mapped_count = pairs[0:1, 0:1]
-        half = LANE // 2
         first = total[:, 2 * BAND : 2 * BAND + 1] / mapped_count
-        second = total[:, 2 * BAND + half : 2 * BAND + half + 1] / mapped_count
+        second = total[:, 2 * BAND + LANE : 2 * BAND + LANE + 1] / mapped_count
         own = own_ref[0:1, :]
         put_lanes(bias_ref, 0, jnp.where(own[:, ROWS : 2 * ROWS] > 0, own[:, :ROWS] / first / second, 1.0))
 
@@ -397,7 +395,7 @@
     return call(
         band_kernel,
         (core, skewed, pair, ahead, own, pairs),
-        [(ROWS, SPAN), (EDGE, SPAN), (EDGE, SPAN), (copies, 1, 2 * BAND + LANE), (8, SPAN)],
+        [(ROWS, SPAN), (EDGE, SPAN), (EDGE, SPAN), (copies, 1, HALF), (8, SPAN)],
         [SMEM] + [VMEM] * 5,
     )
 
@@ -470,7 +468,7 @@
         sums = jnp.broadcast_to(jnp.sum(sums, axis=0, keepdims=True), (size // plane,) + sums.shape[1:])
         sums = lax.all_to_all(sums, "genome", 0, 0, axis_index_groups=lines)
         donut, lower, own = windows(core, final, counts, swap, cross, vectors)
-        pvalue_donut, pvalue_lower, bias = tails(sums, own, donut, lower, counts)
+        pvalue_donut, pvalue_lower, bias = tails(both_cores(sums), own, donut, lower, counts)
         return pvalue_donut, pvalue_lower, bias.reshape(ROWS)
 
     placed = (P("genome", None), P("genome"))

time: 103 us -> 106 us (1.029)
  the two profiles are of different devices: /device:TPU:32 before, /device:TPU:1 now
where the time goes in v6:
time: 106 us; the launch traced here: 105 us
  starting transfers between devices  40.7 us (38%)
  blocking collectives  29.1 us (27%)
  waiting for transfers between devices  16.6 us (16%)
  Pallas kernels  15.5 us (15%)
  local copies, waits for them, and re-layouts  2.57 us (2%)
    all_gather x9, blocking collectives, both_cores(): return lax.all_gather(value, 'genome', axis_index_groups=chips)  29.1 us
    all_to_all x1, starting transfers between devices, shards(): sums = lax.all_to_all(sums, 'genome', 0, 0, axis_index_groups=lines)  16.2 us
    ppermute x7, waiting for transfers between devices, moved(): lax.ppermute(value, 'genome', [(i, t) for i, t in pairs if 0 <= t < size])  13 us
    all_to_all x1, starting transfers between devices, shards(): sums = lax.all_to_all(sums, 'genome', 0, 0, axis_index_groups=planes)  12.5 us
    ppermute x7, starting transfers between devices, moved(): lax.ppermute(value, 'genome', [(i, t) for i, t in pairs if 0 <= t < size])  12 us
    pallas_call x1, Pallas kernels, windows(): pl.pallas_call(window_kernel, out_shape=[jax.ShapeDtypeStruct(s, F32) for...  8.31 us
    pallas_call x1, Pallas kernels, tails(): pl.pallas_call(tail_kernel, grid=(ROWS // rows,), out_shape=[jax.ShapeDty...  3.9 us
    all_to_all x1, waiting for transfers between devices, shards(): sums = lax.all_to_all(sums, 'genome', 0, 0, axis_index_groups=lines)  3.46 us
  transfers between devices with their start and end apart: 9, of which 6 were waited for; matrix products, arithmetic and copies ran while one was open for 0% of the time, Pallas kernels for 9%

profile of v6, /device:TPU:1, one launch (start us, length us, event | category | flops | bytes accessed | tf_op | source)
XLA Modules:
  0.0 105.4 jit_solution(11448590463704968563)
XLA Ops:
  3.0 8.4 %all-gather = f32[32,128]{1,0:T(8,128)S(1)} all-gather(f32[16,128]{1,0:T(8,128)S(1)} %get-tuple-element.21), channel_id=2, replica_groups={{0,1},{2,3},{4,5},{6,7},{8,9},{10,11},{12,13},{14,15},{16,17},{18,19},{..., dimensions={0}, use_global_device_ids=true | all-gather | bytes 24576 | tf_op jit(solution)/shard_map/all_gather | solution.py:441
  11.4 1.3 %collective-permute-start.1 = (f32[2,16,128]{2,1,0:T(8,128)S(1)}, f32[2,16,128]{2,1,0:T(8,128)S(1)}, u32[]{:S(2)}, u32[]{:S(2)}) collective-permute-start(f32[2,16,128]{2,1,0:T(8,128)S(1)} %bitcast.17), channel_id=1, source_target_pairs={{0,4},{2,6},{4,8},{5,1},{6,10},{7,3},{8,12},{9,5},{10,14},{11,7},{... | collective-permute-start | bytes 49160 | tf_op jit(solution)/shard_map/ppermute | solution.py:445
  12.7 1.3 %collective-permute-start = (f32[2,16,128]{2,1,0:T(8,128)S(1)}, f32[2,16,128]{2,1,0:T(8,128)S(1)}, u32[]{:S(2)}, u32[]{:S(2)}) collective-permute-start(f32[2,16,128]{2,1,0:T(8,128)S(1)} %bitcast.18), channel_id=1, source_target_pairs={{0,2},{2,4},{3,1},{4,6},{5,3},{6,8},{7,5},{8,10},{9,7},{10,12},{11... | collective-permute-start | bytes 49160 | tf_op jit(solution)/shard_map/ppermute | solution.py:445
  14.0 3.4 %collective-permute-done.1 = f32[2,16,128]{2,1,0:T(8,128)S(1)} collective-permute-done((f32[2,16,128]{2,1,0:T(8,128)S(1)}, f32[2,16,128]{2,1,0:T(8,128)S(1)}, u32[]{:S(2)}, u32[]{:S(2)}) %collective-permute-start.1) | collective-permute-done | bytes 16416 | tf_op jit(solution)/shard_map/ppermute | solution.py:445
  17.4 1.8 %all-gather.2 = f32[4,16,128]{2,1,0:T(8,128)S(1)} all-gather(f32[2,16,128]{2,1,0:T(8,128)S(1)} %collective-permute-done.1), channel_id=4, replica_groups={{0,1},{2,3},{4,5},{6,7},{8,9},{10,11},{12,13},{14,15},{16,17},{18,19},{..., dimensions={0}, use_global_device_ids=true | all-gather | bytes 49152 | tf_op jit(solution)/shard_map/all_gather | solution.py:441
  19.2 1.8 %all-gather.1 = f32[4,16,128]{2,1,0:T(8,128)S(1)} all-gather(f32[2,16,128]{2,1,0:T(8,128)S(1)} %collective-permute-done), channel_id=3, replica_groups={{0,1},{2,3},{4,5},{6,7},{8,9},{10,11},{12,13},{14,15},{16,17},{18,19},{..., dimensions={0}, use_global_device_ids=true | all-gather | bytes 49152 | tf_op jit(solution)/shard_map/all_gather | solution.py:441
  21.3 1.8 %all-gather.3 = f32[32,128]{1,0:T(8,128)S(1)} all-gather(f32[16,128]{1,0:T(8,128)S(1)} %shard_map.50), channel_id=5, replica_groups={{0,1},{2,3},{4,5},{6,7},{8,9},{10,11},{12,13},{14,15},{16,17},{18,19},{..., dimensions={0}, use_global_device_ids=true | all-gather | bytes 24576 | tf_op jit(solution)/shard_map/all_gather | solution.py:441
  23.2 1.3 %collective-permute-start.3 = (f32[2,16,128]{2,1,0:T(8,128)S(1)}, f32[2,16,128]{2,1,0:T(8,128)S(1)}, u32[]{:S(2)}, u32[]{:S(2)}) collective-permute-start(f32[2,16,128]{2,1,0:T(8,128)S(1)} %bitcast.23), channel_id=1, source_target_pairs={{0,4},{2,6},{4,8},{5,1},{6,10},{7,3},{8,12},{9,5},{10,14},{11,7},{... | collective-permute-start | bytes 49160 | tf_op jit(solution)/shard_map/ppermute | solution.py:445
  24.4 1.3 %collective-permute-start.2 = (f32[2,16,128]{2,1,0:T(8,128)S(1)}, f32[2,16,128]{2,1,0:T(8,128)S(1)}, u32[]{:S(2)}, u32[]{:S(2)}) collective-permute-start(f32[2,16,128]{2,1,0:T(8,128)S(1)} %bitcast.24), channel_id=1, source_target_pairs={{0,2},{2,4},{3,1},{4,6},{5,3},{6,8},{7,5},{8,10},{9,7},{10,12},{11... | collective-permute-start | bytes 49160 | tf_op jit(solution)/shard_map/ppermute | solution.py:445
  25.7 3.4 %collective-permute-done.3 = f32[2,16,128]{2,1,0:T(8,128)S(1)} collective-permute-done((f32[2,16,128]{2,1,0:T(8,128)S(1)}, f32[2,16,128]{2,1,0:T(8,128)S(1)}, u32[]{:S(2)}, u32[]{:S(2)}) %collective-permute-start.3) | collective-permute-done | bytes 16416 | tf_op jit(solution)/shard_map/ppermute | solution.py:445
  29.1 1.8 %all-gather.5 = f32[4,16,128]{2,1,0:T(8,128)S(1)} all-gather(f32[2,16,128]{2,1,0:T(8,128)S(1)} %collective-permute-done.3), channel_id=7, replica_groups={{0,1},{2,3},{4,5},{6,7},{8,9},{10,11},{12,13},{14,15},{16,17},{18,19},{..., dimensions={0}, use_global_device_ids=true | all-gather | bytes 49152 | tf_op jit(solution)/shard_map/all_gather | solution.py:441
  31.0 1.8 %all-gather.4 = f32[4,16,128]{2,1,0:T(8,128)S(1)} all-gather(f32[2,16,128]{2,1,0:T(8,128)S(1)} %collective-permute-done.2), channel_id=6, replica_groups={{0,1},{2,3},{4,5},{6,7},{8,9},{10,11},{12,13},{14,15},{16,17},{18,19},{..., dimensions={0}, use_global_device_ids=true | all-gather | bytes 49152 | tf_op jit(solution)/shard_map/all_gather | solution.py:441
  33.0 1.8 %all-gather.6 = f32[16,128]{1,0:T(8,128)S(1)} all-gather(f32[8,128]{1,0:T(8,128)S(1)} %shard_map.51.own_ref), channel_id=8, replica_groups={{0,1},{2,3},{4,5},{6,7},{8,9},{10,11},{12,13},{14,15},{16,17},{18,19},{..., dimensions={0}, use_global_device_ids=true | all-gather | bytes 12288 | tf_op jit(solution)/shard_map/all_gather | solution.py:441
  37.2 4.1 %collective-permute-done.4 = f32[2,8,128]{2,1,0:T(8,128)S(1)} collective-permute-done((f32[2,8,128]{2,1,0:T(8,128)S(1)}, f32[2,8,128]{2,1,0:T(8,128)S(1)}, u32[]{:S(2)}, u32[]{:S(2)}) %collective-permute-start.4) | collective-permute-done | bytes 8224 | tf_op jit(solution)/shard_map/ppermute | solution.py:445
  41.3 1.8 %all-gather.7 = f32[4,8,128]{2,1,0:T(8,128)S(1)} all-gather(f32[2,8,128]{2,1,0:T(8,128)S(1)} %collective-permute-done.4), channel_id=9, replica_groups={{0,1},{2,3},{4,5},{6,7},{8,9},{10,11},{12,13},{14,15},{16,17},{18,19},{..., dimensions={0}, use_global_device_ids=true | all-gather | bytes 24576 | tf_op jit(solution)/shard_map/all_gather | solution.py:441
  44.3 12.5 %all-to-all-start = ((f32[32,1,1152]{2,1,0:T(1,128)}), f32[32,1,1152]{2,1,0:T(1,128)S(1)}, u32[]{:S(2)}, u32[]{:S(2)}) async-start(f32[32,1,1152]{2,1,0:T(1,128)} %get-tuple-element.22), calls=%async_computation | async-start | bytes 294912 | tf_op jit(solution)/shard_map/all_to_all | solution.py:466
  56.8 2.1 %collective-permute-start.5 = (f32[8,1280]{1,0:T(8,128)S(1)}, f32[8,1280]{1,0:T(8,128)S(1)}, u32[]{:S(2)}, u32[]{:S(2)}) collective-permute-start(f32[8,1280]{1,0:T(8,128)S(1)} %get-tuple-element.23), channel_id=1, source_target_pairs={{0,1},{1,0},{2,3},{3,2},{4,5},{5,4},{6,7},{7,6},{8,9},{9,8},{10,11... | collective-permute-start | bytes 122888 | tf_op jit(solution)/shard_map/ppermute | solution.py:445
  59.0 3.5 %collective-permute-start.6 = (f32[8,1280]{1,0:T(8,128)S(1)}, f32[8,1280]{1,0:T(8,128)S(1)}, u32[]{:S(2)}, u32[]{:S(2)}) collective-permute-start(f32[8,1280]{1,0:T(8,128)S(1)} %get-tuple-element.24), channel_id=1, source_target_pairs={{1,2},{2,1},{3,4},{4,3},{5,6},{6,5},{7,8},{8,7},{9,10},{10,9},{11,... | collective-permute-start | bytes 122888 | tf_op jit(solution)/shard_map/ppermute | solution.py:445
  62.4 2.1 %collective-permute-done.6.cross_ref = f32[8,1280]{1,0:T(8,128)S(1)} collective-permute-done((f32[8,1280]{1,0:T(8,128)S(1)}, f32[8,1280]{1,0:T(8,128)S(1)}, u32[]{:S(2)}, u32[]{:S(2)}) %collective-permute-start.6) | collective-permute-done | bytes 40992 | tf_op jit(solution)/shard_map/ppermute | solution.py:445
  65.4 16.2 %all-to-all-start.1 = ((f32[16,1,1152]{2,1,0:T(1,128)}), f32[16,1,1152]{2,1,0:T(1,128)S(1)}, u32[]{:S(2)}, u32[]{:S(2)}) async-start(f32[16,1,1152]{2,1,0:T(1,128)} %broadcast_in_dim.2), calls=%async_computation.1 | async-start | bytes 147456 | tf_op jit(solution)/shard_map/all_to_all | solution.py:469
  81.6 8.3 %shard_map.54 = (f32[256,1280]{1,0:T(8,128)S(1)}, f32[256,1024]{1,0:T(8,128)S(1)}, f32[8,1024]{1,0:T(8,128)S(1)}) custom-call(s32[1]{0:T(128)} %bitcast.core_ref, f32[256,1280]{1,0:T(8,128)S(1)} %get-tuple-element.26.final_ref, s16[256,1024]{1,0:T(8,128)(2,1)S(1)} %get-tuple-element.27.counts_ref, ...), custom_call_target="tpu_custom_call", output_to_operand_aliasing={{0}: (1, {})} | custom-call | flops 20000000 | bytes 6291456 | tf_op jit(solution)/shard_map/pallas_call | solution.py:404
  89.9 3.5 %all-to-all-done.1 = f32[16,1,1152]{2,1,0:T(1,128)S(1)} async-done(((f32[16,1,1152]{2,1,0:T(1,128)}), f32[16,1,1152]{2,1,0:T(1,128)S(1)}, u32[]{:S(2)}, u32[]{:S(2)}) %all-to-all-start.1) | async-done | bytes 73760 | tf_op jit(solution)/shard_map/all_to_all | solution.py:469
  93.4 8.1 %all-gather.8 = f32[32,1,1152]{2,1,0:T(1,128)S(1)} all-gather(f32[16,1,1152]{2,1,0:T(1,128)S(1)} %all-to-all-done.1), channel_id=10, replica_groups={{0,1},{2,3},{4,5},{6,7},{8,9},{10,11},{12,13},{14,15},{16,17},{18,19},{..., dimensions={0}, use_global_device_ids=true | all-gather | bytes 221184 | tf_op jit(solution)/shard_map/all_gather | solution.py:441
  101.4 3.9 %shard_map.55 = (f32[256,1024]{1,0:T(8,128)}, f32[256,1024]{1,0:T(8,128)}, f32[2,128]{1,0:T(2,128)}) custom-call(f32[2,16,1,1152]{3,2,1,0:T(1,128)S(1)} %bitcast.12, f32[8,1024]{1,0:T(8,128)S(1)} %get-tuple-element.31.own_ref, f32[256,1280]{1,0:T(8,128)S(1)} %get-tuple-element.32.donut_ref, f32[256,1024]{1,0:T(8,128)S(1)} %get-tuple-element.33.lower_ref, ...), custom_call_target="tpu_custom_call" | custom-call | tf_op jit(solution)/shard_map/pallas_call | solution.py:422
  (16 shorter events, 7.3 us)
Async XLA Ops:
  0.6 1.2 %copy-start = (s32[256,1024]{1,0:T(8,128)S(1)}, s32[256,1024]{1,0:T(8,128)}, u32[]{:S(2)}) copy-start(s32[256,1024]{1,0:T(8,128)} %contacts_ref.1) | copy-start | bytes 3145732
  1.9 0.7 copy-start.1
  11.4 6.0 %collective-permute-start.1 = (f32[2,16,128]{2,1,0:T(8,128)S(1)}, f32[2,16,128]{2,1,0:T(8,128)S(1)}, u32[]{:S(2)}, u32[]{:S(2)}) collective-permute-start(f32[2,16,128]{2,1,0:T(8,128)S(1)} %bitcast.17), channel_id=1, source_target_pairs={{0,4},{2,6},{4,8},{5,1},{6,10},{7,3},{8,12},{9,5},{10,14},{11,7},{... | collective-permute-start | bytes 49160 | tf_op jit(solution)/shard_map/ppermute | solution.py:445
  12.7 6.5 %collective-permute-start = (f32[2,16,128]{2,1,0:T(8,128)S(1)}, f32[2,16,128]{2,1,0:T(8,128)S(1)}, u32[]{:S(2)}, u32[]{:S(2)}) collective-permute-start(f32[2,16,128]{2,1,0:T(8,128)S(1)} %bitcast.18), channel_id=1, source_target_pairs={{0,2},{2,4},{3,1},{4,6},{5,3},{6,8},{7,5},{8,10},{9,7},{10,12},{11... | collective-permute-start | bytes 49160 | tf_op jit(solution)/shard_map/ppermute | solution.py:445
  23.2 6.0 %collective-permute-start.3 = (f32[2,16,128]{2,1,0:T(8,128)S(1)}, f32[2,16,128]{2,1,0:T(8,128)S(1)}, u32[]{:S(2)}, u32[]{:S(2)}) collective-permute-start(f32[2,16,128]{2,1,0:T(8,128)S(1)} %bitcast.23), channel_id=1, source_target_pairs={{0,4},{2,6},{4,8},{5,1},{6,10},{7,3},{8,12},{9,5},{10,14},{11,7},{... | collective-permute-start | bytes 49160 | tf_op jit(solution)/shard_map/ppermute | solution.py:445
  24.4 6.5 %collective-permute-start.2 = (f32[2,16,128]{2,1,0:T(8,128)S(1)}, f32[2,16,128]{2,1,0:T(8,128)S(1)}, u32[]{:S(2)}, u32[]{:S(2)}) collective-permute-start(f32[2,16,128]{2,1,0:T(8,128)S(1)} %bitcast.24), channel_id=1, source_target_pairs={{0,2},{2,4},{3,1},{4,6},{5,3},{6,8},{7,5},{8,10},{9,7},{10,12},{11... | collective-permute-start | bytes 49160 | tf_op jit(solution)/shard_map/ppermute | solution.py:445
  34.8 6.5 %collective-permute-start.4 = (f32[2,8,128]{2,1,0:T(8,128)S(1)}, f32[2,8,128]{2,1,0:T(8,128)S(1)}, u32[]{:S(2)}, u32[]{:S(2)}) collective-permute-start(f32[2,8,128]{2,1,0:T(8,128)S(1)} %bitcast.27), channel_id=1, source_target_pairs={{2,0},{4,2},{5,1},{6,4},{7,3},{8,6},{9,5},{10,8},{11,7},{12,10},{1... | collective-permute-start | bytes 24584 | tf_op jit(solution)/shard_map/ppermute | solution.py:445
  44.3 20.4 %all-to-all-start = ((f32[32,1,1152]{2,1,0:T(1,128)}), f32[32,1,1152]{2,1,0:T(1,128)S(1)}, u32[]{:S(2)}, u32[]{:S(2)}) async-start(f32[32,1,1152]{2,1,0:T(1,128)} %get-tuple-element.22), calls=%async_computation | async-start | bytes 294912 | tf_op jit(solution)/shard_map/all_to_all | solution.py:466
  56.8 5.6 %collective-permute-start.5 = (f32[8,1280]{1,0:T(8,128)S(1)}, f32[8,1280]{1,0:T(8,128)S(1)}, u32[]{:S(2)}, u32[]{:S(2)}) collective-permute-start(f32[8,1280]{1,0:T(8,128)S(1)} %get-tuple-element.23), channel_id=1, source_target_pairs={{0,1},{1,0},{2,3},{3,2},{4,5},{5,4},{6,7},{7,6},{8,9},{9,8},{10,11... | collective-permute-start | bytes 122888 | tf_op jit(solution)/shard_map/ppermute | solution.py:445
  59.0 5.6 %collective-permute-start.6 = (f32[8,1280]{1,0:T(8,128)S(1)}, f32[8,1280]{1,0:T(8,128)S(1)}, u32[]{:S(2)}, u32[]{:S(2)}) collective-permute-start(f32[8,1280]{1,0:T(8,128)S(1)} %get-tuple-element.24), channel_id=1, source_target_pairs={{1,2},{2,1},{3,4},{4,3},{5,6},{6,5},{7,8},{8,7},{9,10},{10,9},{11,... | collective-permute-start | bytes 122888 | tf_op jit(solution)/shard_map/ppermute | solution.py:445
  65.4 28.0 %all-to-all-start.1 = ((f32[16,1,1152]{2,1,0:T(1,128)}), f32[16,1,1152]{2,1,0:T(1,128)S(1)}, u32[]{:S(2)}, u32[]{:S(2)}) async-start(f32[16,1,1152]{2,1,0:T(1,128)} %broadcast_in_dim.2), calls=%async_computation.1 | async-start | bytes 147456 | tf_op jit(solution)/shard_map/all_to_all | solution.py:469

commit v7 on v5

--- a/solution.py
+++ b/solution.py
@@ -237,20 +237,14 @@
     return jnp.where((counts > 0) & (distance >= 2 * OUTER) & (value >= 0.0), root, MASKED)
 
 
-def window_kernel(core_ref, final_ref, counts_ref, swap_ref, cross_ref, vectors_ref,
-                  donut_ref, lower_ref, own_ref, left_out_ref, left_ref, sides_out_ref, sides_ref, float_ref):
-    core = core_ref[0]
-    ahead, bias_ahead = vectors_ref[0:1, :], vectors_ref[1:2, :]
+def window_kernel(final_ref, counts_ref, vectors_ref, donut_ref, lower_ref, partial_ref, left_out_ref, left_ref, sides_out_ref, sides_ref, float_ref):
+    bias_ahead = vectors_ref[1:2, :]
     bias_row = bias_ahead[:, :ROWS]
-    own_ref[0:1, :] = jnp.concatenate([vectors_ref[2:3, :ROWS], ahead[:, : BAND - ROWS]], axis=1)
     tables = (left_out_ref, left_ref, sides_out_ref, sides_ref)
-    swap, cross = swap_ref[...], cross_ref[...]
-    before = jnp.where(core == 0, cross, swap)
-    after = jnp.where(core == 0, swap, cross)
     gap = jnp.zeros((EDGE, LANE), F32)
-    put_tables(tables, 0, jnp.concatenate([before[:, ROWS:], gap, before[:, :ROWS]], axis=1))
-    put_tables(tables, ROWS + EDGE, jnp.concatenate([gap] * SLAB + [after[:, : WIDE - ROWS]], axis=1))
-
+    for ref in tables:
+        put_tiles(ref, 0, jnp.zeros((EDGE, WIDE), F32))
+        put_tiles(ref, ROWS + EDGE, jnp.zeros((EDGE, WIDE), F32))
     for start in range(0, ROWS, 8):
         put_tables(tables, start + EDGE, jnp.concatenate([final_ref[start : start + 8, :], gap], axis=1))
 
@@ -270,6 +264,37 @@
             donut_ref[here, :BAND] = root_of(donut, weight, start, i, counts, k, q)
             lower = box_sums(views[0], views[1], start + EDGE, (1,))
             lower_ref[here, :] = root_of(lower, weight, start, i, counts, k, q)
+            if begin + start == 0:
+                partial_ref[0:8, :] = donut
+            if begin + start == ROWS - 8:
+                partial_ref[8:16, :] = donut
+                partial_ref[16:24, :] = lower
+
+
+def edge_kernel(core_ref, swap_ref, cross_ref, partial_ref, counts_ref, vectors_ref, out_ref,
+                left_out_ref, left_ref, sides_out_ref, sides_ref):
+    core = core_ref[0]
+    swap, cross = swap_ref[...], cross_ref[...]
+    before = jnp.where(core == 0, cross, swap)
+    after = jnp.where(core == 0, swap, cross)
+    gap = jnp.zeros((EDGE, LANE), F32)
+    tables = (left_out_ref, left_ref, sides_out_ref, sides_ref)
+    for ref in tables:
+        put_tiles(ref, EDGE, jnp.zeros((EDGE, WIDE), F32))
+    put_tables(tables, 0, jnp.concatenate([before[:, ROWS:], gap, before[:, :ROWS]], axis=1))
+    put_tables(tables, 2 * EDGE, jnp.concatenate([gap] * SLAB + [after[:, : WIDE - ROWS]], axis=1))
+    bias_ahead = vectors_ref[1:2, :]
+    bias_row = bias_ahead[:, :ROWS]
+    last = ROWS - 8
+    donut_first = partial_ref[0:8, :] + box_sums(sides_out_ref, sides_ref, EDGE, (-1,))
+    donut_last = partial_ref[8:16, :] + box_sums(sides_out_ref, sides_ref, EDGE, (1,))
+    lower_last = partial_ref[16:24, :] + box_sums(left_out_ref, left_ref, EDGE, (1,))
+    floats = [counts_ref[r : r + 16, :].astype(jnp.int32).astype(F32) for r in (0, ROWS - 16)]
+    first_counts, last_counts = floats[0][0:8], floats[1][8:16]
+    for at, sums, start, counts in ((0, donut_first, 0, first_counts), (8, donut_last, last, last_counts), (16, lower_last, last, last_counts)):
+        weight = column_of(bias_row, start, 8) * bias_ahead
+        out_ref[at : at + 8, :] = root_of(sums, weight, start % LANE, start // LANE, counts, *inverse_root(counts))
+    out_ref[24:25, :] = jnp.concatenate([vectors_ref[2:3, :ROWS], vectors_ref[0:1, : BAND - ROWS]], axis=1)
 
 
 def half_erfc(x):
@@ -320,7 +345,7 @@
     return jnp.concatenate([row[:, t : t + LANE] for t in range(0, row.shape[1], LANE)], axis=0)
 
 
-def tail_kernel(sums_ref, own_ref, donut_ref, lower_ref, counts_ref, pvalue_donut_ref, pvalue_lower_ref, bias_ref,
+def tail_kernel(sums_ref, edge_ref, donut_ref, lower_ref, counts_ref, pvalue_donut_ref, pvalue_lower_ref, bias_ref,
                 ratio_ref):
     @pl.when(pl.program_id(0) == 0)
     def _():
@@ -336,15 +361,23 @@
         half = LANE // 2
         first = total[:, 2 * BAND : 2 * BAND + 1] / mapped_count
         second = total[:, 2 * BAND + half : 2 * BAND + half + 1] / mapped_count
-        own = own_ref[0:1, :]
+        own = edge_ref[24:25, :]
         put_lanes(bias_ref, 0, jnp.where(own[:, ROWS : 2 * ROWS] > 0, own[:, :ROWS] / first / second, 1.0))
 
-    for start in range(0, pvalue_donut_ref.shape[0], STEP):
+    step, rows = pl.program_id(0), pvalue_donut_ref.shape[0]
+    for start in range(0, rows, STEP):
         here = slice(start, start + STEP)
         k, q = inverse_root(counts_ref[here, :].astype(jnp.int32).astype(F32))
         base = q * (k * (3.0 / 2.0**0.5) - 1.0 / (3.0 * 2.0**0.5))
         for at, root_ref, out_ref in ((0, donut_ref, pvalue_donut_ref), (1, lower_ref, pvalue_lower_ref)):
             root = root_ref[here, :]
+            if start == 0 and at == 0:
+                top = jnp.where(step == 0, edge_ref[0:8, :], root[0:8])
+                root = jnp.concatenate([top, root[8:]], axis=0)
+            if start == rows - STEP:
+                edge = edge_ref[8:16, :] if at == 0 else edge_ref[16:24, :]
+                bottom = jnp.where(step == ROWS // rows - 1, edge, root[STEP - 8 :])
+                root = jnp.concatenate([root[: STEP - 8], bottom], axis=0)
             value = half_erfc(base - root * ratio_ref[at : at + 1, :])
             out_ref[here, :] = jnp.where(root < 0.0, 1.0, value)
 
@@ -402,17 +435,28 @@
     )
 
 
-def windows(core, final, counts, swap, cross, vectors):
+def windows(final, counts, vectors):
     return pl.pallas_call(
         window_kernel,
-        out_shape=[jax.ShapeDtypeStruct(s, F32) for s in ((ROWS, SPAN), (ROWS, BAND), (8, BAND))],
-        in_specs=[SMEM] + [VMEM] * 5,
+        out_shape=[jax.ShapeDtypeStruct(s, F32) for s in ((ROWS, SPAN), (ROWS, BAND), (24, SPAN))],
+        in_specs=[VMEM] * 3,
         out_specs=[VMEM] * 3,
         scratch_shapes=[pltpu.VMEM((WIDE // LANE, ROWS + 2 * EDGE, LANE), F32)] * 4 + [pltpu.VMEM((ROWS, BAND), F32)],
-        input_output_aliases={1: 0},
+        input_output_aliases={0: 0},
         compiler_params=params(16),
         cost_estimate=cost(2 * 10**7, 6 * 2**20),
-    )(core, final, counts, swap, cross, vectors)
+    )(final, counts, vectors)
+
+
+def edges(core, swap, cross, partial, counts, vectors):
+    return call(
+        edge_kernel,
+        (core, swap, cross, partial, counts, vectors),
+        [(32, BAND)],
+        [SMEM] + [VMEM] * 5,
+        scratch_shapes=[pltpu.VMEM((WIDE // LANE, 3 * EDGE, LANE), F32)] * 4,
+        cost_estimate=cost(10**6, 2**20),
+    )[0]
 
 
 def whole(shape):
@@ -463,14 +507,15 @@
         pair = both_cores(own)
         ahead = both_cores(moved(pair, lambda i: i - 2 if i % 2 == 0 else i - 4))
         final, swap, cross, sums, vectors = final_band(core, skewed, pair, ahead, own, pairs, plane)
-        cross = moved(cross, lambda i: i - 1 if i % 2 == 0 else i + 1)
         swap = moved(swap, lambda i: i ^ 1)
         sums = lax.all_to_all(sums, "genome", 0, 0, axis_index_groups=planes)
-        sums, swap, cross = lax.optimization_barrier((sums, swap, cross))
         sums = jnp.broadcast_to(jnp.sum(sums, axis=0, keepdims=True), (size // plane,) + sums.shape[1:])
+        sums, swap, cross, final = lax.optimization_barrier((sums, swap, cross, final))
         sums = lax.all_to_all(sums, "genome", 0, 0, axis_index_groups=lines)
-        donut, lower, own = windows(core, final, counts, swap, cross, vectors)
-        pvalue_donut, pvalue_lower, bias = tails(sums, own, donut, lower, counts)
+        cross = moved(cross, lambda i: i - 1 if i % 2 == 0 else i + 1)
+        donut, lower, partial = windows(final, counts, vectors)
+        edge = edges(core, swap, cross, partial, counts, vectors)
+        pvalue_donut, pvalue_lower, bias = tails(sums, edge, donut, lower, counts)
         return pvalue_donut, pvalue_lower, bias.reshape(ROWS)
 
     placed = (P("genome", None), P("genome"))

time: 103 us -> 101 us (0.981)
  starting transfers between devices: 47.5 us -> 42.9 us
  waiting for transfers between devices: 20.9 us -> 23.4 us
    all_to_all x1, waiting for transfers between devices: 0.01 us -> 6.88 us  [shards(): sums = lax.all_to_all(sums, 'genome', 0, 0, axis_index_groups=planes)]
    ppermute x7, starting transfers between devices: 22.7 us -> 19.2 us  [moved(): lax.ppermute(value, 'genome', [(i, t) for i, t in pairs if 0 <= t < size])]
    ppermute x7, waiting for transfers between devices: 16.6 us -> 13.6 us  [moved(): lax.ppermute(value, 'genome', [(i, t) for i, t in pairs if 0 <= t < size])]
    all_to_all x1, waiting for transfers between devices: 4.28 us -> 2.98 us  [shards(): sums = lax.all_to_all(sums, 'genome', 0, 0, axis_index_groups=lines)]
    pallas_call x4 -> x5, Pallas kernels: 2.89 us -> 3.29 us  [call(): pl.pallas_call(kernel, out_shape=[jax.ShapeDtypeStruct(s, F32) for s in o...]
  transfers between devices with their start and end apart: 9 -> 9, of which waited for: 6 -> 6; matrix products, arithmetic and copies ran while one was open for 0% -> 0% of each run, Pallas kernels for 9% -> 10%
where the time goes in v7:
time: 101 us; the launch traced here: 100 us
  starting transfers between devices  42.9 us (42%)
  waiting for transfers between devices  23.4 us (23%)
  Pallas kernels  15.8 us (16%)
  blocking collectives  14.7 us (15%)
  local copies, waits for them, and re-layouts  2.63 us (3%)
    ppermute x7, starting transfers between devices, moved(): lax.ppermute(value, 'genome', [(i, t) for i, t in pairs if 0 <= t < size])  19.2 us
    all_to_all x1, starting transfers between devices, shards(): sums = lax.all_to_all(sums, 'genome', 0, 0, axis_index_groups=lines)  16.5 us
    all_gather x8, blocking collectives, both_cores(): return lax.all_gather(value, 'genome', axis_index_groups=chips)  14.7 us
    ppermute x7, waiting for transfers between devices, moved(): lax.ppermute(value, 'genome', [(i, t) for i, t in pairs if 0 <= t < size])  13.6 us
    pallas_call x1, Pallas kernels, windows(): pl.pallas_call(window_kernel, out_shape=[jax.ShapeDtypeStruct(s, F32) for...  8.08 us
    all_to_all x1, starting transfers between devices, shards(): sums = lax.all_to_all(sums, 'genome', 0, 0, axis_index_groups=planes)  7.25 us
    all_to_all x1, waiting for transfers between devices, shards(): sums = lax.all_to_all(sums, 'genome', 0, 0, axis_index_groups=planes)  6.88 us
    pallas_call x1, Pallas kernels, tails(): pl.pallas_call(tail_kernel, grid=(ROWS // rows,), out_shape=[jax.ShapeDty...  3.93 us
  transfers between devices with their start and end apart: 9, of which 6 were waited for; matrix products, arithmetic and copies ran while one was open for 0% of the time, Pallas kernels for 10%

profile of v7, /device:TPU:32, one launch (start us, length us, event | category | flops | bytes accessed | tf_op | source)
XLA Modules:
  0.0 100.4 jit_solution(7537933273388222407)
XLA Ops:
  3.0 1.8 %all-gather = f32[32,128]{1,0:T(8,128)S(1)} all-gather(f32[16,128]{1,0:T(8,128)S(1)} %get-tuple-element.22), channel_id=2, replica_groups={{0,1},{2,3},{4,5},{6,7},{8,9},{10,11},{12,13},{14,15},{16,17},{18,19},{..., dimensions={0}, use_global_device_ids=true | all-gather | bytes 24576 | tf_op jit(solution)/shard_map/all_gather | solution.py:487
  4.8 5.1 %collective-permute-start.1 = (f32[2,16,128]{2,1,0:T(8,128)S(1)}, f32[2,16,128]{2,1,0:T(8,128)S(1)}, u32[]{:S(2)}, u32[]{:S(2)}) collective-permute-start(f32[2,16,128]{2,1,0:T(8,128)S(1)} %bitcast.15), channel_id=1, source_target_pairs={{0,4},{2,6},{4,8},{5,1},{6,10},{7,3},{8,12},{9,5},{10,14},{11,7},{... | collective-permute-start | bytes 49160 | tf_op jit(solution)/shard_map/ppermute | solution.py:491
  9.9 2.6 %collective-permute-start = (f32[2,16,128]{2,1,0:T(8,128)S(1)}, f32[2,16,128]{2,1,0:T(8,128)S(1)}, u32[]{:S(2)}, u32[]{:S(2)}) collective-permute-start(f32[2,16,128]{2,1,0:T(8,128)S(1)} %bitcast.16), channel_id=1, source_target_pairs={{0,2},{2,4},{3,1},{4,6},{5,3},{6,8},{7,5},{8,10},{9,7},{10,12},{11... | collective-permute-start | bytes 49160 | tf_op jit(solution)/shard_map/ppermute | solution.py:491
  12.5 2.4 %collective-permute-done.1 = f32[2,16,128]{2,1,0:T(8,128)S(1)} collective-permute-done((f32[2,16,128]{2,1,0:T(8,128)S(1)}, f32[2,16,128]{2,1,0:T(8,128)S(1)}, u32[]{:S(2)}, u32[]{:S(2)}) %collective-permute-start.1) | collective-permute-done | bytes 16416 | tf_op jit(solution)/shard_map/ppermute | solution.py:491
  15.0 1.8 %all-gather.2 = f32[4,16,128]{2,1,0:T(8,128)S(1)} all-gather(f32[2,16,128]{2,1,0:T(8,128)S(1)} %collective-permute-done.1), channel_id=4, replica_groups={{0,1},{2,3},{4,5},{6,7},{8,9},{10,11},{12,13},{14,15},{16,17},{18,19},{..., dimensions={0}, use_global_device_ids=true | all-gather | bytes 49152 | tf_op jit(solution)/shard_map/all_gather | solution.py:487
  16.8 3.0 %collective-permute-done = f32[2,16,128]{2,1,0:T(8,128)S(1)} collective-permute-done((f32[2,16,128]{2,1,0:T(8,128)S(1)}, f32[2,16,128]{2,1,0:T(8,128)S(1)}, u32[]{:S(2)}, u32[]{:S(2)}) %collective-permute-start) | collective-permute-done | bytes 16416 | tf_op jit(solution)/shard_map/ppermute | solution.py:491
  19.8 1.8 %all-gather.1 = f32[4,16,128]{2,1,0:T(8,128)S(1)} all-gather(f32[2,16,128]{2,1,0:T(8,128)S(1)} %collective-permute-done), channel_id=3, replica_groups={{0,1},{2,3},{4,5},{6,7},{8,9},{10,11},{12,13},{14,15},{16,17},{18,19},{..., dimensions={0}, use_global_device_ids=true | all-gather | bytes 49152 | tf_op jit(solution)/shard_map/all_gather | solution.py:487
  21.9 1.8 %all-gather.3 = f32[32,128]{1,0:T(8,128)S(1)} all-gather(f32[16,128]{1,0:T(8,128)S(1)} %shard_map.50), channel_id=5, replica_groups={{0,1},{2,3},{4,5},{6,7},{8,9},{10,11},{12,13},{14,15},{16,17},{18,19},{..., dimensions={0}, use_global_device_ids=true | all-gather | bytes 24576 | tf_op jit(solution)/shard_map/all_gather | solution.py:487
  23.8 1.9 %collective-permute-start.3 = (f32[2,16,128]{2,1,0:T(8,128)S(1)}, f32[2,16,128]{2,1,0:T(8,128)S(1)}, u32[]{:S(2)}, u32[]{:S(2)}) collective-permute-start(f32[2,16,128]{2,1,0:T(8,128)S(1)} %bitcast.21), channel_id=1, source_target_pairs={{0,4},{2,6},{4,8},{5,1},{6,10},{7,3},{8,12},{9,5},{10,14},{11,7},{... | collective-permute-start | bytes 49160 | tf_op jit(solution)/shard_map/ppermute | solution.py:491
  25.7 1.9 %collective-permute-start.2 = (f32[2,16,128]{2,1,0:T(8,128)S(1)}, f32[2,16,128]{2,1,0:T(8,128)S(1)}, u32[]{:S(2)}, u32[]{:S(2)}) collective-permute-start(f32[2,16,128]{2,1,0:T(8,128)S(1)} %bitcast.22), channel_id=1, source_target_pairs={{0,2},{2,4},{3,1},{4,6},{5,3},{6,8},{7,5},{8,10},{9,7},{10,12},{11... | collective-permute-start | bytes 49160 | tf_op jit(solution)/shard_map/ppermute | solution.py:491
  27.6 6.3 %collective-permute-done.3 = f32[2,16,128]{2,1,0:T(8,128)S(1)} collective-permute-done((f32[2,16,128]{2,1,0:T(8,128)S(1)}, f32[2,16,128]{2,1,0:T(8,128)S(1)}, u32[]{:S(2)}, u32[]{:S(2)}) %collective-permute-start.3) | collective-permute-done | bytes 16416 | tf_op jit(solution)/shard_map/ppermute | solution.py:491
  33.9 1.8 %all-gather.5 = f32[4,16,128]{2,1,0:T(8,128)S(1)} all-gather(f32[2,16,128]{2,1,0:T(8,128)S(1)} %collective-permute-done.3), channel_id=7, replica_groups={{0,1},{2,3},{4,5},{6,7},{8,9},{10,11},{12,13},{14,15},{16,17},{18,19},{..., dimensions={0}, use_global_device_ids=true | all-gather | bytes 49152 | tf_op jit(solution)/shard_map/all_gather | solution.py:487
  35.7 1.8 %all-gather.4 = f32[4,16,128]{2,1,0:T(8,128)S(1)} all-gather(f32[2,16,128]{2,1,0:T(8,128)S(1)} %collective-permute-done.2), channel_id=6, replica_groups={{0,1},{2,3},{4,5},{6,7},{8,9},{10,11},{12,13},{14,15},{16,17},{18,19},{..., dimensions={0}, use_global_device_ids=true | all-gather | bytes 49152 | tf_op jit(solution)/shard_map/all_gather | solution.py:487
  39.6 2.6 %collective-permute-start.4 = (f32[2,8,128]{2,1,0:T(8,128)S(1)}, f32[2,8,128]{2,1,0:T(8,128)S(1)}, u32[]{:S(2)}, u32[]{:S(2)}) collective-permute-start(f32[2,8,128]{2,1,0:T(8,128)S(1)} %bitcast.25), channel_id=1, source_target_pairs={{2,0},{4,2},{5,1},{6,4},{7,3},{8,6},{9,5},{10,8},{11,7},{12,10},{1... | collective-permute-start | bytes 24584 | tf_op jit(solution)/shard_map/ppermute | solution.py:491
  43.3 1.8 %collective-permute-done.4 = f32[2,8,128]{2,1,0:T(8,128)S(1)} collective-permute-done((f32[2,8,128]{2,1,0:T(8,128)S(1)}, f32[2,8,128]{2,1,0:T(8,128)S(1)}, u32[]{:S(2)}, u32[]{:S(2)}) %collective-permute-start.4) | collective-permute-done | bytes 8224 | tf_op jit(solution)/shard_map/ppermute | solution.py:491
  45.1 2.0 %all-gather.7 = f32[4,8,128]{2,1,0:T(8,128)S(1)} all-gather(f32[2,8,128]{2,1,0:T(8,128)S(1)} %collective-permute-done.4), channel_id=9, replica_groups={{0,1},{2,3},{4,5},{6,7},{8,9},{10,11},{12,13},{14,15},{16,17},{18,19},{..., dimensions={0}, use_global_device_ids=true | all-gather | bytes 24576 | tf_op jit(solution)/shard_map/all_gather | solution.py:487
  48.3 7.2 %all-to-all-start = ((f32[32,1,2176]{2,1,0:T(1,128)}), f32[32,1,2176]{2,1,0:T(1,128)S(1)}, u32[]{:S(2)}, u32[]{:S(2)}) async-start(f32[32,1,2176]{2,1,0:T(1,128)} %get-tuple-element.23), calls=%async_computation | async-start | bytes 557056 | tf_op jit(solution)/shard_map/all_to_all | solution.py:511
  55.6 2.2 %collective-permute-start.5 = (f32[8,1280]{1,0:T(8,128)S(1)}, f32[8,1280]{1,0:T(8,128)S(1)}, u32[]{:S(2)}, u32[]{:S(2)}) collective-permute-start(f32[8,1280]{1,0:T(8,128)S(1)} %get-tuple-element.24), channel_id=1, source_target_pairs={{0,1},{1,0},{2,3},{3,2},{4,5},{5,4},{6,7},{7,6},{8,9},{9,8},{10,11... | collective-permute-start | bytes 122888 | tf_op jit(solution)/shard_map/ppermute | solution.py:491
  57.8 6.9 %all-to-all-done = f32[32,1,2176]{2,1,0:T(1,128)S(1)} async-done(((f32[32,1,2176]{2,1,0:T(1,128)}), f32[32,1,2176]{2,1,0:T(1,128)S(1)}, u32[]{:S(2)}, u32[]{:S(2)}) %all-to-all-start) | async-done | bytes 278560 | tf_op jit(solution)/shard_map/all_to_all | solution.py:511
  65.6 16.5 %all-to-all-start.1 = ((f32[16,1,2176]{2,1,0:T(1,128)}), f32[16,1,2176]{2,1,0:T(1,128)S(1)}, u32[]{:S(2)}, u32[]{:S(2)}) async-start(f32[16,1,2176]{2,1,0:T(1,128)} %broadcast_in_dim.2), calls=%async_computation.1 | async-start | bytes 278528 | tf_op jit(solution)/shard_map/all_to_all | solution.py:514
  82.0 3.0 %collective-permute-start.6 = (f32[8,1280]{1,0:T(8,128)S(1)}, f32[8,1280]{1,0:T(8,128)S(1)}, u32[]{:S(2)}, u32[]{:S(2)}) collective-permute-start(f32[8,1280]{1,0:T(8,128)S(1)} %get-tuple-element.29), channel_id=1, source_target_pairs={{1,2},{2,1},{3,4},{4,3},{5,6},{6,5},{7,8},{8,7},{9,10},{10,9},{11,... | collective-permute-start | bytes 122888 | tf_op jit(solution)/shard_map/ppermute | solution.py:491
  85.0 8.1 %shard_map.54 = (f32[256,1280]{1,0:T(8,128)S(1)}, f32[256,1024]{1,0:T(8,128)S(1)}, f32[24,1280]{1,0:T(8,128)S(1)}) custom-call(f32[256,1280]{1,0:T(8,128)S(1)} %get-tuple-element.30.final_ref, s16[256,1024]{1,0:T(8,128)(2,1)S(1)} %get-tuple-element.31.counts_ref, f32[8,1280]{1,0:T(8,128)S(1)} %get-tuple-element.32.vectors_ref), custom_call_target="tpu_custom_call", output_to_operand_aliasing={{0}: (0, {})} | custom-call | flops 20000000 | bytes 6291456 | tf_op jit(solution)/shard_map/pallas_call | solution.py:439
  93.5 3.0 %all-to-all-done.1.sums_ref = f32[16,1,2176]{2,1,0:T(1,128)S(1)} async-done(((f32[16,1,2176]{2,1,0:T(1,128)}), f32[16,1,2176]{2,1,0:T(1,128)S(1)}, u32[]{:S(2)}, u32[]{:S(2)}) %all-to-all-start.1) | async-done | bytes 139296 | tf_op jit(solution)/shard_map/all_to_all | solution.py:514
  96.5 3.9 %shard_map.56 = (f32[256,1024]{1,0:T(8,128)}, f32[256,1024]{1,0:T(8,128)}, f32[2,128]{1,0:T(2,128)}) custom-call(f32[16,1,2176]{2,1,0:T(1,128)S(1)} %all-to-all-done.1.sums_ref, f32[32,1024]{1,0:T(8,128)S(1)} %shard_map.55.edge_ref, f32[256,1280]{1,0:T(8,128)S(1)} %get-tuple-element.34.donut_ref, f32[256,1024]{1,0:T(8,128)S(1)} %get-tuple-element.35.lower_ref, ...), custom_call_target="tpu_custom_call" | custom-call | tf_op jit(solution)/shard_map/pallas_call | solution.py:468
  (16 shorter events, 8.4 us)
Async XLA Ops:
  0.6 1.2 %copy-start = (s32[256,1024]{1,0:T(8,128)S(1)}, s32[256,1024]{1,0:T(8,128)}, u32[]{:S(2)}) copy-start(s32[256,1024]{1,0:T(8,128)} %contacts_ref.1) | copy-start | bytes 3145732
  1.9 0.7 copy-start.1
  4.8 10.1 %collective-permute-start.1 = (f32[2,16,128]{2,1,0:T(8,128)S(1)}, f32[2,16,128]{2,1,0:T(8,128)S(1)}, u32[]{:S(2)}, u32[]{:S(2)}) collective-permute-start(f32[2,16,128]{2,1,0:T(8,128)S(1)} %bitcast.15), channel_id=1, source_target_pairs={{0,4},{2,6},{4,8},{5,1},{6,10},{7,3},{8,12},{9,5},{10,14},{11,7},{... | collective-permute-start | bytes 49160 | tf_op jit(solution)/shard_map/ppermute | solution.py:491
  9.9 9.9 %collective-permute-start = (f32[2,16,128]{2,1,0:T(8,128)S(1)}, f32[2,16,128]{2,1,0:T(8,128)S(1)}, u32[]{:S(2)}, u32[]{:S(2)}) collective-permute-start(f32[2,16,128]{2,1,0:T(8,128)S(1)} %bitcast.16), channel_id=1, source_target_pairs={{0,2},{2,4},{3,1},{4,6},{5,3},{6,8},{7,5},{8,10},{9,7},{10,12},{11... | collective-permute-start | bytes 49160 | tf_op jit(solution)/shard_map/ppermute | solution.py:491
  23.8 10.1 %collective-permute-start.3 = (f32[2,16,128]{2,1,0:T(8,128)S(1)}, f32[2,16,128]{2,1,0:T(8,128)S(1)}, u32[]{:S(2)}, u32[]{:S(2)}) collective-permute-start(f32[2,16,128]{2,1,0:T(8,128)S(1)} %bitcast.21), channel_id=1, source_target_pairs={{0,4},{2,6},{4,8},{5,1},{6,10},{7,3},{8,12},{9,5},{10,14},{11,7},{... | collective-permute-start | bytes 49160 | tf_op jit(solution)/shard_map/ppermute | solution.py:491
  25.7 10.0 %collective-permute-start.2 = (f32[2,16,128]{2,1,0:T(8,128)S(1)}, f32[2,16,128]{2,1,0:T(8,128)S(1)}, u32[]{:S(2)}, u32[]{:S(2)}) collective-permute-start(f32[2,16,128]{2,1,0:T(8,128)S(1)} %bitcast.22), channel_id=1, source_target_pairs={{0,2},{2,4},{3,1},{4,6},{5,3},{6,8},{7,5},{8,10},{9,7},{10,12},{11... | collective-permute-start | bytes 49160 | tf_op jit(solution)/shard_map/ppermute | solution.py:491
  39.6 5.5 %collective-permute-start.4 = (f32[2,8,128]{2,1,0:T(8,128)S(1)}, f32[2,8,128]{2,1,0:T(8,128)S(1)}, u32[]{:S(2)}, u32[]{:S(2)}) collective-permute-start(f32[2,8,128]{2,1,0:T(8,128)S(1)} %bitcast.25), channel_id=1, source_target_pairs={{2,0},{4,2},{5,1},{6,4},{7,3},{8,6},{9,5},{10,8},{11,7},{12,10},{1... | collective-permute-start | bytes 24584 | tf_op jit(solution)/shard_map/ppermute | solution.py:491
  48.3 16.3 %all-to-all-start = ((f32[32,1,2176]{2,1,0:T(1,128)}), f32[32,1,2176]{2,1,0:T(1,128)S(1)}, u32[]{:S(2)}, u32[]{:S(2)}) async-start(f32[32,1,2176]{2,1,0:T(1,128)} %get-tuple-element.23), calls=%async_computation | async-start | bytes 557056 | tf_op jit(solution)/shard_map/all_to_all | solution.py:511
  55.6 9.2 %collective-permute-start.5 = (f32[8,1280]{1,0:T(8,128)S(1)}, f32[8,1280]{1,0:T(8,128)S(1)}, u32[]{:S(2)}, u32[]{:S(2)}) collective-permute-start(f32[8,1280]{1,0:T(8,128)S(1)} %get-tuple-element.24), channel_id=1, source_target_pairs={{0,1},{1,0},{2,3},{3,2},{4,5},{5,4},{6,7},{7,6},{8,9},{9,8},{10,11... | collective-permute-start | bytes 122888 | tf_op jit(solution)/shard_map/ppermute | solution.py:491
  65.6 30.9 %all-to-all-start.1 = ((f32[16,1,2176]{2,1,0:T(1,128)}), f32[16,1,2176]{2,1,0:T(1,128)S(1)}, u32[]{:S(2)}, u32[]{:S(2)}) async-start(f32[16,1,2176]{2,1,0:T(1,128)} %broadcast_in_dim.2), calls=%async_computation.1 | async-start | bytes 278528 | tf_op jit(solution)/shard_map/all_to_all | solution.py:514
  82.0 11.1 %collective-permute-start.6 = (f32[8,1280]{1,0:T(8,128)S(1)}, f32[8,1280]{1,0:T(8,128)S(1)}, u32[]{:S(2)}, u32[]{:S(2)}) collective-permute-start(f32[8,1280]{1,0:T(8,128)S(1)} %get-tuple-element.29), channel_id=1, source_target_pairs={{1,2},{2,1},{3,4},{4,3},{5,6},{6,5},{7,8},{8,7},{9,10},{10,9},{11,... | collective-permute-start | bytes 122888 | tf_op jit(solution)/shard_map/ppermute | solution.py:491

commit v8 on v7

--- a/solution.py
+++ b/solution.py
@@ -137,20 +137,23 @@
         out_ref[at : at + 1, :] = jnp.broadcast_to(total, (1, LANE))
 
 
+def line_kernel(sums_ref, out_ref):
+    total = sums_ref[0]
+    for n in range(1, sums_ref.shape[0]):
+        total = total + sums_ref[n]
+    for n in range(out_ref.shape[0]):
+        out_ref[n] = total
+
+
 def flipped(rows):
     order = 7 - lax.broadcasted_iota(jnp.int32, (8, LANE), 0)
     tiles = [jnp.take_along_axis(rows[:, t : t + LANE], order, axis=0, mode="promise_in_bounds") for t in range(0, rows.shape[1], LANE)]
     return jnp.concatenate(tiles, axis=1)
 
 
-def along_diagonals(rows_of, width):
+def diagonal_sums(groups, width):
     total = None
-    for g in range(LANE // 8):
-        part = None
-        for h in range(SLAB):
-            rows = rows_of(h * LANE + 8 * g)
-            rows = rows[:, h * LANE : h * LANE + SPAN - LANE]
-            part = rows if part is None else part + rows
+    for g, part in enumerate(groups):
         if g:
             part = pltpu.roll(part, SPAN - LANE - 8 * g, 1)
         total = part if total is None else total + part
@@ -158,11 +161,22 @@
     return jnp.sum(total[:, :width], axis=0, keepdims=True)
 
 
+def along_diagonals(ref, width):
+    groups = []
+    for g in range(0, LANE, 8):
+        rows = [ref[h * LANE + g : h * LANE + g + 8, h * LANE : h * LANE + SPAN - LANE] for h in range(SLAB)]
+        groups.append(sum(rows[1:], rows[0]))
+    return diagonal_sums(groups, width)
+
+
 def pairs_kernel(core_ref, pair_ref, near_ref, far_ref, out_ref):
     refs = [pair_ref.at[0], pair_ref.at[1], near_ref.at[1, 0], near_ref.at[1, 1], far_ref.at[1, 0], far_ref.at[1, 1]]
     ahead = ahead_of(core_ref[0], [r[MAPPED_AT : MAPPED_AT + SLAB, :] for r in refs])
-    row = ahead[:, :ROWS]
-    out_ref[...] = along_diagonals(lambda r: column_of(row, r, 8) * ahead, BAND)
+    width = SPAN - LANE
+    none = jnp.zeros((8 - SLAB, width), F32)
+    rows = jnp.concatenate([ahead[:, h * LANE : h * LANE + width] for h in range(SLAB)] + [none], axis=0)
+    products = lax.dot_general(rows[:, :LANE], rows, (((0,), (0,)), ((), ())), preferred_element_type=F32)
+    out_ref[...] = diagonal_sums([products[r : r + 8] for r in range(0, LANE, 8)], BAND)
 
 
 def band_kernel(core_ref, skewed_ref, pair_ref, ahead_ref, own_ref, pairs_ref,
@@ -178,7 +192,7 @@
     first, last = final_ref[0:EDGE, :], final_ref[ROWS - EDGE : ROWS, :]
     swap_ref[...] = jnp.where(core == 0, last, first)
     cross_ref[...] = jnp.where(core == 0, first, last)
-    diagonals = along_diagonals(lambda r: final_ref[r : r + 8, :], BAND)
+    diagonals = along_diagonals(final_ref, BAND)
     own = own_ref[...]
     row = jnp.concatenate([diagonals, pairs_ref[...], own[4:5, : LANE // 2], own[5:6, : LANE // 2]], axis=1)
     for n in range(sums_ref.shape[0]):
@@ -223,8 +237,7 @@
 
 def inverse_root(count):
     k = jnp.maximum(count, 1.0)
-    q = lax.rsqrt(k)
-    return k, q * (1.5 - 0.5 * k * q * q)
+    return k, lax.rsqrt(k)
 
 
 def root_of(sums, weight, start, tile, counts, k, q):
@@ -509,7 +522,7 @@
         final, swap, cross, sums, vectors = final_band(core, skewed, pair, ahead, own, pairs, plane)
         swap = moved(swap, lambda i: i ^ 1)
         sums = lax.all_to_all(sums, "genome", 0, 0, axis_index_groups=planes)
-        sums = jnp.broadcast_to(jnp.sum(sums, axis=0, keepdims=True), (size // plane,) + sums.shape[1:])
+        sums = call(line_kernel, (sums,), [(size // plane,) + sums.shape[1:]])[0]
         sums, swap, cross, final = lax.optimization_barrier((sums, swap, cross, final))
         sums = lax.all_to_all(sums, "genome", 0, 0, axis_index_groups=lines)
         cross = moved(cross, lambda i: i - 1 if i % 2 == 0 else i + 1)

time: 101 us -> 101 us (level)
    pallas_call x5 -> x6, Pallas kernels: 3.29 us -> 3.38 us  [call(): pl.pallas_call(kernel, out_shape=[jax.ShapeDtypeStruct(s, F32) for s in o...]
where the time goes in v8:
time: 101 us; the launch traced here: 100 us
  starting transfers between devices  42.9 us (42%)
  waiting for transfers between devices  24 us (24%)
  Pallas kernels  15.7 us (16%)
  blocking collectives  14.7 us (15%)
  local copies, waits for them, and re-layouts  1.9 us (2%)
    ppermute x7, starting transfers between devices, moved(): lax.ppermute(value, 'genome', [(i, t) for i, t in pairs if 0 <= t < size])  19.2 us
    all_to_all x1, starting transfers between devices, shards(): sums = lax.all_to_all(sums, 'genome', 0, 0, axis_index_groups=lines)  16.5 us
    all_gather x8, blocking collectives, both_cores(): return lax.all_gather(value, 'genome', axis_index_groups=chips)  14.7 us
    ppermute x7, waiting for transfers between devices, moved(): lax.ppermute(value, 'genome', [(i, t) for i, t in pairs if 0 <= t < size])  14.2 us
    pallas_call x1, Pallas kernels, windows(): pl.pallas_call(window_kernel, out_shape=[jax.ShapeDtypeStruct(s, F32) for...  8.1 us
    all_to_all x1, starting transfers between devices, shards(): sums = lax.all_to_all(sums, 'genome', 0, 0, axis_index_groups=planes)  7.25 us
    all_to_all x1, waiting for transfers between devices, shards(): sums = lax.all_to_all(sums, 'genome', 0, 0, axis_index_groups=planes)  6.88 us
    pallas_call x1, Pallas kernels, tails(): pl.pallas_call(tail_kernel, grid=(ROWS // rows,), out_shape=[jax.ShapeDty...  3.76 us
  transfers between devices with their start and end apart: 9, of which 6 were waited for; matrix products, arithmetic and copies ran while one was open for 0% of the time, Pallas kernels for 10%

profile of v8, /device:TPU:32, one launch (start us, length us, event | category | flops | bytes accessed | tf_op | source)
XLA Modules:
  0.0 100.1 jit_solution(15432643386877805003)
XLA Ops:
  3.0 1.8 %all-gather = f32[32,128]{1,0:T(8,128)S(1)} all-gather(f32[16,128]{1,0:T(8,128)S(1)} %get-tuple-element.22), channel_id=2, replica_groups={{0,1},{2,3},{4,5},{6,7},{8,9},{10,11},{12,13},{14,15},{16,17},{18,19},{..., dimensions={0}, use_global_device_ids=true | all-gather | bytes 24576 | tf_op jit(solution)/shard_map/all_gather | solution.py:500
  4.8 5.1 %collective-permute-start.1 = (f32[2,16,128]{2,1,0:T(8,128)S(1)}, f32[2,16,128]{2,1,0:T(8,128)S(1)}, u32[]{:S(2)}, u32[]{:S(2)}) collective-permute-start(f32[2,16,128]{2,1,0:T(8,128)S(1)} %bitcast.15), channel_id=1, source_target_pairs={{0,4},{2,6},{4,8},{5,1},{6,10},{7,3},{8,12},{9,5},{10,14},{11,7},{... | collective-permute-start | bytes 49160 | tf_op jit(solution)/shard_map/ppermute | solution.py:504
  9.9 2.6 %collective-permute-start = (f32[2,16,128]{2,1,0:T(8,128)S(1)}, f32[2,16,128]{2,1,0:T(8,128)S(1)}, u32[]{:S(2)}, u32[]{:S(2)}) collective-permute-start(f32[2,16,128]{2,1,0:T(8,128)S(1)} %bitcast.16), channel_id=1, source_target_pairs={{0,2},{2,4},{3,1},{4,6},{5,3},{6,8},{7,5},{8,10},{9,7},{10,12},{11... | collective-permute-start | bytes 49160 | tf_op jit(solution)/shard_map/ppermute | solution.py:504
  12.5 2.4 %collective-permute-done.1 = f32[2,16,128]{2,1,0:T(8,128)S(1)} collective-permute-done((f32[2,16,128]{2,1,0:T(8,128)S(1)}, f32[2,16,128]{2,1,0:T(8,128)S(1)}, u32[]{:S(2)}, u32[]{:S(2)}) %collective-permute-start.1) | collective-permute-done | bytes 16416 | tf_op jit(solution)/shard_map/ppermute | solution.py:504
  15.0 1.8 %all-gather.2 = f32[4,16,128]{2,1,0:T(8,128)S(1)} all-gather(f32[2,16,128]{2,1,0:T(8,128)S(1)} %collective-permute-done.1), channel_id=4, replica_groups={{0,1},{2,3},{4,5},{6,7},{8,9},{10,11},{12,13},{14,15},{16,17},{18,19},{..., dimensions={0}, use_global_device_ids=true | all-gather | bytes 49152 | tf_op jit(solution)/shard_map/all_gather | solution.py:500
  16.8 3.0 %collective-permute-done = f32[2,16,128]{2,1,0:T(8,128)S(1)} collective-permute-done((f32[2,16,128]{2,1,0:T(8,128)S(1)}, f32[2,16,128]{2,1,0:T(8,128)S(1)}, u32[]{:S(2)}, u32[]{:S(2)}) %collective-permute-start) | collective-permute-done | bytes 16416 | tf_op jit(solution)/shard_map/ppermute | solution.py:504
  19.8 1.8 %all-gather.1 = f32[4,16,128]{2,1,0:T(8,128)S(1)} all-gather(f32[2,16,128]{2,1,0:T(8,128)S(1)} %collective-permute-done), channel_id=3, replica_groups={{0,1},{2,3},{4,5},{6,7},{8,9},{10,11},{12,13},{14,15},{16,17},{18,19},{..., dimensions={0}, use_global_device_ids=true | all-gather | bytes 49152 | tf_op jit(solution)/shard_map/all_gather | solution.py:500
  21.9 1.8 %all-gather.3 = f32[32,128]{1,0:T(8,128)S(1)} all-gather(f32[16,128]{1,0:T(8,128)S(1)} %shard_map.50), channel_id=5, replica_groups={{0,1},{2,3},{4,5},{6,7},{8,9},{10,11},{12,13},{14,15},{16,17},{18,19},{..., dimensions={0}, use_global_device_ids=true | all-gather | bytes 24576 | tf_op jit(solution)/shard_map/all_gather | solution.py:500
  23.8 1.9 %collective-permute-start.3 = (f32[2,16,128]{2,1,0:T(8,128)S(1)}, f32[2,16,128]{2,1,0:T(8,128)S(1)}, u32[]{:S(2)}, u32[]{:S(2)}) collective-permute-start(f32[2,16,128]{2,1,0:T(8,128)S(1)} %bitcast.21), channel_id=1, source_target_pairs={{0,4},{2,6},{4,8},{5,1},{6,10},{7,3},{8,12},{9,5},{10,14},{11,7},{... | collective-permute-start | bytes 49160 | tf_op jit(solution)/shard_map/ppermute | solution.py:504
  25.7 1.9 %collective-permute-start.2 = (f32[2,16,128]{2,1,0:T(8,128)S(1)}, f32[2,16,128]{2,1,0:T(8,128)S(1)}, u32[]{:S(2)}, u32[]{:S(2)}) collective-permute-start(f32[2,16,128]{2,1,0:T(8,128)S(1)} %bitcast.22), channel_id=1, source_target_pairs={{0,2},{2,4},{3,1},{4,6},{5,3},{6,8},{7,5},{8,10},{9,7},{10,12},{11... | collective-permute-start | bytes 49160 | tf_op jit(solution)/shard_map/ppermute | solution.py:504
  27.6 6.3 %collective-permute-done.3 = f32[2,16,128]{2,1,0:T(8,128)S(1)} collective-permute-done((f32[2,16,128]{2,1,0:T(8,128)S(1)}, f32[2,16,128]{2,1,0:T(8,128)S(1)}, u32[]{:S(2)}, u32[]{:S(2)}) %collective-permute-start.3) | collective-permute-done | bytes 16416 | tf_op jit(solution)/shard_map/ppermute | solution.py:504
  33.9 1.8 %all-gather.5 = f32[4,16,128]{2,1,0:T(8,128)S(1)} all-gather(f32[2,16,128]{2,1,0:T(8,128)S(1)} %collective-permute-done.3), channel_id=7, replica_groups={{0,1},{2,3},{4,5},{6,7},{8,9},{10,11},{12,13},{14,15},{16,17},{18,19},{..., dimensions={0}, use_global_device_ids=true | all-gather | bytes 49152 | tf_op jit(solution)/shard_map/all_gather | solution.py:500
  35.7 1.8 %all-gather.4 = f32[4,16,128]{2,1,0:T(8,128)S(1)} all-gather(f32[2,16,128]{2,1,0:T(8,128)S(1)} %collective-permute-done.2), channel_id=6, replica_groups={{0,1},{2,3},{4,5},{6,7},{8,9},{10,11},{12,13},{14,15},{16,17},{18,19},{..., dimensions={0}, use_global_device_ids=true | all-gather | bytes 49152 | tf_op jit(solution)/shard_map/all_gather | solution.py:500
  39.6 2.6 %collective-permute-start.4 = (f32[2,8,128]{2,1,0:T(8,128)S(1)}, f32[2,8,128]{2,1,0:T(8,128)S(1)}, u32[]{:S(2)}, u32[]{:S(2)}) collective-permute-start(f32[2,8,128]{2,1,0:T(8,128)S(1)} %bitcast.25), channel_id=1, source_target_pairs={{2,0},{4,2},{5,1},{6,4},{7,3},{8,6},{9,5},{10,8},{11,7},{12,10},{1... | collective-permute-start | bytes 24584 | tf_op jit(solution)/shard_map/ppermute | solution.py:504
  42.7 2.4 %collective-permute-done.4 = f32[2,8,128]{2,1,0:T(8,128)S(1)} collective-permute-done((f32[2,8,128]{2,1,0:T(8,128)S(1)}, f32[2,8,128]{2,1,0:T(8,128)S(1)}, u32[]{:S(2)}, u32[]{:S(2)}) %collective-permute-start.4) | collective-permute-done | bytes 8224 | tf_op jit(solution)/shard_map/ppermute | solution.py:504
  45.1 2.0 %all-gather.7 = f32[4,8,128]{2,1,0:T(8,128)S(1)} all-gather(f32[2,8,128]{2,1,0:T(8,128)S(1)} %collective-permute-done.4), channel_id=9, replica_groups={{0,1},{2,3},{4,5},{6,7},{8,9},{10,11},{12,13},{14,15},{16,17},{18,19},{..., dimensions={0}, use_global_device_ids=true | all-gather | bytes 24576 | tf_op jit(solution)/shard_map/all_gather | solution.py:500
  48.3 7.2 %all-to-all-start = ((f32[32,1,2176]{2,1,0:T(1,128)}), f32[32,1,2176]{2,1,0:T(1,128)S(1)}, u32[]{:S(2)}, u32[]{:S(2)}) async-start(f32[32,1,2176]{2,1,0:T(1,128)} %get-tuple-element.23), calls=%async_computation | async-start | bytes 557056 | tf_op jit(solution)/shard_map/all_to_all | solution.py:524
  55.6 2.2 %collective-permute-start.5 = (f32[8,1280]{1,0:T(8,128)S(1)}, f32[8,1280]{1,0:T(8,128)S(1)}, u32[]{:S(2)}, u32[]{:S(2)}) collective-permute-start(f32[8,1280]{1,0:T(8,128)S(1)} %get-tuple-element.24), channel_id=1, source_target_pairs={{0,1},{1,0},{2,3},{3,2},{4,5},{5,4},{6,7},{7,6},{8,9},{9,8},{10,11... | collective-permute-start | bytes 122888 | tf_op jit(solution)/shard_map/ppermute | solution.py:504
  57.8 6.9 %all-to-all-done.sums_ref = f32[32,1,2176]{2,1,0:T(1,128)S(1)} async-done(((f32[32,1,2176]{2,1,0:T(1,128)}), f32[32,1,2176]{2,1,0:T(1,128)S(1)}, u32[]{:S(2)}, u32[]{:S(2)}) %all-to-all-start) | async-done | bytes 278560 | tf_op jit(solution)/shard_map/all_to_all | solution.py:524
  65.4 16.5 %all-to-all-start.1 = ((f32[16,1,2176]{2,1,0:T(1,128)}), f32[16,1,2176]{2,1,0:T(1,128)S(1)}, u32[]{:S(2)}, u32[]{:S(2)}) async-start(f32[16,1,2176]{2,1,0:T(1,128)} %shard_map.54), calls=%async_computation.1 | async-start | bytes 278528 | tf_op jit(solution)/shard_map/all_to_all | solution.py:527
  81.8 3.0 %collective-permute-start.6 = (f32[8,1280]{1,0:T(8,128)S(1)}, f32[8,1280]{1,0:T(8,128)S(1)}, u32[]{:S(2)}, u32[]{:S(2)}) collective-permute-start(f32[8,1280]{1,0:T(8,128)S(1)} %get-tuple-element.29), channel_id=1, source_target_pairs={{1,2},{2,1},{3,4},{4,3},{5,6},{6,5},{7,8},{8,7},{9,10},{10,9},{11,... | collective-permute-start | bytes 122888 | tf_op jit(solution)/shard_map/ppermute | solution.py:504
  84.8 8.1 %shard_map.55 = (f32[256,1280]{1,0:T(8,128)S(1)}, f32[256,1024]{1,0:T(8,128)S(1)}, f32[24,1280]{1,0:T(8,128)S(1)}) custom-call(f32[256,1280]{1,0:T(8,128)S(1)} %get-tuple-element.30.final_ref, s16[256,1024]{1,0:T(8,128)(2,1)S(1)} %get-tuple-element.31.counts_ref, f32[8,1280]{1,0:T(8,128)S(1)} %get-tuple-element.32.vectors_ref), custom_call_target="tpu_custom_call", output_to_operand_aliasing={{0}: (0, {})} | custom-call | flops 20000000 | bytes 6291456 | tf_op jit(solution)/shard_map/pallas_call | solution.py:452
  93.3 3.0 %all-to-all-done.1.sums_ref = f32[16,1,2176]{2,1,0:T(1,128)S(1)} async-done(((f32[16,1,2176]{2,1,0:T(1,128)}), f32[16,1,2176]{2,1,0:T(1,128)S(1)}, u32[]{:S(2)}, u32[]{:S(2)}) %all-to-all-start.1) | async-done | bytes 139296 | tf_op jit(solution)/shard_map/all_to_all | solution.py:527
  96.3 3.8 %shard_map.57 = (f32[256,1024]{1,0:T(8,128)}, f32[256,1024]{1,0:T(8,128)}, f32[2,128]{1,0:T(2,128)}) custom-call(f32[16,1,2176]{2,1,0:T(1,128)S(1)} %all-to-all-done.1.sums_ref, f32[32,1024]{1,0:T(8,128)S(1)} %shard_map.56.edge_ref, f32[256,1280]{1,0:T(8,128)S(1)} %get-tuple-element.34.donut_ref, f32[256,1024]{1,0:T(8,128)S(1)} %get-tuple-element.35.lower_ref, ...), custom_call_target="tpu_custom_call" | custom-call | tf_op jit(solution)/shard_map/pallas_call | solution.py:481
  (15 shorter events, 7.6 us)
Async XLA Ops:
  0.6 1.2 %copy-start = (s32[256,1024]{1,0:T(8,128)S(1)}, s32[256,1024]{1,0:T(8,128)}, u32[]{:S(2)}) copy-start(s32[256,1024]{1,0:T(8,128)} %contacts_ref.1) | copy-start | bytes 3145732
  1.9 0.7 copy-start.1
  4.8 10.1 %collective-permute-start.1 = (f32[2,16,128]{2,1,0:T(8,128)S(1)}, f32[2,16,128]{2,1,0:T(8,128)S(1)}, u32[]{:S(2)}, u32[]{:S(2)}) collective-permute-start(f32[2,16,128]{2,1,0:T(8,128)S(1)} %bitcast.15), channel_id=1, source_target_pairs={{0,4},{2,6},{4,8},{5,1},{6,10},{7,3},{8,12},{9,5},{10,14},{11,7},{... | collective-permute-start | bytes 49160 | tf_op jit(solution)/shard_map/ppermute | solution.py:504
  9.9 9.9 %collective-permute-start = (f32[2,16,128]{2,1,0:T(8,128)S(1)}, f32[2,16,128]{2,1,0:T(8,128)S(1)}, u32[]{:S(2)}, u32[]{:S(2)}) collective-permute-start(f32[2,16,128]{2,1,0:T(8,128)S(1)} %bitcast.16), channel_id=1, source_target_pairs={{0,2},{2,4},{3,1},{4,6},{5,3},{6,8},{7,5},{8,10},{9,7},{10,12},{11... | collective-permute-start | bytes 49160 | tf_op jit(solution)/shard_map/ppermute | solution.py:504
  23.8 10.1 %collective-permute-start.3 = (f32[2,16,128]{2,1,0:T(8,128)S(1)}, f32[2,16,128]{2,1,0:T(8,128)S(1)}, u32[]{:S(2)}, u32[]{:S(2)}) collective-permute-start(f32[2,16,128]{2,1,0:T(8,128)S(1)} %bitcast.21), channel_id=1, source_target_pairs={{0,4},{2,6},{4,8},{5,1},{6,10},{7,3},{8,12},{9,5},{10,14},{11,7},{... | collective-permute-start | bytes 49160 | tf_op jit(solution)/shard_map/ppermute | solution.py:504
  25.7 10.0 %collective-permute-start.2 = (f32[2,16,128]{2,1,0:T(8,128)S(1)}, f32[2,16,128]{2,1,0:T(8,128)S(1)}, u32[]{:S(2)}, u32[]{:S(2)}) collective-permute-start(f32[2,16,128]{2,1,0:T(8,128)S(1)} %bitcast.22), channel_id=1, source_target_pairs={{0,2},{2,4},{3,1},{4,6},{5,3},{6,8},{7,5},{8,10},{9,7},{10,12},{11... | collective-permute-start | bytes 49160 | tf_op jit(solution)/shard_map/ppermute | solution.py:504
  39.6 5.5 %collective-permute-start.4 = (f32[2,8,128]{2,1,0:T(8,128)S(1)}, f32[2,8,128]{2,1,0:T(8,128)S(1)}, u32[]{:S(2)}, u32[]{:S(2)}) collective-permute-start(f32[2,8,128]{2,1,0:T(8,128)S(1)} %bitcast.25), channel_id=1, source_target_pairs={{2,0},{4,2},{5,1},{6,4},{7,3},{8,6},{9,5},{10,8},{11,7},{12,10},{1... | collective-permute-start | bytes 24584 | tf_op jit(solution)/shard_map/ppermute | solution.py:504
  48.3 16.3 %all-to-all-start = ((f32[32,1,2176]{2,1,0:T(1,128)}), f32[32,1,2176]{2,1,0:T(1,128)S(1)}, u32[]{:S(2)}, u32[]{:S(2)}) async-start(f32[32,1,2176]{2,1,0:T(1,128)} %get-tuple-element.23), calls=%async_computation | async-start | bytes 557056 | tf_op jit(solution)/shard_map/all_to_all | solution.py:524
  55.6 9.8 %collective-permute-start.5 = (f32[8,1280]{1,0:T(8,128)S(1)}, f32[8,1280]{1,0:T(8,128)S(1)}, u32[]{:S(2)}, u32[]{:S(2)}) collective-permute-start(f32[8,1280]{1,0:T(8,128)S(1)} %get-tuple-element.24), channel_id=1, source_target_pairs={{0,1},{1,0},{2,3},{3,2},{4,5},{5,4},{6,7},{7,6},{8,9},{9,8},{10,11... | collective-permute-start | bytes 122888 | tf_op jit(solution)/shard_map/ppermute | solution.py:504
  65.4 30.9 %all-to-all-start.1 = ((f32[16,1,2176]{2,1,0:T(1,128)}), f32[16,1,2176]{2,1,0:T(1,128)S(1)}, u32[]{:S(2)}, u32[]{:S(2)}) async-start(f32[16,1,2176]{2,1,0:T(1,128)} %shard_map.54), calls=%async_computation.1 | async-start | bytes 278528 | tf_op jit(solution)/shard_map/all_to_all | solution.py:527
  81.8 11.1 %collective-permute-start.6 = (f32[8,1280]{1,0:T(8,128)S(1)}, f32[8,1280]{1,0:T(8,128)S(1)}, u32[]{:S(2)}, u32[]{:S(2)}) collective-permute-start(f32[8,1280]{1,0:T(8,128)S(1)} %get-tuple-element.29), channel_id=1, source_target_pairs={{1,2},{2,1},{3,4},{4,3},{5,6},{6,5},{7,8},{8,7},{9,10},{10,9},{11,... | collective-permute-start | bytes 122888 | tf_op jit(solution)/shard_map/ppermute | solution.py:504

commit v9 on v8

--- a/solution.py
+++ b/solution.py
@@ -1,3 +1,5 @@
+import math
+
 import jax
 import jax.numpy as jnp
 from jax import lax
@@ -5,6 +7,8 @@
 from jax.experimental.pallas import tpu as pltpu
 from jax.sharding import PartitionSpec as P
 
+UNIT = math.log2(math.e) ** 0.5
+SPREAD = 3.0 / 2.0**0.5 * UNIT
 OUTER = 5
 INNER = 2
 ROWS = 256
@@ -245,7 +249,7 @@
     value = straight(value, start, tile)
     positive = value > 0.0
     root = jnp.exp(jnp.log(jnp.where(positive, value, 1.0) * (q * q)) * (1.0 / 3.0))
-    root = jnp.where(positive, root * (k * q * (3.0 / 2.0**0.5)), 0.0)
+    root = jnp.where(positive, root * (k * q * SPREAD), 0.0)
     distance = lax.broadcasted_iota(jnp.int32, (8, BAND), 1)
     return jnp.where((counts > 0) & (distance >= 2 * OUTER) & (value >= 0.0), root, MASKED)
 
@@ -310,14 +314,23 @@
     out_ref[24:25, :] = jnp.concatenate([vectors_ref[2:3, :ROWS], vectors_ref[0:1, : BAND - ROWS]], axis=1)
 
 
-def half_erfc(x):
-    size = jnp.abs(x)
-    t = 1.0 / (1.0 + 0.5 * size)
-    poly = 0.17087277
-    for c in (-0.82215223, 1.48851587, -1.13520398, 0.27886807, -0.18628806, 0.09678418, 0.37409196, 1.00002368, -1.26551223):
+ERFC_FIT = (
+    -1.26551223, 1.00002368, 0.37409196, 0.09678418, -0.18628806,
+    0.27886807, -1.13520398, 1.48851587, -0.82215223, 0.17087277,
+)
+ERFC_AT = 2.0 * UNIT
+ERFC_TERMS = [c * UNIT**2 * ERFC_AT**n for n, c in enumerate(ERFC_FIT)]
+ERFC_TERMS[0] += math.log2(0.5 * ERFC_AT)
+
+
+def half_erfc(y):
+    size = jnp.abs(y)
+    t = 1.0 / (ERFC_AT + size)
+    poly = ERFC_TERMS[-1]
+    for c in ERFC_TERMS[-2::-1]:
         poly = poly * t + c
-    tail = 0.5 * t * jnp.exp(poly - size * size)
-    return jnp.where(x >= 0.0, tail, 1.0 - tail)
+    tail = t * jnp.exp2(poly - y * y)
+    return jnp.where(y >= 0.0, tail, 1.0 - tail)
 
 
 def filter_sums(expected):
@@ -380,8 +393,8 @@
     step, rows = pl.program_id(0), pvalue_donut_ref.shape[0]
     for start in range(0, rows, STEP):
         here = slice(start, start + STEP)
-        k, q = inverse_root(counts_ref[here, :].astype(jnp.int32).astype(F32))
-        base = q * (k * (3.0 / 2.0**0.5) - 1.0 / (3.0 * 2.0**0.5))
+        k = counts_ref[here, :].astype(jnp.int32).astype(F32)
+        base = lax.rsqrt(k) * (k * SPREAD - SPREAD / 9.0)
         for at, root_ref, out_ref in ((0, donut_ref, pvalue_donut_ref), (1, lower_ref, pvalue_lower_ref)):
             root = root_ref[here, :]
             if start == 0 and at == 0:

time: 101 us -> 100 us (0.990)
  no operation moved by 1% of the time
where the time goes in v9:
time: 100 us; the launch traced here: 99.8 us
  starting transfers between devices  42.9 us (43%)
  waiting for transfers between devices  24 us (24%)
  Pallas kernels  15.5 us (16%)
  blocking collectives  14.7 us (15%)
  local copies, waits for them, and re-layouts  1.9 us (2%)
    ppermute x7, starting transfers between devices, moved(): lax.ppermute(value, 'genome', [(i, t) for i, t in pairs if 0 <= t < size])  19.2 us
    all_to_all x1, starting transfers between devices, shards(): sums = lax.all_to_all(sums, 'genome', 0, 0, axis_index_groups=lines)  16.5 us
    all_gather x8, blocking collectives, both_cores(): return lax.all_gather(value, 'genome', axis_index_groups=chips)  14.7 us
    ppermute x7, waiting for transfers between devices, moved(): lax.ppermute(value, 'genome', [(i, t) for i, t in pairs if 0 <= t < size])  14.2 us
    pallas_call x1, Pallas kernels, windows(): pl.pallas_call(window_kernel, out_shape=[jax.ShapeDtypeStruct(s, F32) for...  8.1 us
    all_to_all x1, starting transfers between devices, shards(): sums = lax.all_to_all(sums, 'genome', 0, 0, axis_index_groups=planes)  7.25 us
    all_to_all x1, waiting for transfers between devices, shards(): sums = lax.all_to_all(sums, 'genome', 0, 0, axis_index_groups=planes)  6.88 us
    pallas_call x1, Pallas kernels, tails(): pl.pallas_call(tail_kernel, grid=(ROWS // rows,), out_shape=[jax.ShapeDty...  3.54 us
  transfers between devices with their start and end apart: 9, of which 6 were waited for; matrix products, arithmetic and copies ran while one was open for 0% of the time, Pallas kernels for 10%

profile of v9, /device:TPU:32, one launch (start us, length us, event | category | flops | bytes accessed | tf_op | source)
XLA Modules:
  0.0 99.8 jit_solution(6013051771066180922)
XLA Ops:
  3.0 1.8 %all-gather = f32[32,128]{1,0:T(8,128)S(1)} all-gather(f32[16,128]{1,0:T(8,128)S(1)} %get-tuple-element.22), channel_id=2, replica_groups={{0,1},{2,3},{4,5},{6,7},{8,9},{10,11},{12,13},{14,15},{16,17},{18,19},{..., dimensions={0}, use_global_device_ids=true | all-gather | bytes 24576 | tf_op jit(solution)/shard_map/all_gather | solution.py:513
  4.8 5.1 %collective-permute-start.1 = (f32[2,16,128]{2,1,0:T(8,128)S(1)}, f32[2,16,128]{2,1,0:T(8,128)S(1)}, u32[]{:S(2)}, u32[]{:S(2)}) collective-permute-start(f32[2,16,128]{2,1,0:T(8,128)S(1)} %bitcast.15), channel_id=1, source_target_pairs={{0,4},{2,6},{4,8},{5,1},{6,10},{7,3},{8,12},{9,5},{10,14},{11,7},{... | collective-permute-start | bytes 49160 | tf_op jit(solution)/shard_map/ppermute | solution.py:517
  9.9 2.6 %collective-permute-start = (f32[2,16,128]{2,1,0:T(8,128)S(1)}, f32[2,16,128]{2,1,0:T(8,128)S(1)}, u32[]{:S(2)}, u32[]{:S(2)}) collective-permute-start(f32[2,16,128]{2,1,0:T(8,128)S(1)} %bitcast.16), channel_id=1, source_target_pairs={{0,2},{2,4},{3,1},{4,6},{5,3},{6,8},{7,5},{8,10},{9,7},{10,12},{11... | collective-permute-start | bytes 49160 | tf_op jit(solution)/shard_map/ppermute | solution.py:517
  12.5 2.4 %collective-permute-done.1 = f32[2,16,128]{2,1,0:T(8,128)S(1)} collective-permute-done((f32[2,16,128]{2,1,0:T(8,128)S(1)}, f32[2,16,128]{2,1,0:T(8,128)S(1)}, u32[]{:S(2)}, u32[]{:S(2)}) %collective-permute-start.1) | collective-permute-done | bytes 16416 | tf_op jit(solution)/shard_map/ppermute | solution.py:517
  15.0 1.8 %all-gather.2 = f32[4,16,128]{2,1,0:T(8,128)S(1)} all-gather(f32[2,16,128]{2,1,0:T(8,128)S(1)} %collective-permute-done.1), channel_id=4, replica_groups={{0,1},{2,3},{4,5},{6,7},{8,9},{10,11},{12,13},{14,15},{16,17},{18,19},{..., dimensions={0}, use_global_device_ids=true | all-gather | bytes 49152 | tf_op jit(solution)/shard_map/all_gather | solution.py:513
  16.8 3.0 %collective-permute-done = f32[2,16,128]{2,1,0:T(8,128)S(1)} collective-permute-done((f32[2,16,128]{2,1,0:T(8,128)S(1)}, f32[2,16,128]{2,1,0:T(8,128)S(1)}, u32[]{:S(2)}, u32[]{:S(2)}) %collective-permute-start) | collective-permute-done | bytes 16416 | tf_op jit(solution)/shard_map/ppermute | solution.py:517
  19.8 1.8 %all-gather.1 = f32[4,16,128]{2,1,0:T(8,128)S(1)} all-gather(f32[2,16,128]{2,1,0:T(8,128)S(1)} %collective-permute-done), channel_id=3, replica_groups={{0,1},{2,3},{4,5},{6,7},{8,9},{10,11},{12,13},{14,15},{16,17},{18,19},{..., dimensions={0}, use_global_device_ids=true | all-gather | bytes 49152 | tf_op jit(solution)/shard_map/all_gather | solution.py:513
  21.9 1.8 %all-gather.3 = f32[32,128]{1,0:T(8,128)S(1)} all-gather(f32[16,128]{1,0:T(8,128)S(1)} %shard_map.50), channel_id=5, replica_groups={{0,1},{2,3},{4,5},{6,7},{8,9},{10,11},{12,13},{14,15},{16,17},{18,19},{..., dimensions={0}, use_global_device_ids=true | all-gather | bytes 24576 | tf_op jit(solution)/shard_map/all_gather | solution.py:513
  23.8 1.9 %collective-permute-start.3 = (f32[2,16,128]{2,1,0:T(8,128)S(1)}, f32[2,16,128]{2,1,0:T(8,128)S(1)}, u32[]{:S(2)}, u32[]{:S(2)}) collective-permute-start(f32[2,16,128]{2,1,0:T(8,128)S(1)} %bitcast.21), channel_id=1, source_target_pairs={{0,4},{2,6},{4,8},{5,1},{6,10},{7,3},{8,12},{9,5},{10,14},{11,7},{... | collective-permute-start | bytes 49160 | tf_op jit(solution)/shard_map/ppermute | solution.py:517
  25.7 1.9 %collective-permute-start.2 = (f32[2,16,128]{2,1,0:T(8,128)S(1)}, f32[2,16,128]{2,1,0:T(8,128)S(1)}, u32[]{:S(2)}, u32[]{:S(2)}) collective-permute-start(f32[2,16,128]{2,1,0:T(8,128)S(1)} %bitcast.22), channel_id=1, source_target_pairs={{0,2},{2,4},{3,1},{4,6},{5,3},{6,8},{7,5},{8,10},{9,7},{10,12},{11... | collective-permute-start | bytes 49160 | tf_op jit(solution)/shard_map/ppermute | solution.py:517
  27.6 6.3 %collective-permute-done.3 = f32[2,16,128]{2,1,0:T(8,128)S(1)} collective-permute-done((f32[2,16,128]{2,1,0:T(8,128)S(1)}, f32[2,16,128]{2,1,0:T(8,128)S(1)}, u32[]{:S(2)}, u32[]{:S(2)}) %collective-permute-start.3) | collective-permute-done | bytes 16416 | tf_op jit(solution)/shard_map/ppermute | solution.py:517
  33.9 1.8 %all-gather.5 = f32[4,16,128]{2,1,0:T(8,128)S(1)} all-gather(f32[2,16,128]{2,1,0:T(8,128)S(1)} %collective-permute-done.3), channel_id=7, replica_groups={{0,1},{2,3},{4,5},{6,7},{8,9},{10,11},{12,13},{14,15},{16,17},{18,19},{..., dimensions={0}, use_global_device_ids=true | all-gather | bytes 49152 | tf_op jit(solution)/shard_map/all_gather | solution.py:513
  35.7 1.8 %all-gather.4 = f32[4,16,128]{2,1,0:T(8,128)S(1)} all-gather(f32[2,16,128]{2,1,0:T(8,128)S(1)} %collective-permute-done.2), channel_id=6, replica_groups={{0,1},{2,3},{4,5},{6,7},{8,9},{10,11},{12,13},{14,15},{16,17},{18,19},{..., dimensions={0}, use_global_device_ids=true | all-gather | bytes 49152 | tf_op jit(solution)/shard_map/all_gather | solution.py:513
  39.6 2.6 %collective-permute-start.4 = (f32[2,8,128]{2,1,0:T(8,128)S(1)}, f32[2,8,128]{2,1,0:T(8,128)S(1)}, u32[]{:S(2)}, u32[]{:S(2)}) collective-permute-start(f32[2,8,128]{2,1,0:T(8,128)S(1)} %bitcast.25), channel_id=1, source_target_pairs={{2,0},{4,2},{5,1},{6,4},{7,3},{8,6},{9,5},{10,8},{11,7},{12,10},{1... | collective-permute-start | bytes 24584 | tf_op jit(solution)/shard_map/ppermute | solution.py:517
  42.7 2.4 %collective-permute-done.4 = f32[2,8,128]{2,1,0:T(8,128)S(1)} collective-permute-done((f32[2,8,128]{2,1,0:T(8,128)S(1)}, f32[2,8,128]{2,1,0:T(8,128)S(1)}, u32[]{:S(2)}, u32[]{:S(2)}) %collective-permute-start.4) | collective-permute-done | bytes 8224 | tf_op jit(solution)/shard_map/ppermute | solution.py:517
  45.1 2.0 %all-gather.7 = f32[4,8,128]{2,1,0:T(8,128)S(1)} all-gather(f32[2,8,128]{2,1,0:T(8,128)S(1)} %collective-permute-done.4), channel_id=9, replica_groups={{0,1},{2,3},{4,5},{6,7},{8,9},{10,11},{12,13},{14,15},{16,17},{18,19},{..., dimensions={0}, use_global_device_ids=true | all-gather | bytes 24576 | tf_op jit(solution)/shard_map/all_gather | solution.py:513
  48.3 7.2 %all-to-all-start = ((f32[32,1,2176]{2,1,0:T(1,128)}), f32[32,1,2176]{2,1,0:T(1,128)S(1)}, u32[]{:S(2)}, u32[]{:S(2)}) async-start(f32[32,1,2176]{2,1,0:T(1,128)} %get-tuple-element.23), calls=%async_computation | async-start | bytes 557056 | tf_op jit(solution)/shard_map/all_to_all | solution.py:537
  55.6 2.2 %collective-permute-start.5 = (f32[8,1280]{1,0:T(8,128)S(1)}, f32[8,1280]{1,0:T(8,128)S(1)}, u32[]{:S(2)}, u32[]{:S(2)}) collective-permute-start(f32[8,1280]{1,0:T(8,128)S(1)} %get-tuple-element.24), channel_id=1, source_target_pairs={{0,1},{1,0},{2,3},{3,2},{4,5},{5,4},{6,7},{7,6},{8,9},{9,8},{10,11... | collective-permute-start | bytes 122888 | tf_op jit(solution)/shard_map/ppermute | solution.py:517
  57.8 6.9 %all-to-all-done.sums_ref = f32[32,1,2176]{2,1,0:T(1,128)S(1)} async-done(((f32[32,1,2176]{2,1,0:T(1,128)}), f32[32,1,2176]{2,1,0:T(1,128)S(1)}, u32[]{:S(2)}, u32[]{:S(2)}) %all-to-all-start) | async-done | bytes 278560 | tf_op jit(solution)/shard_map/all_to_all | solution.py:537
  65.4 16.5 %all-to-all-start.1 = ((f32[16,1,2176]{2,1,0:T(1,128)}), f32[16,1,2176]{2,1,0:T(1,128)S(1)}, u32[]{:S(2)}, u32[]{:S(2)}) async-start(f32[16,1,2176]{2,1,0:T(1,128)} %shard_map.54), calls=%async_computation.1 | async-start | bytes 278528 | tf_op jit(solution)/shard_map/all_to_all | solution.py:540
  81.8 3.0 %collective-permute-start.6 = (f32[8,1280]{1,0:T(8,128)S(1)}, f32[8,1280]{1,0:T(8,128)S(1)}, u32[]{:S(2)}, u32[]{:S(2)}) collective-permute-start(f32[8,1280]{1,0:T(8,128)S(1)} %get-tuple-element.29), channel_id=1, source_target_pairs={{1,2},{2,1},{3,4},{4,3},{5,6},{6,5},{7,8},{8,7},{9,10},{10,9},{11,... | collective-permute-start | bytes 122888 | tf_op jit(solution)/shard_map/ppermute | solution.py:517
  84.8 8.1 %shard_map.55 = (f32[256,1280]{1,0:T(8,128)S(1)}, f32[256,1024]{1,0:T(8,128)S(1)}, f32[24,1280]{1,0:T(8,128)S(1)}) custom-call(f32[256,1280]{1,0:T(8,128)S(1)} %get-tuple-element.30.final_ref, s16[256,1024]{1,0:T(8,128)(2,1)S(1)} %get-tuple-element.31.counts_ref, f32[8,1280]{1,0:T(8,128)S(1)} %get-tuple-element.32.vectors_ref), custom_call_target="tpu_custom_call", output_to_operand_aliasing={{0}: (0, {})} | custom-call | flops 20000000 | bytes 6291456 | tf_op jit(solution)/shard_map/pallas_call | solution.py:465
  93.3 3.0 %all-to-all-done.1.sums_ref = f32[16,1,2176]{2,1,0:T(1,128)S(1)} async-done(((f32[16,1,2176]{2,1,0:T(1,128)}), f32[16,1,2176]{2,1,0:T(1,128)S(1)}, u32[]{:S(2)}, u32[]{:S(2)}) %all-to-all-start.1) | async-done | bytes 139296 | tf_op jit(solution)/shard_map/all_to_all | solution.py:540
  96.3 3.5 %shard_map.57 = (f32[256,1024]{1,0:T(8,128)}, f32[256,1024]{1,0:T(8,128)}, f32[2,128]{1,0:T(2,128)}) custom-call(f32[16,1,2176]{2,1,0:T(1,128)S(1)} %all-to-all-done.1.sums_ref, f32[32,1024]{1,0:T(8,128)S(1)} %shard_map.56.edge_ref, f32[256,1280]{1,0:T(8,128)S(1)} %get-tuple-element.34.donut_ref, f32[256,1024]{1,0:T(8,128)S(1)} %get-tuple-element.35.lower_ref, ...), custom_call_target="tpu_custom_call" | custom-call | tf_op jit(solution)/shard_map/pallas_call | solution.py:494
  (15 shorter events, 7.6 us)
Async XLA Ops:
  0.6 1.2 %copy-start = (s32[256,1024]{1,0:T(8,128)S(1)}, s32[256,1024]{1,0:T(8,128)}, u32[]{:S(2)}) copy-start(s32[256,1024]{1,0:T(8,128)} %contacts_ref.1) | copy-start | bytes 3145732
  1.9 0.7 copy-start.1
  4.8 10.1 %collective-permute-start.1 = (f32[2,16,128]{2,1,0:T(8,128)S(1)}, f32[2,16,128]{2,1,0:T(8,128)S(1)}, u32[]{:S(2)}, u32[]{:S(2)}) collective-permute-start(f32[2,16,128]{2,1,0:T(8,128)S(1)} %bitcast.15), channel_id=1, source_target_pairs={{0,4},{2,6},{4,8},{5,1},{6,10},{7,3},{8,12},{9,5},{10,14},{11,7},{... | collective-permute-start | bytes 49160 | tf_op jit(solution)/shard_map/ppermute | solution.py:517
  9.9 9.9 %collective-permute-start = (f32[2,16,128]{2,1,0:T(8,128)S(1)}, f32[2,16,128]{2,1,0:T(8,128)S(1)}, u32[]{:S(2)}, u32[]{:S(2)}) collective-permute-start(f32[2,16,128]{2,1,0:T(8,128)S(1)} %bitcast.16), channel_id=1, source_target_pairs={{0,2},{2,4},{3,1},{4,6},{5,3},{6,8},{7,5},{8,10},{9,7},{10,12},{11... | collective-permute-start | bytes 49160 | tf_op jit(solution)/shard_map/ppermute | solution.py:517
  23.8 10.1 %collective-permute-start.3 = (f32[2,16,128]{2,1,0:T(8,128)S(1)}, f32[2,16,128]{2,1,0:T(8,128)S(1)}, u32[]{:S(2)}, u32[]{:S(2)}) collective-permute-start(f32[2,16,128]{2,1,0:T(8,128)S(1)} %bitcast.21), channel_id=1, source_target_pairs={{0,4},{2,6},{4,8},{5,1},{6,10},{7,3},{8,12},{9,5},{10,14},{11,7},{... | collective-permute-start | bytes 49160 | tf_op jit(solution)/shard_map/ppermute | solution.py:517
  25.7 10.0 %collective-permute-start.2 = (f32[2,16,128]{2,1,0:T(8,128)S(1)}, f32[2,16,128]{2,1,0:T(8,128)S(1)}, u32[]{:S(2)}, u32[]{:S(2)}) collective-permute-start(f32[2,16,128]{2,1,0:T(8,128)S(1)} %bitcast.22), channel_id=1, source_target_pairs={{0,2},{2,4},{3,1},{4,6},{5,3},{6,8},{7,5},{8,10},{9,7},{10,12},{11... | collective-permute-start | bytes 49160 | tf_op jit(solution)/shard_map/ppermute | solution.py:517
  39.6 5.5 %collective-permute-start.4 = (f32[2,8,128]{2,1,0:T(8,128)S(1)}, f32[2,8,128]{2,1,0:T(8,128)S(1)}, u32[]{:S(2)}, u32[]{:S(2)}) collective-permute-start(f32[2,8,128]{2,1,0:T(8,128)S(1)} %bitcast.25), channel_id=1, source_target_pairs={{2,0},{4,2},{5,1},{6,4},{7,3},{8,6},{9,5},{10,8},{11,7},{12,10},{1... | collective-permute-start | bytes 24584 | tf_op jit(solution)/shard_map/ppermute | solution.py:517
  48.3 16.3 %all-to-all-start = ((f32[32,1,2176]{2,1,0:T(1,128)}), f32[32,1,2176]{2,1,0:T(1,128)S(1)}, u32[]{:S(2)}, u32[]{:S(2)}) async-start(f32[32,1,2176]{2,1,0:T(1,128)} %get-tuple-element.23), calls=%async_computation | async-start | bytes 557056 | tf_op jit(solution)/shard_map/all_to_all | solution.py:537
  55.6 9.8 %collective-permute-start.5 = (f32[8,1280]{1,0:T(8,128)S(1)}, f32[8,1280]{1,0:T(8,128)S(1)}, u32[]{:S(2)}, u32[]{:S(2)}) collective-permute-start(f32[8,1280]{1,0:T(8,128)S(1)} %get-tuple-element.24), channel_id=1, source_target_pairs={{0,1},{1,0},{2,3},{3,2},{4,5},{5,4},{6,7},{7,6},{8,9},{9,8},{10,11... | collective-permute-start | bytes 122888 | tf_op jit(solution)/shard_map/ppermute | solution.py:517
  65.4 30.9 %all-to-all-start.1 = ((f32[16,1,2176]{2,1,0:T(1,128)}), f32[16,1,2176]{2,1,0:T(1,128)S(1)}, u32[]{:S(2)}, u32[]{:S(2)}) async-start(f32[16,1,2176]{2,1,0:T(1,128)} %shard_map.54), calls=%async_computation.1 | async-start | bytes 278528 | tf_op jit(solution)/shard_map/all_to_all | solution.py:540
  81.8 11.1 %collective-permute-start.6 = (f32[8,1280]{1,0:T(8,128)S(1)}, f32[8,1280]{1,0:T(8,128)S(1)}, u32[]{:S(2)}, u32[]{:S(2)}) collective-permute-start(f32[8,1280]{1,0:T(8,128)S(1)} %get-tuple-element.29), channel_id=1, source_target_pairs={{1,2},{2,1},{3,4},{4,3},{5,6},{6,5},{7,8},{8,7},{9,10},{10,9},{11,... | collective-permute-start | bytes 122888 | tf_op jit(solution)/shard_map/ppermute | solution.py:517

commit v10 on v9

--- a/solution.py
+++ b/solution.py
@@ -17,6 +17,7 @@
 SLAB = ROWS // LANE
 HOPS = BAND // ROWS
 SPAN = ROWS + BAND
+HALF = BAND + LANE
 WIDE = SPAN + LANE
 STEP = 32
 EDGE = 8
@@ -198,9 +199,9 @@
     cross_ref[...] = jnp.where(core == 0, first, last)
     diagonals = along_diagonals(final_ref, BAND)
     own = own_ref[...]
-    row = jnp.concatenate([diagonals, pairs_ref[...], own[4:5, : LANE // 2], own[5:6, : LANE // 2]], axis=1)
+    row = jnp.concatenate([diagonals, pairs_ref[...], own[4:5], own[5:6]], axis=1)
     for n in range(sums_ref.shape[0]):
-        sums_ref[n] = row
+        sums_ref[n] = row[:, :HALF] if n % 2 == 0 else row[:, HALF:]
     vectors_ref[0:1, :] = ahead
     vectors_ref[1:2, :] = jnp.where(ahead > 0, 1.0 / jnp.where(ahead > 0, ahead, 1.0), 0.0)
     vectors_ref[2:3, :] = jnp.concatenate([lanes(own[SLAB : 2 * SLAB]), jnp.zeros((1, SPAN - ROWS), F32)], axis=1)
@@ -375,18 +376,15 @@
                 ratio_ref):
     @pl.when(pl.program_id(0) == 0)
     def _():
-        total = sums_ref[0]
-        for n in range(1, sums_ref.shape[0]):
-            total = total + sums_ref[n]
+        total = jnp.concatenate([sum(sums_ref[core, n] for n in range(sums_ref.shape[1])) for core in range(2)], axis=1)
         pairs = tiled(total[:, BAND : 2 * BAND])
         expected = tiled(total[:, :BAND]) / pairs
         donut_exp, lower_exp = filter_sums(expected)
         ratio_ref[0:1, :] = lanes(cube_root(expected / donut_exp))
         ratio_ref[1:2, :] = lanes(cube_root(expected / lower_exp))
         mapped_count = pairs[0:1, 0:1]
-        half = LANE // 2
         first = total[:, 2 * BAND : 2 * BAND + 1] / mapped_count
-        second = total[:, 2 * BAND + half : 2 * BAND + half + 1] / mapped_count
+        second = total[:, 2 * BAND + LANE : 2 * BAND + LANE + 1] / mapped_count
         own = edge_ref[24:25, :]
         put_lanes(bias_ref, 0, jnp.where(own[:, ROWS : 2 * ROWS] > 0, own[:, :ROWS] / first / second, 1.0))
 
@@ -456,7 +454,7 @@
     return call(
         band_kernel,
         (core, skewed, pair, ahead, own, pairs),
-        [(ROWS, SPAN), (EDGE, SPAN), (EDGE, SPAN), (copies, 1, 2 * BAND + LANE), (8, SPAN)],
+        [(ROWS, SPAN), (EDGE, SPAN), (EDGE, SPAN), (copies, 1, HALF), (8, SPAN)],
         [SMEM] + [VMEM] * 5,
     )
 
@@ -541,7 +539,7 @@
         cross = moved(cross, lambda i: i - 1 if i % 2 == 0 else i + 1)
         donut, lower, partial = windows(final, counts, vectors)
         edge = edges(core, swap, cross, partial, counts, vectors)
-        pvalue_donut, pvalue_lower, bias = tails(sums, edge, donut, lower, counts)
+        pvalue_donut, pvalue_lower, bias = tails(both_cores(sums), edge, donut, lower, counts)
         return pvalue_donut, pvalue_lower, bias.reshape(ROWS)
 
     placed = (P("genome", None), P("genome"))

time: 100 us -> 101 us (1.010)
  the two profiles are of different devices: /device:TPU:32 before, /device:TPU:1 now
where the time goes in v10:
time: 101 us; the launch traced here: 100 us
  starting transfers between devices  40 us (40%)
  blocking collectives  24.6 us (24%)
  waiting for transfers between devices  17.7 us (18%)
  Pallas kernels  15.4 us (15%)
  local copies, waits for them, and re-layouts  1.9 us (2%)
    all_gather x9, blocking collectives, both_cores(): return lax.all_gather(value, 'genome', axis_index_groups=chips)  24.6 us
    all_to_all x1, starting transfers between devices, shards(): sums = lax.all_to_all(sums, 'genome', 0, 0, axis_index_groups=lines)  16.2 us
    all_to_all x1, starting transfers between devices, shards(): sums = lax.all_to_all(sums, 'genome', 0, 0, axis_index_groups=planes)  12.5 us
    ppermute x7, waiting for transfers between devices, moved(): lax.ppermute(value, 'genome', [(i, t) for i, t in pairs if 0 <= t < size])  11.5 us
    ppermute x7, starting transfers between devices, moved(): lax.ppermute(value, 'genome', [(i, t) for i, t in pairs if 0 <= t < size])  11.3 us
    pallas_call x1, Pallas kernels, windows(): pl.pallas_call(window_kernel, out_shape=[jax.ShapeDtypeStruct(s, F32) for...  8.1 us
    all_to_all x1, waiting for transfers between devices, shards(): sums = lax.all_to_all(sums, 'genome', 0, 0, axis_index_groups=planes)  5.68 us
    pallas_call x1, Pallas kernels, tails(): pl.pallas_call(tail_kernel, grid=(ROWS // rows,), out_shape=[jax.ShapeDty...  3.54 us
  transfers between devices with their start and end apart: 9, of which 5 were waited for; matrix products, arithmetic and copies ran while one was open for 0% of the time, Pallas kernels for 10%

profile of v10, /device:TPU:1, one launch (start us, length us, event | category | flops | bytes accessed | tf_op | source)
XLA Modules:
  0.0 100.3 jit_solution(7821137243964563758)
XLA Ops:
  3.0 8.4 %all-gather = f32[32,128]{1,0:T(8,128)S(1)} all-gather(f32[16,128]{1,0:T(8,128)S(1)} %get-tuple-element.22), channel_id=2, replica_groups={{0,1},{2,3},{4,5},{6,7},{8,9},{10,11},{12,13},{14,15},{16,17},{18,19},{..., dimensions={0}, use_global_device_ids=true | all-gather | bytes 24576 | tf_op jit(solution)/shard_map/all_gather | solution.py:511
  11.4 1.3 %collective-permute-start.1 = (f32[2,16,128]{2,1,0:T(8,128)S(1)}, f32[2,16,128]{2,1,0:T(8,128)S(1)}, u32[]{:S(2)}, u32[]{:S(2)}) collective-permute-start(f32[2,16,128]{2,1,0:T(8,128)S(1)} %bitcast.17), channel_id=1, source_target_pairs={{0,4},{2,6},{4,8},{5,1},{6,10},{7,3},{8,12},{9,5},{10,14},{11,7},{... | collective-permute-start | bytes 49160 | tf_op jit(solution)/shard_map/ppermute | solution.py:515
  12.7 1.3 %collective-permute-start = (f32[2,16,128]{2,1,0:T(8,128)S(1)}, f32[2,16,128]{2,1,0:T(8,128)S(1)}, u32[]{:S(2)}, u32[]{:S(2)}) collective-permute-start(f32[2,16,128]{2,1,0:T(8,128)S(1)} %bitcast.18), channel_id=1, source_target_pairs={{0,2},{2,4},{3,1},{4,6},{5,3},{6,8},{7,5},{8,10},{9,7},{10,12},{11... | collective-permute-start | bytes 49160 | tf_op jit(solution)/shard_map/ppermute | solution.py:515
  14.0 3.4 %collective-permute-done.1 = f32[2,16,128]{2,1,0:T(8,128)S(1)} collective-permute-done((f32[2,16,128]{2,1,0:T(8,128)S(1)}, f32[2,16,128]{2,1,0:T(8,128)S(1)}, u32[]{:S(2)}, u32[]{:S(2)}) %collective-permute-start.1) | collective-permute-done | bytes 16416 | tf_op jit(solution)/shard_map/ppermute | solution.py:515
  17.4 1.8 %all-gather.2 = f32[4,16,128]{2,1,0:T(8,128)S(1)} all-gather(f32[2,16,128]{2,1,0:T(8,128)S(1)} %collective-permute-done.1), channel_id=4, replica_groups={{0,1},{2,3},{4,5},{6,7},{8,9},{10,11},{12,13},{14,15},{16,17},{18,19},{..., dimensions={0}, use_global_device_ids=true | all-gather | bytes 49152 | tf_op jit(solution)/shard_map/all_gather | solution.py:511
  19.2 1.8 %all-gather.1 = f32[4,16,128]{2,1,0:T(8,128)S(1)} all-gather(f32[2,16,128]{2,1,0:T(8,128)S(1)} %collective-permute-done), channel_id=3, replica_groups={{0,1},{2,3},{4,5},{6,7},{8,9},{10,11},{12,13},{14,15},{16,17},{18,19},{..., dimensions={0}, use_global_device_ids=true | all-gather | bytes 49152 | tf_op jit(solution)/shard_map/all_gather | solution.py:511
  21.3 1.8 %all-gather.3 = f32[32,128]{1,0:T(8,128)S(1)} all-gather(f32[16,128]{1,0:T(8,128)S(1)} %shard_map.50), channel_id=5, replica_groups={{0,1},{2,3},{4,5},{6,7},{8,9},{10,11},{12,13},{14,15},{16,17},{18,19},{..., dimensions={0}, use_global_device_ids=true | all-gather | bytes 24576 | tf_op jit(solution)/shard_map/all_gather | solution.py:511
  23.2 1.3 %collective-permute-start.3 = (f32[2,16,128]{2,1,0:T(8,128)S(1)}, f32[2,16,128]{2,1,0:T(8,128)S(1)}, u32[]{:S(2)}, u32[]{:S(2)}) collective-permute-start(f32[2,16,128]{2,1,0:T(8,128)S(1)} %bitcast.23), channel_id=1, source_target_pairs={{0,4},{2,6},{4,8},{5,1},{6,10},{7,3},{8,12},{9,5},{10,14},{11,7},{... | collective-permute-start | bytes 49160 | tf_op jit(solution)/shard_map/ppermute | solution.py:515
  24.4 1.3 %collective-permute-start.2 = (f32[2,16,128]{2,1,0:T(8,128)S(1)}, f32[2,16,128]{2,1,0:T(8,128)S(1)}, u32[]{:S(2)}, u32[]{:S(2)}) collective-permute-start(f32[2,16,128]{2,1,0:T(8,128)S(1)} %bitcast.24), channel_id=1, source_target_pairs={{0,2},{2,4},{3,1},{4,6},{5,3},{6,8},{7,5},{8,10},{9,7},{10,12},{11... | collective-permute-start | bytes 49160 | tf_op jit(solution)/shard_map/ppermute | solution.py:515
  25.7 3.4 %collective-permute-done.3 = f32[2,16,128]{2,1,0:T(8,128)S(1)} collective-permute-done((f32[2,16,128]{2,1,0:T(8,128)S(1)}, f32[2,16,128]{2,1,0:T(8,128)S(1)}, u32[]{:S(2)}, u32[]{:S(2)}) %collective-permute-start.3) | collective-permute-done | bytes 16416 | tf_op jit(solution)/shard_map/ppermute | solution.py:515
  29.1 1.8 %all-gather.5 = f32[4,16,128]{2,1,0:T(8,128)S(1)} all-gather(f32[2,16,128]{2,1,0:T(8,128)S(1)} %collective-permute-done.3), channel_id=7, replica_groups={{0,1},{2,3},{4,5},{6,7},{8,9},{10,11},{12,13},{14,15},{16,17},{18,19},{..., dimensions={0}, use_global_device_ids=true | all-gather | bytes 49152 | tf_op jit(solution)/shard_map/all_gather | solution.py:511
  31.0 1.8 %all-gather.4 = f32[4,16,128]{2,1,0:T(8,128)S(1)} all-gather(f32[2,16,128]{2,1,0:T(8,128)S(1)} %collective-permute-done.2), channel_id=6, replica_groups={{0,1},{2,3},{4,5},{6,7},{8,9},{10,11},{12,13},{14,15},{16,17},{18,19},{..., dimensions={0}, use_global_device_ids=true | all-gather | bytes 49152 | tf_op jit(solution)/shard_map/all_gather | solution.py:511
  33.0 1.8 %all-gather.6 = f32[16,128]{1,0:T(8,128)S(1)} all-gather(f32[8,128]{1,0:T(8,128)S(1)} %shard_map.51.own_ref), channel_id=8, replica_groups={{0,1},{2,3},{4,5},{6,7},{8,9},{10,11},{12,13},{14,15},{16,17},{18,19},{..., dimensions={0}, use_global_device_ids=true | all-gather | bytes 12288 | tf_op jit(solution)/shard_map/all_gather | solution.py:511
  34.8 1.3 %collective-permute-start.4 = (f32[2,8,128]{2,1,0:T(8,128)S(1)}, f32[2,8,128]{2,1,0:T(8,128)S(1)}, u32[]{:S(2)}, u32[]{:S(2)}) collective-permute-start(f32[2,8,128]{2,1,0:T(8,128)S(1)} %bitcast.27), channel_id=1, source_target_pairs={{2,0},{4,2},{5,1},{6,4},{7,3},{8,6},{9,5},{10,8},{11,7},{12,10},{1... | collective-permute-start | bytes 24584 | tf_op jit(solution)/shard_map/ppermute | solution.py:515
  36.6 4.7 %collective-permute-done.4 = f32[2,8,128]{2,1,0:T(8,128)S(1)} collective-permute-done((f32[2,8,128]{2,1,0:T(8,128)S(1)}, f32[2,8,128]{2,1,0:T(8,128)S(1)}, u32[]{:S(2)}, u32[]{:S(2)}) %collective-permute-start.4) | collective-permute-done | bytes 8224 | tf_op jit(solution)/shard_map/ppermute | solution.py:515
  41.3 1.8 %all-gather.7 = f32[4,8,128]{2,1,0:T(8,128)S(1)} all-gather(f32[2,8,128]{2,1,0:T(8,128)S(1)} %collective-permute-done.4), channel_id=9, replica_groups={{0,1},{2,3},{4,5},{6,7},{8,9},{10,11},{12,13},{14,15},{16,17},{18,19},{..., dimensions={0}, use_global_device_ids=true | all-gather | bytes 24576 | tf_op jit(solution)/shard_map/all_gather | solution.py:511
  44.3 12.5 %all-to-all-start = ((f32[32,1,1152]{2,1,0:T(1,128)}), f32[32,1,1152]{2,1,0:T(1,128)S(1)}, u32[]{:S(2)}, u32[]{:S(2)}) async-start(f32[32,1,1152]{2,1,0:T(1,128)} %get-tuple-element.23), calls=%async_computation | async-start | bytes 294912 | tf_op jit(solution)/shard_map/all_to_all | solution.py:535
  56.8 2.1 %collective-permute-start.5 = (f32[8,1280]{1,0:T(8,128)S(1)}, f32[8,1280]{1,0:T(8,128)S(1)}, u32[]{:S(2)}, u32[]{:S(2)}) collective-permute-start(f32[8,1280]{1,0:T(8,128)S(1)} %get-tuple-element.24), channel_id=1, source_target_pairs={{0,1},{1,0},{2,3},{3,2},{4,5},{5,4},{6,7},{7,6},{8,9},{9,8},{10,11... | collective-permute-start | bytes 122888 | tf_op jit(solution)/shard_map/ppermute | solution.py:515
  59.0 5.7 %all-to-all-done.sums_ref = f32[32,1,1152]{2,1,0:T(1,128)S(1)} async-done(((f32[32,1,1152]{2,1,0:T(1,128)}), f32[32,1,1152]{2,1,0:T(1,128)S(1)}, u32[]{:S(2)}, u32[]{:S(2)}) %all-to-all-start) | async-done | bytes 147488 | tf_op jit(solution)/shard_map/all_to_all | solution.py:535
  65.3 16.2 %all-to-all-start.1 = ((f32[16,1,1152]{2,1,0:T(1,128)}), f32[16,1,1152]{2,1,0:T(1,128)S(1)}, u32[]{:S(2)}, u32[]{:S(2)}) async-start(f32[16,1,1152]{2,1,0:T(1,128)} %shard_map.54), calls=%async_computation.1 | async-start | bytes 147456 | tf_op jit(solution)/shard_map/all_to_all | solution.py:538
  81.5 2.7 %collective-permute-start.6 = (f32[8,1280]{1,0:T(8,128)S(1)}, f32[8,1280]{1,0:T(8,128)S(1)}, u32[]{:S(2)}, u32[]{:S(2)}) collective-permute-start(f32[8,1280]{1,0:T(8,128)S(1)} %get-tuple-element.29), channel_id=1, source_target_pairs={{1,2},{2,1},{3,4},{4,3},{5,6},{6,5},{7,8},{8,7},{9,10},{10,9},{11,... | collective-permute-start | bytes 122888 | tf_op jit(solution)/shard_map/ppermute | solution.py:515
  84.2 8.1 %shard_map.55 = (f32[256,1280]{1,0:T(8,128)S(1)}, f32[256,1024]{1,0:T(8,128)S(1)}, f32[24,1280]{1,0:T(8,128)S(1)}) custom-call(f32[256,1280]{1,0:T(8,128)S(1)} %get-tuple-element.30.final_ref, s16[256,1024]{1,0:T(8,128)(2,1)S(1)} %get-tuple-element.31.counts_ref, f32[8,1280]{1,0:T(8,128)S(1)} %get-tuple-element.32.vectors_ref), custom_call_target="tpu_custom_call", output_to_operand_aliasing={{0}: (0, {})} | custom-call | flops 20000000 | bytes 6291456 | tf_op jit(solution)/shard_map/pallas_call | solution.py:463
  93.2 3.6 %all-gather.8 = f32[32,1,1152]{2,1,0:T(1,128)S(1)} all-gather(f32[16,1,1152]{2,1,0:T(1,128)S(1)} %all-to-all-done.1), channel_id=10, replica_groups={{0,1},{2,3},{4,5},{6,7},{8,9},{10,11},{12,13},{14,15},{16,17},{18,19},{..., dimensions={0}, use_global_device_ids=true | all-gather | bytes 221184 | tf_op jit(solution)/shard_map/all_gather | solution.py:511
  96.8 3.5 %shard_map.57 = (f32[256,1024]{1,0:T(8,128)}, f32[256,1024]{1,0:T(8,128)}, f32[2,128]{1,0:T(2,128)}) custom-call(f32[2,16,1,1152]{3,2,1,0:T(1,128)S(1)} %bitcast.12, f32[32,1024]{1,0:T(8,128)S(1)} %shard_map.56.edge_ref, f32[256,1280]{1,0:T(8,128)S(1)} %get-tuple-element.34.donut_ref, f32[256,1024]{1,0:T(8,128)S(1)} %get-tuple-element.35.lower_ref, ...), custom_call_target="tpu_custom_call" | custom-call | tf_op jit(solution)/shard_map/pallas_call | solution.py:492
  (16 shorter events, 6.2 us)
Async XLA Ops:
  0.6 1.2 %copy-start = (s32[256,1024]{1,0:T(8,128)S(1)}, s32[256,1024]{1,0:T(8,128)}, u32[]{:S(2)}) copy-start(s32[256,1024]{1,0:T(8,128)} %contacts_ref.1) | copy-start | bytes 3145732
  1.9 0.7 copy-start.1
  11.4 6.0 %collective-permute-start.1 = (f32[2,16,128]{2,1,0:T(8,128)S(1)}, f32[2,16,128]{2,1,0:T(8,128)S(1)}, u32[]{:S(2)}, u32[]{:S(2)}) collective-permute-start(f32[2,16,128]{2,1,0:T(8,128)S(1)} %bitcast.17), channel_id=1, source_target_pairs={{0,4},{2,6},{4,8},{5,1},{6,10},{7,3},{8,12},{9,5},{10,14},{11,7},{... | collective-permute-start | bytes 49160 | tf_op jit(solution)/shard_map/ppermute | solution.py:515
  12.7 6.5 %collective-permute-start = (f32[2,16,128]{2,1,0:T(8,128)S(1)}, f32[2,16,128]{2,1,0:T(8,128)S(1)}, u32[]{:S(2)}, u32[]{:S(2)}) collective-permute-start(f32[2,16,128]{2,1,0:T(8,128)S(1)} %bitcast.18), channel_id=1, source_target_pairs={{0,2},{2,4},{3,1},{4,6},{5,3},{6,8},{7,5},{8,10},{9,7},{10,12},{11... | collective-permute-start | bytes 49160 | tf_op jit(solution)/shard_map/ppermute | solution.py:515
  23.2 6.0 %collective-permute-start.3 = (f32[2,16,128]{2,1,0:T(8,128)S(1)}, f32[2,16,128]{2,1,0:T(8,128)S(1)}, u32[]{:S(2)}, u32[]{:S(2)}) collective-permute-start(f32[2,16,128]{2,1,0:T(8,128)S(1)} %bitcast.23), channel_id=1, source_target_pairs={{0,4},{2,6},{4,8},{5,1},{6,10},{7,3},{8,12},{9,5},{10,14},{11,7},{... | collective-permute-start | bytes 49160 | tf_op jit(solution)/shard_map/ppermute | solution.py:515
  24.4 6.5 %collective-permute-start.2 = (f32[2,16,128]{2,1,0:T(8,128)S(1)}, f32[2,16,128]{2,1,0:T(8,128)S(1)}, u32[]{:S(2)}, u32[]{:S(2)}) collective-permute-start(f32[2,16,128]{2,1,0:T(8,128)S(1)} %bitcast.24), channel_id=1, source_target_pairs={{0,2},{2,4},{3,1},{4,6},{5,3},{6,8},{7,5},{8,10},{9,7},{10,12},{11... | collective-permute-start | bytes 49160 | tf_op jit(solution)/shard_map/ppermute | solution.py:515
  34.8 6.5 %collective-permute-start.4 = (f32[2,8,128]{2,1,0:T(8,128)S(1)}, f32[2,8,128]{2,1,0:T(8,128)S(1)}, u32[]{:S(2)}, u32[]{:S(2)}) collective-permute-start(f32[2,8,128]{2,1,0:T(8,128)S(1)} %bitcast.27), channel_id=1, source_target_pairs={{2,0},{4,2},{5,1},{6,4},{7,3},{8,6},{9,5},{10,8},{11,7},{12,10},{1... | collective-permute-start | bytes 24584 | tf_op jit(solution)/shard_map/ppermute | solution.py:515
  44.3 20.4 %all-to-all-start = ((f32[32,1,1152]{2,1,0:T(1,128)}), f32[32,1,1152]{2,1,0:T(1,128)S(1)}, u32[]{:S(2)}, u32[]{:S(2)}) async-start(f32[32,1,1152]{2,1,0:T(1,128)} %get-tuple-element.23), calls=%async_computation | async-start | bytes 294912 | tf_op jit(solution)/shard_map/all_to_all | solution.py:535
  56.8 8.5 %collective-permute-start.5 = (f32[8,1280]{1,0:T(8,128)S(1)}, f32[8,1280]{1,0:T(8,128)S(1)}, u32[]{:S(2)}, u32[]{:S(2)}) collective-permute-start(f32[8,1280]{1,0:T(8,128)S(1)} %get-tuple-element.24), channel_id=1, source_target_pairs={{0,1},{1,0},{2,3},{3,2},{4,5},{5,4},{6,7},{7,6},{8,9},{9,8},{10,11... | collective-permute-start | bytes 122888 | tf_op jit(solution)/shard_map/ppermute | solution.py:515
  65.3 27.9 %all-to-all-start.1 = ((f32[16,1,1152]{2,1,0:T(1,128)}), f32[16,1,1152]{2,1,0:T(1,128)S(1)}, u32[]{:S(2)}, u32[]{:S(2)}) async-start(f32[16,1,1152]{2,1,0:T(1,128)} %shard_map.54), calls=%async_computation.1 | async-start | bytes 147456 | tf_op jit(solution)/shard_map/all_to_all | solution.py:538
  81.5 10.8 %collective-permute-start.6 = (f32[8,1280]{1,0:T(8,128)S(1)}, f32[8,1280]{1,0:T(8,128)S(1)}, u32[]{:S(2)}, u32[]{:S(2)}) collective-permute-start(f32[8,1280]{1,0:T(8,128)S(1)} %get-tuple-element.29), channel_id=1, source_target_pairs={{1,2},{2,1},{3,4},{4,3},{5,6},{6,5},{7,8},{8,7},{9,10},{10,9},{11,... | collective-permute-start | bytes 122888 | tf_op jit(solution)/shard_map/ppermute | solution.py:515
